TPU v7x, 512 devices: a whole 4x4x16 slice. The times are simulated.
512 devices in a mesh: section: 128 (over x, z, y_hi), ch: 4 (over y_lo, core).
Axes of the slice: x: 4, y: 4 (y_hi: 2, y_lo: 2; y = y_hi * 2 + y_lo), z: 16, core: 2. Of those that a mesh axis runs over, the one named last changes fastest.
Arguments:
- act_carried: bfloat16 [128, 1280, 384], P('section', 'ch'), may hold values from -6 to 6
- cot_carried: bfloat16 [128, 1280, 384], P('section', 'ch'), may hold values from -6 to 6
- entry_latent: bfloat16 [1280, 384], P('ch'), may hold values from -6 to 6
- reward_head: bfloat16 [1280, 384], P('ch'), may hold values from -6 to 6
- stored_inputs: bfloat16 [128, 2, 1280, 384], P('section', None, 'ch'), may hold values from -6 to 6
- skip_buffer: bfloat16 [128, 2, 1280, 384], P('section', None, 'ch'), may hold values from -6 to 6
- conv_weight: bfloat16 [128, 3, 1280, 1280], P('section', None, 'ch'), may hold values from -0.09375 to 0.09375
- time_gain: float32 [25, 1280], P(None, 'ch'), may hold values from 0.5 to 1.5
- plan: int32 [128, 2], P('section'), may hold values from 0 to 1
- timesteps: int32 [128, 2], P('section'), may hold values from 0 to 24
Outputs:
- act_out: bfloat16 [128, 1280, 384], P('section', 'ch')
- cot_out: bfloat16 [128, 1280, 384], P('section', 'ch')
- mirror_in: bfloat16 [128, 1280, 384], P('section', 'ch')
All inputs are finite; a program needn't handle non-finite values.
Results may differ from a plain program's by a relative error of at most 0.0032.
Values may be sent and summed in bfloat16 or wider, within the bound.
No kernel may reach another device: no remote copies, remote signals or barrier semaphores. Data moves between devices by JAX's collectives and lax.ppermute only.
A program may use at most 64 MiB of HBM per device.

v0:
```python
import jax
import jax.numpy as jnp
from jax import lax
from jax.sharding import PartitionSpec as P

C = 1280
GROUPS = 32
CELLS = 64


epsilon = 1e-05


def shifted(block, axis, distance):
    devices = range(lax.axis_size(axis))
    route = [(i - distance, i) for i in devices if i - distance in devices]
    return lax.ppermute(block, axis, route)


def frame_shift(values, frames_by):
    step = frames_by * CELLS
    if step > 0:
        return jnp.concatenate(
            [values[:, step:], jnp.zeros((values.shape[0], step), values.dtype)], 1
        )
    if step < 0:
        return jnp.concatenate(
            [jnp.zeros((values.shape[0], -step), values.dtype), values[:, :step]], 1
        )
    return values


def normalize(values):
    grouped = values.reshape(values.shape[0] // (C // GROUPS), -1)
    average = jnp.mean(grouped, axis=1, keepdims=True)
    centred = grouped - average
    spread = jnp.mean(centred * centred, axis=1, keepdims=True)
    factor = lax.rsqrt(spread + epsilon)
    return ((centred * factor).reshape(values.shape), factor)


def norm_back(normed, factor, d_normed):
    normed_g = normed.reshape(factor.shape[0], -1)
    grad_g = d_normed.reshape(factor.shape[0], -1)
    result = factor * (
        grad_g
        - jnp.mean(grad_g, axis=1, keepdims=True)
        - normed_g * jnp.mean(grad_g * normed_g, axis=1, keepdims=True)
    )
    return result.reshape(normed.shape)


def silu_slope(normed):
    sigmoid = jax.nn.sigmoid(normed)
    return sigmoid * (1.0 + normed * (1.0 - sigmoid))


def local(
    act_carried,
    cot_carried,
    entry_latent,
    reward_head,
    stored_inputs,
    skip_buffer,
    conv_weight,
    time_gain,
    plan,
    timesteps,
):
    sections = lax.axis_size("section")
    section_place = lax.axis_index("section")
    weight = conv_weight[0]
    arrived = shifted(act_carried[0], "section", 1)
    returned = shifted(cot_carried[0], "section", -1)
    encoder = section_place < sections // 2
    x_in = jnp.where(section_place == 0, entry_latent, arrived)
    cot_in = jnp.where(section_place == sections - 1, reward_head, returned)
    slot_ids = plan[0]
    stamps = timesteps[0]
    one_hot = (stamps[:, None] == lax.iota(jnp.int32, time_gain.shape[0])[None, :]).astype(
        jnp.float32
    )
    gains = jnp.dot(
        one_hot, time_gain, precision=lax.Precision.HIGHEST, preferred_element_type=jnp.float32
    )
    skip_fwd = lax.dynamic_index_in_dim(skip_buffer[0], slot_ids[0], 0, False).astype(jnp.float32)
    skip_bwd = lax.dynamic_index_in_dim(skip_buffer[0], slot_ids[1], 0, False).astype(jnp.float32)
    saved = lax.dynamic_index_in_dim(stored_inputs[0], slot_ids[1], 0, False).astype(jnp.float32)
    normed, factor = normalize(x_in.astype(jnp.float32))
    acted = jax.nn.silu(normed).astype(jnp.bfloat16)
    stacked = jnp.stack([frame_shift(acted, k - 1) for k in range(3)])
    columns = weight
    conv_out = lax.psum_scatter(
        jnp.einsum("kio,kir->or", columns, stacked, preferred_element_type=jnp.float32),
        "ch",
        scatter_dimension=0,
        tiled=True,
    )
    added = jnp.where(encoder, jnp.zeros_like(skip_fwd), skip_fwd)
    act_out = (x_in.astype(jnp.float32) + conv_out * gains[0][:, None] + added).astype(jnp.bfloat16)
    cot_total = cot_in.astype(jnp.float32) + jnp.where(encoder, skip_bwd, jnp.zeros_like(skip_bwd))
    scaled = (cot_total * gains[1][:, None]).astype(jnp.bfloat16)
    columns = weight
    folded = jnp.einsum(
        "kio,or->kir",
        columns,
        lax.all_gather(scaled, "ch", axis=0, tiled=True),
        preferred_element_type=jnp.float32,
    )
    d_acted = frame_shift(folded[0], 1) + folded[1] + frame_shift(folded[2], -1)
    saved_normed, saved_factor = normalize(saved)
    d_normed = d_acted * silu_slope(saved_normed)
    cot_out = (cot_total + norm_back(saved_normed, saved_factor, d_normed)).astype(jnp.bfloat16)
    sent = jnp.where(encoder, act_out, cot_in)
    pieces = sent.reshape(sections, -1)
    spread = lax.all_to_all(pieces, "section", split_axis=0, concat_axis=0, tiled=True)
    gathered = lax.all_to_all(spread[::-1], "section", split_axis=0, concat_axis=0, tiled=True)
    sent = gathered.reshape(sent.shape)
    return (act_out[None], cot_out[None], sent[None])


def solution(mesh):
    placed = (
        P("section", "ch", None),
        P("section", "ch", None),
        P("ch", None),
        P("ch", None),
        P("section", None, "ch", None),
        P("section", None, "ch", None),
        P("section", None, "ch", None),
        P(None, "ch"),
        P("section", None),
        P("section", None),
    )
    return jax.shard_map(
        local,
        mesh=mesh,
        in_specs=placed,
        out_specs=(P("section", "ch", None), P("section", "ch", None), P("section", "ch", None)),
        check_vma=False,
    )
```

profile of v0, /device:TPU:1, one launch (start us, length us, event | category | flops | bytes accessed | tf_op | source)
XLA Modules:
  0.0 172.7 jit_solution(5265897284696152649)
XLA Ops:
  7.2 5.8 %collective-permute-start = (bf16[320,384]{1,0:T(8,128)(2,1)}, bf16[320,384]{1,0:T(8,128)(2,1)S(1)}, u32[]{:S(2)}, u32[]{:S(2)}) collective-permute-start(bf16[320,384]{1,0:T(8,128)(2,1)} %bitcast.103), channel_id=1, source_target_pairs={{0,4},{4,8},{8,12},{12,16},{16,20},{20,24},{24,28},{28,32},{32,36}... | collective-permute-start | bytes 737288 | tf_op jit(solution)/shard_map/ppermute | solution.py:17
  13.0 3.4 %collective-permute-done = bf16[320,384]{1,0:T(8,128)(2,1)S(1)} collective-permute-done((bf16[320,384]{1,0:T(8,128)(2,1)}, bf16[320,384]{1,0:T(8,128)(2,1)S(1)}, u32[]{:S(2)}, u32[]{:S(2)}) %collective-permute-start) | collective-permute-done | bytes 245792 | tf_op jit(solution)/shard_map/ppermute | solution.py:17
  19.4 2.9 %convolution_bitcast_fusion = f32[1280,384]{1,0:T(8,128)} fusion(bf16[1,3,320,1280]{3,2,1,0:T(8,128)(2,1)S(1)} %copy-done, bf16[1,320,384]{2,1,0:T(8,128)(2,1)S(1)} %get-tuple-element.19, bf16[1,320,384]{2,1,0:T(8,128)(2,1)S(1)} %fusion.56, bf16[1,320,384]{2,1,0:T(8,128)(2,1)S(1)} %get-tuple-element.20), kind=kOutput, calls=%fused_computation | convolution fusion | flops 944455680 | bytes 5160960 | tf_op jit(solution)/shard_map/kio,kir->or/dot_general | solution.py:94
  22.3 1.4 collective-permute-start.1
  29.4 1.8 %collective-permute-done.1 = bf16[320,384]{1,0:T(8,128)(2,1)} collective-permute-done((bf16[320,384]{1,0:T(8,128)(2,1)}, bf16[320,384]{1,0:T(8,128)(2,1)}, u32[]{:S(2)}, u32[]{:S(2)}) %collective-permute-start.1) | collective-permute-done | bytes 245792 | tf_op jit(solution)/shard_map/ppermute | solution.py:17
  31.2 33.4 %reduce-scatter.2.cloned.1.call-done = f32[320,384]{1,0:T(8,128)} async-done(((f32[1280,384]{1,0:T(8,128)}), f32[320,384]{1,0:T(8,128)}) %reduce-scatter.2.cloned.1.call-update) | async-done | bytes 491536 | tf_op jit(solution)/shard_map/reduce_scatter | solution.py:93
  64.6 2.3 %broadcast_select_fusion = (bf16[320,384]{1,0:T(8,128)(2,1)}, bf16[320,384]{1,0:T(8,128)(2,1)S(1)}, bf16[320,384]{1,0:T(8,128)(2,1)}) fusion(pred[]{:T(512)S(6)} %lt.11, bf16[320,384]{1,0:T(8,128)(2,1)S(1)} %copy-done.3, bf16[320,384]{1,0:T(8,128)(2,1)} %collective-permute-done.1, pred[]{:T(512)S(6)} %eq.26, bf16[1,2,320,384]{3,2,1,0:T(8,128)(2,1)} %param.15, ...), kind=kLoop, calls=%fused_computation.56 | loop fusion | flops 1105920 | bytes 2215168 | tf_op jit(solution)/shard_map/jit(_where)/select_n | solution.py:114
  68.7 2.9 %reduce.17 = bf16[128,960]{1,0:T(8,128)(2,1)} reduce(bf16[128,1,960]{2,1,0:T(2,128)(2,1)S(1)} %all_to_all.19, bf16[]{:T(256)} %broadcast.123), dimensions={1}, to_apply=%all_to_all.19.reduce_sub_computation | reduce | bytes 491522 | tf_op jit(solution)/shard_map/all_to_all | solution.py:116
  71.6 1.9 %reshape.110 = bf16[128,2,480]{2,1,0:T(2,128)(2,1)} reshape(bf16[128,960]{1,0:T(8,128)(2,1)} %reduce.17) | data formatting | bytes 491520
  73.5 19.2 %all-to-all-start = ((bf16[128,2,480]{2,1,0:T(2,128)(2,1)}), bf16[128,2,480]{2,1,0:T(2,128)(2,1)}, u32[]{:S(2)}, u32[]{:S(2)}) async-start(bf16[128,2,480]{2,1,0:T(2,128)(2,1)} %reshape.110), calls=%async_computation.1 | async-start | bytes 524288 | tf_op jit(solution)/shard_map/all_to_all | solution.py:116
  94.0 11.2 %all_gather.3 = bf16[1280,384]{1,0:T(8,128)(2,1)S(1)} all-gather(bf16[320,384]{1,0:T(8,128)(2,1)S(1)} %multiply_convert_fusion), channel_id=1, replica_groups=mesh['section'=128,'ch'=4] {'ch'}, dimensions={0}, use_global_device_ids=true | all-gather | bytes 1228800 | tf_op jit(solution)/shard_map/all_gather | solution.py:107
  105.2 2.6 %fusion.3 = f32[3,320,384]{2,1,0:T(8,128)} fusion(bf16[1,3,320,1280]{3,2,1,0:T(8,128)(2,1)S(1)} %copy-done, bf16[1280,384]{1,0:T(8,128)(2,1)S(1)} %all_gather.3), kind=kOutput, calls=%fused_computation.4 | convolution fusion | flops 943718400 | bytes 4915200 | tf_op jit(solution)/shard_map/kio,or->kir/dot_general | solution.py:104
  107.8 7.1 %all-to-all-done = bf16[128,2,480]{2,1,0:T(2,128)(2,1)} async-done(((bf16[128,2,480]{2,1,0:T(2,128)(2,1)}), bf16[128,2,480]{2,1,0:T(2,128)(2,1)}, u32[]{:S(2)}, u32[]{:S(2)}) %all-to-all-start) | async-done | bytes 245792 | tf_op jit(solution)/shard_map/all_to_all | solution.py:116
  114.9 2.4 %reshape.111 = bf16[128,1,960]{2,1,0:T(2,128)(2,1)S(1)} reshape(bf16[128,2,480]{2,1,0:T(2,128)(2,1)} %all-to-all-done) | data formatting | bytes 491520
  118.3 3.6 %rev.3 = bf16[128,960]{0,1:T(8,128)(2,1)S(1)} reverse(bf16[128,960]{0,1:T(8,128)(2,1)} %bitcast.101), dimensions={0} | reverse | bytes 491520 | tf_op jit(solution)/shard_map/rev | solution.py:117
  121.9 1.5 reduce.18
  123.4 1.8 %copy.28 = bf16[128,960]{1,0:T(8,128)(2,1)} copy(bf16[128,960]{0,1:T(8,128)(2,1)} %reduce.18) | data formatting | bytes 491520
  125.1 1.9 %reshape.112 = bf16[128,2,480]{2,1,0:T(2,128)(2,1)} reshape(bf16[128,960]{1,0:T(8,128)(2,1)} %copy.28) | data formatting | bytes 491520
  127.1 11.5 %all-to-all-start.1 = ((bf16[128,2,480]{2,1,0:T(2,128)(2,1)}), bf16[128,2,480]{2,1,0:T(2,128)(2,1)}, u32[]{:S(2)}, u32[]{:S(2)}) async-start(bf16[128,2,480]{2,1,0:T(2,128)(2,1)} %reshape.112), calls=%async_computation.2 | async-start | bytes 524288 | tf_op jit(solution)/shard_map/all_to_all | solution.py:117
  140.0 2.2 %fusion.50 = (f32[320]{0:T(512)S(1)}, f32[320]{0:T(512)S(1)}, f32[320,384]{1,0:T(8,128)}) fusion(f32[320]{0:T(512)S(1)} %mul.104, f32[320]{0:T(512)S(1)} %sub.59, bf16[1,2,320,384]{3,2,1,0:T(8,128)(2,1)S(1)} %copy-done.2, s32[]{:T(128)S(6)} %select_n.54, f32[320,320]{1,0:T(8,128)S(1)} %bitcast.99, f32[3,320,384]{2,1,0:T(8,128)} %fusion.3, ...), kind=kLoop, calls=%fused_computation.73 | loop fusion | flops 1965440 | bytes 2053124 | tf_op jit(solution)/shard_map/reduce_sum | solution.py:47
  142.9 2.1 %fusion.44 = bf16[1,320,384]{2,1,0:T(8,128)(2,1)} fusion(f32[320]{0:T(512)S(1)} %mul.115, f32[320]{0:T(512)S(1)} %sub.59, f32[320,384]{1,0:T(8,128)} %get-tuple-element.10, f32[320]{0:T(512)S(1)} %sub.66, f32[320]{0:T(512)S(1)} %mul.104, pred[]{:T(512)S(6)} %lt.11, bf16[320,384]{1,0:T(8,128)(2,1)S(1)} %get-tuple-element.8, ...), kind=kLoop, calls=%fused_computation.59 | loop fusion | flops 1597440 | bytes 1479685 | tf_op jit(solution)/shard_map/broadcast_in_dim | solution.py:119
  145.0 15.8 %all-to-all-done.1 = bf16[128,2,480]{2,1,0:T(2,128)(2,1)} async-done(((bf16[128,2,480]{2,1,0:T(2,128)(2,1)}), bf16[128,2,480]{2,1,0:T(2,128)(2,1)}, u32[]{:S(2)}, u32[]{:S(2)}) %all-to-all-start.1) | async-done | bytes 245792 | tf_op jit(solution)/shard_map/all_to_all | solution.py:117
  160.8 2.4 %reshape.113 = bf16[128,1,960]{2,1,0:T(2,128)(2,1)S(1)} reshape(bf16[128,2,480]{2,1,0:T(2,128)(2,1)} %all-to-all-done.1) | data formatting | bytes 491520
  163.2 1.6 reduce.14
  (64 shorter events, 12.0 us)
Async XLA Ops:
  7.2 12.2 %copy-start = (bf16[1,3,320,1280]{3,2,1,0:T(8,128)(2,1)S(1)}, bf16[1,3,320,1280]{3,2,1,0:T(8,128)(2,1)}, u32[]{:S(2)}) copy-start(bf16[1,3,320,1280]{3,2,1,0:T(8,128)(2,1)} %param.16) | copy-start | bytes 7372804
  7.2 57.4 %reduce-scatter.2.cloned.1.call-start = ((), (), s32[]{:S(2)}) async-start(), calls=%async_computation.3 | async-start | bytes 2457600 | tf_op jit(solution)/shard_map/reduce_scatter | solution.py:93
  7.2 9.2 %collective-permute-start = (bf16[320,384]{1,0:T(8,128)(2,1)}, bf16[320,384]{1,0:T(8,128)(2,1)S(1)}, u32[]{:S(2)}, u32[]{:S(2)}) collective-permute-start(bf16[320,384]{1,0:T(8,128)(2,1)} %bitcast.103), channel_id=1, source_target_pairs={{0,4},{4,8},{8,12},{12,16},{16,20},{20,24},{24,28},{28,32},{32,36}... | collective-permute-start | bytes 737288 | tf_op jit(solution)/shard_map/ppermute | solution.py:17
  19.4 4.3 %copy-start.4 = (s32[1,2]{1,0:T(1,128)S(1)}, s32[1,2]{1,0:T(1,128)}, u32[]{:S(2)}) copy-start(s32[1,2]{1,0:T(1,128)} %param.18) | copy-start | bytes 28
  19.4 8.2 %copy-start.1 = (bf16[1,2,320,384]{3,2,1,0:T(8,128)(2,1)S(1)}, bf16[1,2,320,384]{3,2,1,0:T(8,128)(2,1)}, u32[]{:S(2)}) copy-start(bf16[1,2,320,384]{3,2,1,0:T(8,128)(2,1)} %param.14) | copy-start | bytes 1474564
  22.3 6.9 %copy-start.5 = (f32[25,320]{1,0:T(8,128)S(1)}, f32[25,320]{1,0:T(8,128)}, u32[]{:S(2)}) copy-start(f32[25,320]{1,0:T(8,128)} %param.17) | copy-start | bytes 96004
  22.3 6.9 %copy-start.6 = (s32[1,2]{1,0:T(1,128)S(1)}, s32[1,2]{1,0:T(1,128)}, u32[]{:S(2)}) copy-start(s32[1,2]{1,0:T(1,128)} %param.19) | copy-start | bytes 28
  22.3 42.3 %copy-start.3 = (bf16[320,384]{1,0:T(8,128)(2,1)S(1)}, bf16[320,384]{1,0:T(8,128)(2,1)}, u32[]{:S(2)}) copy-start(bf16[320,384]{1,0:T(8,128)(2,1)} %param.13) | copy-start | bytes 737284
  22.3 8.9 %collective-permute-start.1 = (bf16[320,384]{1,0:T(8,128)(2,1)}, bf16[320,384]{1,0:T(8,128)(2,1)}, u32[]{:S(2)}, u32[]{:S(2)}) collective-permute-start(bf16[320,384]{1,0:T(8,128)(2,1)} %bitcast.104), channel_id=1, source_target_pairs={{4,0},{8,4},{12,8},{16,12},{20,16},{24,20},{28,24},{32,28},{36,32}... | collective-permute-start | bytes 737288 | tf_op jit(solution)/shard_map/ppermute | solution.py:17
  73.5 41.4 %all-to-all-start = ((bf16[128,2,480]{2,1,0:T(2,128)(2,1)}), bf16[128,2,480]{2,1,0:T(2,128)(2,1)}, u32[]{:S(2)}, u32[]{:S(2)}) async-start(bf16[128,2,480]{2,1,0:T(2,128)(2,1)} %reshape.110), calls=%async_computation.1 | async-start | bytes 524288 | tf_op jit(solution)/shard_map/all_to_all | solution.py:116
  121.9 18.2 %copy-start.2 = (bf16[1,2,320,384]{3,2,1,0:T(8,128)(2,1)S(1)}, bf16[1,2,320,384]{3,2,1,0:T(8,128)(2,1)}, u32[]{:S(2)}) copy-start(bf16[1,2,320,384]{3,2,1,0:T(8,128)(2,1)} %param.14) | copy-start | bytes 1474564
  127.1 33.8 %all-to-all-start.1 = ((bf16[128,2,480]{2,1,0:T(2,128)(2,1)}), bf16[128,2,480]{2,1,0:T(2,128)(2,1)}, u32[]{:S(2)}, u32[]{:S(2)}) async-start(bf16[128,2,480]{2,1,0:T(2,128)(2,1)} %reshape.112), calls=%async_computation.2 | async-start | bytes 524288 | tf_op jit(solution)/shard_map/all_to_all | solution.py:117
Sparse Core Ops, SparseCore 0:
  22.4 42.1 reduce-scatter.1
where the time goes:
time: 174 us; the launch traced here: 173 us
  waiting for transfers between devices  61.5 us (35%)
  starting transfers between devices  38 us (22%)
  local copies, waits for them, and re-layouts  21.6 us (12%)
  between operations  18.2 us (10%)
  other arithmetic  16.6 us (10%)
  blocking collectives  11.2 us (6%)
  matrix products  5.63 us (3%)
    reduce_scatter x1, waiting for transfers between devices, local(): lax.psum_scatter(jnp.einsum('kio,kir->or', columns, stacked, preferred_el...  33.4 us
    all_to_all x1, starting transfers between devices, local(): lax.all_to_all(pieces, 'section', split_axis=0, concat_axis=0, tiled=True)  19.2 us
    all_to_all x1, waiting for transfers between devices, local(): lax.all_to_all(spread[::-1], 'section', split_axis=0, concat_axis=0, tile...  15.8 us
    all_to_all x1, starting transfers between devices, local(): lax.all_to_all(spread[::-1], 'section', split_axis=0, concat_axis=0, tile...  11.5 us
    all_gather x1, blocking collectives, local(): lax.all_gather(scaled, 'ch', axis=0, tiled=True)  11.2 us
    unnamed x19, local copies, waits for them, and re-layouts  10.4 us
    ppermute x2, starting transfers between devices, shifted(): return lax.ppermute(block, axis, route)  7.22 us
    all_to_all x1, waiting for transfers between devices, local(): lax.all_to_all(pieces, 'section', split_axis=0, concat_axis=0, tiled=True)  7.06 us
  transfers between devices with their start and end apart: 5, of which 5 were waited for; matrix products, arithmetic and copies ran while one was open for 7% of the time, Pallas kernels for 0%

commit v1 on v0

--- a/solution.py
+++ b/solution.py
@@ -55,6 +55,18 @@
     return sigmoid * (1.0 + normed * (1.0 - sigmoid))
 
 
+def swap_core(block):
+    return lax.ppermute(block, "ch", [(0, 1), (1, 0), (2, 3), (3, 2)])
+
+
+def swap_chip(block):
+    return lax.ppermute(block, "ch", [(0, 2), (2, 0), (1, 3), (3, 1)])
+
+
+def pick(pair, index, axis):
+    return lax.dynamic_index_in_dim(pair, index, axis, False)
+
+
 def local(
     act_carried,
     cot_carried,
@@ -69,12 +81,16 @@
 ):
     sections = lax.axis_size("section")
     section_place = lax.axis_index("section")
+    place = lax.axis_index("ch")
+    core = place % 2
+    chip = place // 2
+    rows = act_carried.shape[1]
     weight = conv_weight[0]
+    encoder = section_place < sections // 2
+
     arrived = shifted(act_carried[0], "section", 1)
-    returned = shifted(cot_carried[0], "section", -1)
-    encoder = section_place < sections // 2
+
     x_in = jnp.where(section_place == 0, entry_latent, arrived)
-    cot_in = jnp.where(section_place == sections - 1, reward_head, returned)
     slot_ids = plan[0]
     stamps = timesteps[0]
     one_hot = (stamps[:, None] == lax.iota(jnp.int32, time_gain.shape[0])[None, :]).astype(
@@ -86,37 +102,63 @@
     skip_fwd = lax.dynamic_index_in_dim(skip_buffer[0], slot_ids[0], 0, False).astype(jnp.float32)
     skip_bwd = lax.dynamic_index_in_dim(skip_buffer[0], slot_ids[1], 0, False).astype(jnp.float32)
     saved = lax.dynamic_index_in_dim(stored_inputs[0], slot_ids[1], 0, False).astype(jnp.float32)
+
+    saved_normed, saved_factor = normalize(saved)
+    slope = silu_slope(saved_normed)
+    cot_source, slope = lax.optimization_barrier((cot_carried[0], slope))
+    returned = shifted(cot_source, "section", -1)
+
     normed, factor = normalize(x_in.astype(jnp.float32))
     acted = jax.nn.silu(normed).astype(jnp.bfloat16)
-    stacked = jnp.stack([frame_shift(acted, k - 1) for k in range(3)])
-    columns = weight
-    conv_out = lax.psum_scatter(
-        jnp.einsum("kio,kir->or", columns, stacked, preferred_element_type=jnp.float32),
-        "ch",
-        scatter_dimension=0,
-        tiled=True,
+    stacked = jnp.concatenate([frame_shift(acted, k - 1) for k in range(3)], 0)
+    partial = lax.dot_general(
+        weight.reshape(3 * rows, -1),
+        stacked,
+        (((0,), (0,)), ((), ())),
+        preferred_element_type=jnp.float32,
+    ).reshape(2, 2, rows, -1)
+    returned, partial = lax.optimization_barrier((returned, partial))
+    mate_part = swap_core(pick(partial, 1 - core, 1))
+
+    cot_in = jnp.where(section_place == sections - 1, reward_head, returned)
+    cot_total = cot_in.astype(jnp.float32) + jnp.where(encoder, skip_bwd, jnp.zeros_like(skip_bwd))
+    scaled = (cot_total * gains[1][:, None]).astype(jnp.bfloat16)
+    scaled, mate_part = lax.optimization_barrier((scaled, mate_part))
+    other = swap_chip(scaled)
+    chip_sum = pick(partial, core, 1) + mate_part
+    far = swap_chip(pick(chip_sum, 1 - chip, 0).astype(jnp.bfloat16))
+    cot_source, chip_sum = lax.optimization_barrier((cot_source, chip_sum))
+    mirrored_cot = lax.ppermute(
+        cot_source, "section", [(sections - s, s) for s in range(1, sections // 2)]
     )
+    far, other = lax.optimization_barrier((far, other))
+    conv_out = pick(chip_sum, chip, 0) + far.astype(jnp.float32)
     added = jnp.where(encoder, jnp.zeros_like(skip_fwd), skip_fwd)
     act_out = (x_in.astype(jnp.float32) + conv_out * gains[0][:, None] + added).astype(jnp.bfloat16)
-    cot_total = cot_in.astype(jnp.float32) + jnp.where(encoder, skip_bwd, jnp.zeros_like(skip_bwd))
-    scaled = (cot_total * gains[1][:, None]).astype(jnp.bfloat16)
-    columns = weight
+    mirrored_act = lax.ppermute(
+        act_out, "section", [(s, sections - 1 - s) for s in range(sections // 2)]
+    )
+
+    pair = jnp.stack([jnp.where(chip == 0, scaled, other), jnp.where(chip == 0, other, scaled)])
+    mate = swap_core(pair)
+    mate, act_out = lax.optimization_barrier((mate, act_out))
+    whole = jnp.stack([jnp.where(core == 0, pair, mate), jnp.where(core == 0, mate, pair)], 1)
     folded = jnp.einsum(
         "kio,or->kir",
-        columns,
-        lax.all_gather(scaled, "ch", axis=0, tiled=True),
+        weight,
+        whole.reshape(4 * rows, -1),
         preferred_element_type=jnp.float32,
     )
     d_acted = frame_shift(folded[0], 1) + folded[1] + frame_shift(folded[2], -1)
-    saved_normed, saved_factor = normalize(saved)
-    d_normed = d_acted * silu_slope(saved_normed)
+    d_normed = d_acted * slope
     cot_out = (cot_total + norm_back(saved_normed, saved_factor, d_normed)).astype(jnp.bfloat16)
-    sent = jnp.where(encoder, act_out, cot_in)
-    pieces = sent.reshape(sections, -1)
-    spread = lax.all_to_all(pieces, "section", split_axis=0, concat_axis=0, tiled=True)
-    gathered = lax.all_to_all(spread[::-1], "section", split_axis=0, concat_axis=0, tiled=True)
-    sent = gathered.reshape(sent.shape)
-    return (act_out[None], cot_out[None], sent[None])
+
+    mirrored_cot, mirrored_act, cot_out = lax.optimization_barrier(
+        (mirrored_cot, mirrored_act, cot_out)
+    )
+    mirrored_cot = jnp.where(section_place == 0, reward_head, mirrored_cot)
+    mirror_in = jnp.where(encoder, mirrored_cot, mirrored_act)
+    return (act_out[None], cot_out[None], mirror_in[None])
 
 
 def solution(mesh):

time: 174 us -> 105 us (0.60)
  the two profiles are of different devices: /device:TPU:1 before, /device:TPU:30 now
where the time goes in v1:
time: 105 us; the launch traced here: 104 us
  waiting for transfers between devices  34 us (32%)
  starting transfers between devices  30.4 us (29%)
  other arithmetic  19.5 us (19%)
  local copies, waits for them, and re-layouts  10.9 us (10%)
  between operations  4.86 us (5%)
  matrix products  4.3 us (4%)
    ppermute x1, waiting for transfers between devices, local(): lax.ppermute(act_out, 'section', [(s, sections - 1 - s) for s in range(se...  12.6 us
    ppermute x1, starting transfers between devices, local(): lax.ppermute(cot_source, 'section', [(sections - s, s) for s in range(1,...  11.8 us
    ppermute x1, waiting for transfers between devices, local(): lax.ppermute(cot_source, 'section', [(sections - s, s) for s in range(1,...  9.86 us
    ppermute x2, waiting for transfers between devices, swap_chip(): return lax.ppermute(block, 'ch', [(0, 2), (2, 0), (1, 3), (3, 1)])  8.7 us
    ppermute x2, starting transfers between devices, shifted(): return lax.ppermute(block, axis, route)  7.6 us
    ppermute x2, starting transfers between devices, swap_chip(): return lax.ppermute(block, 'ch', [(0, 2), (2, 0), (1, 3), (3, 1)])  5.84 us
    ppermute x2, starting transfers between devices, swap_core(): return lax.ppermute(block, 'ch', [(0, 1), (1, 0), (2, 3), (3, 2)])  3.82 us
    dot_general x1, local copies, waits for them, and re-layouts, local(): lax.dot_general(weight.reshape(3 * rows, -1), stacked, (((0,), (0,)), (()...  2.87 us
  transfers between devices with their start and end apart: 8, of which 6 were waited for; matrix products, arithmetic and copies ran while one was open for 24% of the time, Pallas kernels for 0%

profile of v1, /device:TPU:30, one launch (start us, length us, event | category | flops | bytes accessed | tf_op | source)
XLA Modules:
  0.0 103.9 jit_solution(14195474973562935780)
XLA Ops:
  0.7 4.8 %collective-permute-start.1 = (bf16[320,384]{1,0:T(8,128)(2,1)}, bf16[320,384]{1,0:T(8,128)(2,1)S(1)}, u32[]{:S(2)}, u32[]{:S(2)}) collective-permute-start(bf16[320,384]{1,0:T(8,128)(2,1)} %bitcast.110), channel_id=1, source_target_pairs={{0,4},{4,8},{8,12},{12,16},{16,20},{20,24},{24,28},{28,32},{32,36}... | collective-permute-start | bytes 737288 | tf_op jit(solution)/shard_map/ppermute | solution.py:17
  5.4 1.3 %fusion.62 = (s32[1,1]{1,0:T(1,128)}, s32[1,1]{1,0:T(1,128)}) fusion(s32[1,2]{1,0:T(1,128)} %param.18), kind=kLoop, calls=%fused_computation.92 | loop fusion | bytes 16 | tf_op jit(solution)/shard_map/slice | solution.py:102
  11.7 2.0 %fusion.37 = f32[320,384]{1,0:T(8,128)} fusion(f32[320]{0:T(512)S(1)} %mul.95, f32[320]{0:T(512)S(1)} %sub.66, bf16[1,2,320,384]{3,2,1,0:T(8,128)(2,1)} %param.14, s32[]{:T(128)S(6)} %select_n.100), kind=kLoop, calls=%fused_computation.45 | loop fusion | flops 1228800 | bytes 739844 | tf_op jit(solution)/shard_map/mul | solution.py:55
  13.7 2.8 %collective-permute-start = (bf16[320,384]{1,0:T(8,128)(2,1)}, bf16[320,384]{1,0:T(8,128)(2,1)}, u32[]{:S(2)}, u32[]{:S(2)}) collective-permute-start(bf16[320,384]{1,0:T(8,128)(2,1)} %bitcast.111), channel_id=1, source_target_pairs={{4,0},{8,4},{12,8},{16,12},{20,16},{24,20},{28,24},{32,28},{36,32}... | collective-permute-start | bytes 737288 | tf_op jit(solution)/shard_map/ppermute | solution.py:17
  18.2 2.7 %convolution_bitcast_fusion = f32[1280,384]{0,1:T(8,128)} fusion(bf16[960,1280]{1,0:T(8,128)(2,1)S(1)} %bitcast.104, bf16[320,320]{1,0:T(8,128)(2,1)S(1)} %get-tuple-element.47, bf16[320,320]{1,0:T(8,128)(2,1)S(1)} %get-tuple-element.46, bf16[320,384]{1,0:T(8,128)(2,1)S(1)} %fusion.23), kind=kOutput, calls=%fused_computation | convolution fusion | flops 947404800 | bytes 5079040 | tf_op jit(solution)/shard_map/dot_general | solution.py:114
  20.8 2.9 %copy.18 = f32[1280,384]{1,0:T(8,128)} copy(f32[1280,384]{0,1:T(8,128)} %convolution_bitcast_fusion) | data formatting | bytes 3932160 | tf_op jit(solution)/shard_map/dot_general | solution.py:114
  23.7 2.0 %collective-permute-done = bf16[320,384]{1,0:T(8,128)(2,1)} collective-permute-done((bf16[320,384]{1,0:T(8,128)(2,1)}, bf16[320,384]{1,0:T(8,128)(2,1)}, u32[]{:S(2)}, u32[]{:S(2)}) %collective-permute-start) | collective-permute-done | bytes 245792 | tf_op jit(solution)/shard_map/ppermute | solution.py:17
  25.7 2.2 %dynamic-slice_bitcast_fusion = f32[2,320,384]{2,1,0:T(8,128)} fusion(f32[2,2,320,384]{3,2,1,0:T(8,128)} %bitcast.105, s32[]{:T(128)S(6)} %select_n.108), kind=kLoop, calls=%fused_computation.10 | loop fusion | bytes 1966084 | tf_op jit(solution)/shard_map/jit(dynamic_index_in_dim)/squeeze | solution.py:67
  27.9 1.9 %collective-permute-start.2 = (f32[2,320,384]{2,1,0:T(8,128)}, f32[2,320,384]{2,1,0:T(8,128)}, u32[]{:S(2)}, u32[]{:S(2)}) collective-permute-start(f32[2,320,384]{2,1,0:T(8,128)} %dynamic-slice_bitcast_fusion), channel_id=1, source_target_pairs={{0,1},{1,0},{2,3},{3,2},{4,5},{5,4},{6,7},{7,6},{8,9},{9,8},{10,11... | collective-permute-start | bytes 2949128 | tf_op jit(solution)/shard_map/ppermute | solution.py:59
  30.1 1.8 %multiply_convert_fusion = bf16[320,384]{1,0:T(8,128)(2,1)} fusion(f32[320]{0:T(512)S(1)} %get-tuple-element.36, pred[]{:T(512)S(6)} %lt.32, bf16[1,2,320,384]{3,2,1,0:T(8,128)(2,1)S(1)} %copy-done.5, s32[]{:T(128)S(6)} %select_n.100, bf16[320,384]{1,0:T(8,128)(2,1)S(1)} %copy-done.3, bf16[320,384]{1,0:T(8,128)(2,1)} %collective-permute-done, pred[]{:T(512)S(6)} %eq.33), kind=kLoop, calls=%fused_computation.66 | loop fusion | flops 860160 | bytes 984326 | tf_op jit(solution)/shard_map/convert_element_type | solution.py:125
  32.7 1.6 %bitcast_add_fusion = f32[2,320,384]{2,1,0:T(8,128)S(1)} fusion(f32[2,320,384]{2,1,0:T(8,128)} %collective-permute-done.2, f32[2,2,320,384]{3,2,1,0:T(8,128)} %bitcast.106, s32[]{:T(128)S(6)} %select_n.109), kind=kLoop, calls=%fused_computation.9 | loop fusion | flops 245760 | bytes 2949124 | tf_op jit(solution)/shard_map/add | solution.py:128
  35.3 1.9 %collective-permute-start.3 = (bf16[320,384]{1,0:T(8,128)(2,1)S(1)}, bf16[320,384]{1,0:T(8,128)(2,1)S(1)}, u32[]{:S(2)}, u32[]{:S(2)}) collective-permute-start(bf16[320,384]{1,0:T(8,128)(2,1)S(1)} %fusion.50), channel_id=1, source_target_pairs={{0,2},{2,0},{1,3},{3,1},{4,6},{6,4},{5,7},{7,5},{8,10},{10,8},{9,1... | collective-permute-start | bytes 737288 | tf_op jit(solution)/shard_map/ppermute | solution.py:63
  37.2 3.9 %collective-permute-start.4 = (bf16[320,384]{1,0:T(8,128)(2,1)}, bf16[320,384]{1,0:T(8,128)(2,1)}, u32[]{:S(2)}, u32[]{:S(2)}) collective-permute-start(bf16[320,384]{1,0:T(8,128)(2,1)} %multiply_convert_fusion), channel_id=1, source_target_pairs={{0,2},{2,0},{1,3},{3,1},{4,6},{6,4},{5,7},{7,5},{8,10},{10,8},{9,1... | collective-permute-start | bytes 737288 | tf_op jit(solution)/shard_map/ppermute | solution.py:63
  41.2 4.8 %collective-permute-done.3 = bf16[320,384]{1,0:T(8,128)(2,1)S(1)} collective-permute-done((bf16[320,384]{1,0:T(8,128)(2,1)S(1)}, bf16[320,384]{1,0:T(8,128)(2,1)S(1)}, u32[]{:S(2)}, u32[]{:S(2)}) %collective-permute-start.3) | collective-permute-done | bytes 245792 | tf_op jit(solution)/shard_map/ppermute | solution.py:63
  46.7 3.9 %collective-permute-done.4 = bf16[320,384]{1,0:T(8,128)(2,1)} collective-permute-done((bf16[320,384]{1,0:T(8,128)(2,1)}, bf16[320,384]{1,0:T(8,128)(2,1)}, u32[]{:S(2)}, u32[]{:S(2)}) %collective-permute-start.4) | collective-permute-done | bytes 245792 | tf_op jit(solution)/shard_map/ppermute | solution.py:63
  52.5 1.9 %collective-permute-start.5 = (bf16[2,320,384]{2,1,0:T(8,128)(2,1)}, bf16[2,320,384]{2,1,0:T(8,128)(2,1)}, u32[]{:S(2)}, u32[]{:S(2)}) collective-permute-start(bf16[2,320,384]{2,1,0:T(8,128)(2,1)} %pad_maximum_fusion.1), channel_id=1, source_target_pairs={{0,1},{1,0},{2,3},{3,2},{4,5},{5,4},{6,7},{7,6},{8,9},{9,8},{10,11... | collective-permute-start | bytes 1474568 | tf_op jit(solution)/shard_map/ppermute | solution.py:59
  56.4 11.8 %collective-permute-start.6 = (bf16[320,384]{1,0:T(8,128)(2,1)}, bf16[320,384]{1,0:T(8,128)(2,1)}, u32[]{:S(2)}, u32[]{:S(2)}) collective-permute-start(bf16[320,384]{1,0:T(8,128)(2,1)} %bitcast.112), channel_id=1, source_target_pairs={{508,4},{504,8},{500,12},{496,16},{492,20},{488,24},{484,28},{480,... | collective-permute-start | bytes 737288 | tf_op jit(solution)/shard_map/ppermute | solution.py:131
  68.2 2.1 %fusion.26 = bf16[320,384]{1,0:T(8,128)(2,1)} fusion(bf16[320,384]{1,0:T(8,128)(2,1)S(1)} %get-tuple-element.39, bf16[320,384]{1,0:T(8,128)(2,1)} %copy-done.6, f32[2,320,384]{2,1,0:T(8,128)} %copy-done.2, s32[]{:T(128)S(6)} %select_n.113, bf16[1,2,320,384]{3,2,1,0:T(8,128)(2,1)} %param.15, s32[]{:T(128)S(6)} %select_n.114, f32[320]{0:T(512)S(1)} %get-tuple-element.35, ...), kind=kLoop, calls=%fused_computation.34 | loop fusion | flops 1105920 | bytes 1475849 | tf_op jit(solution)/shard_map/convert_element_type | solution.py:137
  70.3 1.3 %collective-permute-start.7 = (bf16[320,384]{1,0:T(8,128)(2,1)}, bf16[320,384]{1,0:T(8,128)(2,1)}, u32[]{:S(2)}, u32[]{:S(2)}) collective-permute-start(bf16[320,384]{1,0:T(8,128)(2,1)} %fusion.26), channel_id=1, source_target_pairs={{0,508},{4,504},{8,500},{12,496},{16,492},{20,488},{24,484},{28,48... | collective-permute-start | bytes 737288 | tf_op jit(solution)/shard_map/ppermute | solution.py:138
  73.0 1.4 %fusion.4 = f32[3,320,384]{2,1,0:T(8,128)S(1)} fusion(bf16[1280,384,1]{1,0,2:T(8,128)(2,1)S(1)} %bitcast.108, bf16[1,3,320,1280]{3,2,1,0:T(8,128)(2,1)S(1)} %copy-done), kind=kOutput, calls=%fused_computation.7 | convolution fusion | flops 943718400 | bytes 4915200 | tf_op jit(solution)/shard_map/kio,or->kir/dot_general | solution.py:146
  77.5 2.2 %fusion.42 = bf16[320,384]{1,0:T(8,128)(2,1)} fusion(f32[320,384]{1,0:T(8,128)} %get-tuple-element.37, f32[320]{0:T(512)S(1)} %mul.115, f32[320]{0:T(512)S(1)} %sub.79, f32[320]{0:T(512)S(1)} %mul.95, f32[320]{0:T(512)S(1)} %sub.66, pred[]{:T(512)S(6)} %lt.32, bf16[1,2,320,384]{3,2,1,0:T(8,128)(2,1)} %param.15, s32[]{:T(128)S(6)} %select_n.100, ...), kind=kLoop, calls=%fused_computation.50 | loop fusion | flops 1720320 | bytes 1725446 | tf_op jit(solution)/shard_map/convert_element_type | solution.py:154
  79.7 9.9 %collective-permute-done.6 = bf16[320,384]{1,0:T(8,128)(2,1)} collective-permute-done((bf16[320,384]{1,0:T(8,128)(2,1)}, bf16[320,384]{1,0:T(8,128)(2,1)}, u32[]{:S(2)}, u32[]{:S(2)}) %collective-permute-start.6) | collective-permute-done | bytes 245792 | tf_op jit(solution)/shard_map/ppermute | solution.py:131
  89.5 12.6 %collective-permute-done.7 = bf16[320,384]{1,0:T(8,128)(2,1)} collective-permute-done((bf16[320,384]{1,0:T(8,128)(2,1)}, bf16[320,384]{1,0:T(8,128)(2,1)}, u32[]{:S(2)}, u32[]{:S(2)}) %collective-permute-start.7) | collective-permute-done | bytes 245792 | tf_op jit(solution)/shard_map/ppermute | solution.py:138
  102.1 1.8 %select_bitcast_fusion.2 = bf16[1,320,384]{2,1,0:T(8,128)(2,1)} fusion(bf16[320,384]{1,0:T(8,128)(2,1)} %collective-permute-done.7, bf16[320,384]{1,0:T(8,128)(2,1)S(1)} %copy-done.3, bf16[320,384]{1,0:T(8,128)(2,1)} %collective-permute-done.6, pred[]{:T(512)S(6)} %lt.32, pred[]{:T(512)S(6)} %eq.34), kind=kLoop, calls=%fused_computation.69 | loop fusion | flops 245760 | bytes 983042 | tf_op jit(solution)/shard_map/broadcast_in_dim | solution.py:161
  (70 shorter events, 13.6 us)
Async XLA Ops:
  0.6 17.5 %copy-start = (bf16[1,3,320,1280]{3,2,1,0:T(8,128)(2,1)S(1)}, bf16[1,3,320,1280]{3,2,1,0:T(8,128)(2,1)}, u32[]{:S(2)}) copy-start(bf16[1,3,320,1280]{3,2,1,0:T(8,128)(2,1)} %param.16) | copy-start | bytes 7372804
  0.6 15.9 %copy-start.7 = (bf16[320,384]{1,0:T(8,128)(2,1)S(1)}, bf16[320,384]{1,0:T(8,128)(2,1)}, u32[]{:S(2)}) copy-start(bf16[320,384]{1,0:T(8,128)(2,1)} %param.12) | copy-start | bytes 737284
  0.7 15.9 %collective-permute-start.1 = (bf16[320,384]{1,0:T(8,128)(2,1)}, bf16[320,384]{1,0:T(8,128)(2,1)S(1)}, u32[]{:S(2)}, u32[]{:S(2)}) collective-permute-start(bf16[320,384]{1,0:T(8,128)(2,1)} %bitcast.110), channel_id=1, source_target_pairs={{0,4},{4,8},{8,12},{12,16},{16,20},{20,24},{24,28},{28,32},{32,36}... | collective-permute-start | bytes 737288 | tf_op jit(solution)/shard_map/ppermute | solution.py:17
  13.7 12.0 %collective-permute-start = (bf16[320,384]{1,0:T(8,128)(2,1)}, bf16[320,384]{1,0:T(8,128)(2,1)}, u32[]{:S(2)}, u32[]{:S(2)}) collective-permute-start(bf16[320,384]{1,0:T(8,128)(2,1)} %bitcast.111), channel_id=1, source_target_pairs={{4,0},{8,4},{12,8},{16,12},{20,16},{24,20},{28,24},{32,28},{36,32}... | collective-permute-start | bytes 737288 | tf_op jit(solution)/shard_map/ppermute | solution.py:17
  23.7 6.2 %copy-start.8 = (f32[25,320]{1,0:T(8,128)S(1)}, f32[25,320]{1,0:T(8,128)}, u32[]{:S(2)}) copy-start(f32[25,320]{1,0:T(8,128)} %param.17) | copy-start | bytes 96004
  23.7 6.2 %copy-start.9 = (s32[1,2]{1,0:T(1,128)S(1)}, s32[1,2]{1,0:T(1,128)}, u32[]{:S(2)}) copy-start(s32[1,2]{1,0:T(1,128)} %param.19) | copy-start | bytes 28
  23.7 6.4 %copy-start.3 = (bf16[320,384]{1,0:T(8,128)(2,1)S(1)}, bf16[320,384]{1,0:T(8,128)(2,1)}, u32[]{:S(2)}) copy-start(bf16[320,384]{1,0:T(8,128)(2,1)} %param.13) | copy-start | bytes 737284
  23.7 6.4 %copy-start.5 = (bf16[1,2,320,384]{3,2,1,0:T(8,128)(2,1)S(1)}, bf16[1,2,320,384]{3,2,1,0:T(8,128)(2,1)}, u32[]{:S(2)}) copy-start(bf16[1,2,320,384]{3,2,1,0:T(8,128)(2,1)} %param.15) | copy-start | bytes 1474564
  27.9 4.8 %collective-permute-start.2 = (f32[2,320,384]{2,1,0:T(8,128)}, f32[2,320,384]{2,1,0:T(8,128)}, u32[]{:S(2)}, u32[]{:S(2)}) collective-permute-start(f32[2,320,384]{2,1,0:T(8,128)} %dynamic-slice_bitcast_fusion), channel_id=1, source_target_pairs={{0,1},{1,0},{2,3},{3,2},{4,5},{5,4},{6,7},{7,6},{8,9},{9,8},{10,11... | collective-permute-start | bytes 2949128 | tf_op jit(solution)/shard_map/ppermute | solution.py:59
  34.3 1.0 copy-start.2
  35.3 10.7 %collective-permute-start.3 = (bf16[320,384]{1,0:T(8,128)(2,1)S(1)}, bf16[320,384]{1,0:T(8,128)(2,1)S(1)}, u32[]{:S(2)}, u32[]{:S(2)}) collective-permute-start(bf16[320,384]{1,0:T(8,128)(2,1)S(1)} %fusion.50), channel_id=1, source_target_pairs={{0,2},{2,0},{1,3},{3,1},{4,6},{6,4},{5,7},{7,5},{8,10},{10,8},{9,1... | collective-permute-start | bytes 737288 | tf_op jit(solution)/shard_map/ppermute | solution.py:63
  37.2 13.3 %collective-permute-start.4 = (bf16[320,384]{1,0:T(8,128)(2,1)}, bf16[320,384]{1,0:T(8,128)(2,1)}, u32[]{:S(2)}, u32[]{:S(2)}) collective-permute-start(bf16[320,384]{1,0:T(8,128)(2,1)} %multiply_convert_fusion), channel_id=1, source_target_pairs={{0,2},{2,0},{1,3},{3,1},{4,6},{6,4},{5,7},{7,5},{8,10},{10,8},{9,1... | collective-permute-start | bytes 737288 | tf_op jit(solution)/shard_map/ppermute | solution.py:63
  46.0 0.7 copy-start.6
  52.5 19.1 %collective-permute-start.5 = (bf16[2,320,384]{2,1,0:T(8,128)(2,1)}, bf16[2,320,384]{2,1,0:T(8,128)(2,1)}, u32[]{:S(2)}, u32[]{:S(2)}) collective-permute-start(bf16[2,320,384]{2,1,0:T(8,128)(2,1)} %pad_maximum_fusion.1), channel_id=1, source_target_pairs={{0,1},{1,0},{2,3},{3,2},{4,5},{5,4},{6,7},{7,6},{8,9},{9,8},{10,11... | collective-permute-start | bytes 1474568 | tf_op jit(solution)/shard_map/ppermute | solution.py:59
  56.4 33.1 %collective-permute-start.6 = (bf16[320,384]{1,0:T(8,128)(2,1)}, bf16[320,384]{1,0:T(8,128)(2,1)}, u32[]{:S(2)}, u32[]{:S(2)}) collective-permute-start(bf16[320,384]{1,0:T(8,128)(2,1)} %bitcast.112), channel_id=1, source_target_pairs={{508,4},{504,8},{500,12},{496,16},{492,20},{488,24},{484,28},{480,... | collective-permute-start | bytes 737288 | tf_op jit(solution)/shard_map/ppermute | solution.py:131
  70.3 31.8 %collective-permute-start.7 = (bf16[320,384]{1,0:T(8,128)(2,1)}, bf16[320,384]{1,0:T(8,128)(2,1)}, u32[]{:S(2)}, u32[]{:S(2)}) collective-permute-start(bf16[320,384]{1,0:T(8,128)(2,1)} %fusion.26), channel_id=1, source_target_pairs={{0,508},{4,504},{8,500},{12,496},{16,492},{20,488},{24,484},{28,48... | collective-permute-start | bytes 737288 | tf_op jit(solution)/shard_map/ppermute | solution.py:138
  74.4 1.0 copy-start.1
  74.4 1.2 %copy-start.4 = (f32[320,384]{1,0:T(8,128)S(1)}, f32[320,384]{1,0:T(8,128)}, u32[]{:S(2)}) copy-start(f32[320,384]{1,0:T(8,128)} %fusion.37) | copy-start | bytes 1474564

commit v2 on v0

v2 whole, which is shorter than its diff:
```python
import jax
import jax.numpy as jnp
from jax import lax
from jax.experimental import pallas as pl
from jax.experimental.pallas import tpu as pltpu
from jax.sharding import PartitionSpec as P

C = 1280
GROUPS = 32
CELLS = 64
WIDTH = C // GROUPS

epsilon = 1e-05

VMEM = pl.BlockSpec(memory_space=pltpu.VMEM)
SMEM = pl.BlockSpec(memory_space=pltpu.SMEM)


def shifted(block, axis, distance):
    devices = range(lax.axis_size(axis))
    route = [(i - distance, i) for i in devices if i - distance in devices]
    return lax.ppermute(block, axis, route)


def swap_core(block):
    return lax.ppermute(block, "ch", [(0, 1), (1, 0), (2, 3), (3, 2)])


def swap_chip(block):
    return lax.ppermute(block, "ch", [(0, 2), (2, 0), (1, 3), (3, 1)])


def frame_shift(values, frames_by):
    step = frames_by * CELLS
    if step == 0:
        return values
    width = values.shape[1]
    lane = lax.broadcasted_iota(jnp.int32, values.shape, 1)
    rolled = pltpu.roll(values, (-step) % width, 1)
    kept = lane < width - step if step > 0 else lane >= -step
    return jnp.where(kept, rolled, 0.0)


def group_mean(grouped):
    total = jnp.sum(jnp.sum(grouped, axis=1, keepdims=True), axis=2, keepdims=True)
    return total * (1.0 / (grouped.shape[1] * grouped.shape[2]))


def by_group(values):
    return values.reshape(values.shape[0] // WIDTH, WIDTH, values.shape[1])


def normalize(values):
    grouped = by_group(values)
    centred = grouped - group_mean(grouped)
    factor = lax.rsqrt(group_mean(centred * centred) + epsilon)
    return (centred * factor).reshape(values.shape), factor


def column(table_ref, stamp):
    width = table_ref.shape[1]
    row = jnp.broadcast_to(table_ref[pl.ds(stamp, 1), :], (width, width))
    across = lax.broadcasted_iota(jnp.int32, (width, width), 0)
    along = lax.broadcasted_iota(jnp.int32, (width, width), 1)
    return jnp.sum(jnp.where(across == along, row, 0.0), axis=1, keepdims=True)


def transpose_kernel(weight_ref, out_ref):
    depth = weight_ref.shape[0]
    for start in range(0, depth, 128):
        size = min(128, depth - start)
        out_ref[:, start : start + size] = weight_ref[start : start + size, :].T


def forward_kernel(place_ref, arrived_ref, entry_ref, weight_ref, mate_ref, stacked_ref):
    rows = arrived_ref.shape[0]
    first = place_ref[0] == 0
    x_in = jnp.where(first, entry_ref[...], arrived_ref[...]).astype(jnp.float32)
    normed, _ = normalize(x_in)
    acted = normed / (1.0 + jnp.exp(-normed))
    for k in range(3):
        stacked_ref[k * rows : (k + 1) * rows, :] = frame_shift(acted, k - 1).astype(jnp.bfloat16)
    own_side(1 - place_ref[1], weight_ref, stacked_ref, mate_ref)


def own_side(core, weight_ref, stacked_ref, out_ref):
    rows = out_ref.shape[1]
    for chip in range(2):
        start = pl.multiple_of((chip * 2 + core) * rows, rows)
        out_ref[chip] = jnp.dot(
            weight_ref[pl.ds(start, rows), :], stacked_ref[...], preferred_element_type=jnp.float32
        )


def own_kernel(place_ref, weight_ref, stacked_ref, own_ref):
    own_side(place_ref[1], weight_ref, stacked_ref, own_ref)


def cotangent(place_ref, plan_ref, returned_ref, reward_ref, skip_ref):
    last = place_ref[3] == 1
    cot_in = jnp.where(last, reward_ref[...], returned_ref[...])
    skip = skip_ref[plan_ref[0, 1]].astype(jnp.float32)
    skip = jnp.where(place_ref[4] == 1, skip, 0.0)
    return cot_in, cot_in.astype(jnp.float32) + skip


def scaled_kernel(
    place_ref, plan_ref, stamps_ref, returned_ref, reward_ref, skip_ref, gain_ref, scaled_ref
):
    _, cot_total = cotangent(place_ref, plan_ref, returned_ref, reward_ref, skip_ref)
    scaled_ref[...] = (cot_total * column(gain_ref, stamps_ref[0, 1])).astype(jnp.bfloat16)


def halves_kernel(place_ref, own_ref, mate_ref, near_ref, far_ref):
    chip = place_ref[2]
    near_ref[...] = own_ref[chip] + mate_ref[chip]
    far_ref[...] = (own_ref[1 - chip] + mate_ref[1 - chip]).astype(jnp.bfloat16)


def output_kernel(
    place_ref,
    plan_ref,
    stamps_ref,
    near_ref,
    far_ref,
    arrived_ref,
    entry_ref,
    skip_ref,
    gain_ref,
    returned_ref,
    reward_ref,
    out_ref,
    sent_ref,
):
    x_in = jnp.where(place_ref[0] == 0, entry_ref[...], arrived_ref[...]).astype(jnp.float32)
    encoder = place_ref[4] == 1
    skip = jnp.where(encoder, 0.0, skip_ref[plan_ref[0, 0]].astype(jnp.float32))
    conv_sum = near_ref[...] + far_ref[...].astype(jnp.float32)
    act_out = (x_in + conv_sum * column(gain_ref, stamps_ref[0, 0]) + skip).astype(jnp.bfloat16)
    cot_in = jnp.where(place_ref[3] == 1, reward_ref[...], returned_ref[...])
    out_ref[...] = act_out
    sent_ref[...] = jnp.where(encoder, act_out, cot_in)


def pair_kernel(scaled_ref, other_ref, pair_ref):
    pair_ref[0] = scaled_ref[...]
    pair_ref[1] = other_ref[...]


def gradient_kernel(
    place_ref,
    plan_ref,
    stored_ref,
    returned_ref,
    reward_ref,
    skip_ref,
    scaled_ref,
    other_ref,
    mate_ref,
    weight_ref,
    out_ref,
    whole_ref,
):
    rows = scaled_ref.shape[0]
    core, chip = place_ref[1], place_ref[2]

    def put(chip, core, block):
        whole_ref[pl.ds(pl.multiple_of((chip * 2 + core) * rows, rows), rows), :] = block

    put(chip, core, scaled_ref[...])
    put(1 - chip, core, other_ref[...])
    put(chip, 1 - core, mate_ref[0])
    put(1 - chip, 1 - core, mate_ref[1])
    _, cot_total = cotangent(place_ref, plan_ref, returned_ref, reward_ref, skip_ref)
    normed, factor = normalize(stored_ref[plan_ref[0, 1]].astype(jnp.float32))
    sigmoid = 1.0 / (1.0 + jnp.exp(-normed))
    slope = sigmoid * (1.0 + normed * (1.0 - sigmoid))
    folded = jnp.dot(weight_ref[...], whole_ref[...], preferred_element_type=jnp.float32)
    d_acted = (
        frame_shift(folded[:rows], 1)
        + folded[rows : 2 * rows]
        + frame_shift(folded[2 * rows :], -1)
    )
    d_normed = by_group(d_acted * slope)
    grouped = by_group(normed)
    result = factor * (
        d_normed - group_mean(d_normed) - grouped * group_mean(d_normed * grouped)
    )
    out_ref[...] = (cot_total + result.reshape(cot_total.shape)).astype(jnp.bfloat16)


def call(kernel, outs, specs, args, scratch=(), cost=0.0, limit=16):
    return pl.pallas_call(
        kernel,
        out_shape=[jax.ShapeDtypeStruct(shape, kind) for shape, kind in outs],
        in_specs=specs,
        out_specs=[VMEM] * len(outs),
        scratch_shapes=list(scratch),
        compiler_params=pltpu.CompilerParams(vmem_limit_bytes=limit * 2**20),
        cost_estimate=pl.CostEstimate(
            flops=int(cost * 1e9), bytes_accessed=int(cost * 1e6), transcendentals=0
        ),
        name=kernel.__name__,
    )(*args)


def local(
    act_carried,
    cot_carried,
    entry_latent,
    reward_head,
    stored_inputs,
    skip_buffer,
    conv_weight,
    time_gain,
    plan,
    timesteps,
):
    sections = lax.axis_size("section")
    section = lax.axis_index("section")
    ch = lax.axis_index("ch")
    rows, cells = act_carried.shape[1:]
    weight = conv_weight[0].reshape(3 * rows, -1)
    full = weight.shape[1]
    stored, skips = stored_inputs[0], skip_buffer[0]
    last = (section == sections - 1).astype(jnp.int32)
    encoder = (section < sections // 2).astype(jnp.int32)
    place = jnp.stack([section, ch % 2, ch // 2, last, encoder])
    field = ((rows, cells), jnp.bfloat16)
    pair = ((2, rows, cells), jnp.float32)

    arrived = shifted(act_carried[0], "section", 1)
    returned = shifted(cot_carried[0], "section", -1)
    (turned,) = call(transpose_kernel, [((full, 3 * rows), jnp.bfloat16)], [VMEM], [weight])

    mate_side, stacked = call(
        forward_kernel,
        [pair, ((3 * rows, cells), jnp.bfloat16)],
        [SMEM, VMEM, VMEM, VMEM],
        [place, arrived, entry_latent, turned],
    )
    returned, mate_side = lax.optimization_barrier((returned, mate_side))
    mate_part = swap_core(mate_side)
    (own,) = call(own_kernel, [pair], [SMEM, VMEM, VMEM], [place, turned, stacked])
    returned, own = lax.optimization_barrier((returned, own))
    (scaled,) = call(
        scaled_kernel,
        [field],
        [SMEM] * 3 + [VMEM] * 4,
        [place, plan, timesteps, returned, reward_head, skips, time_gain],
    )
    scaled, mate_part = lax.optimization_barrier((scaled, mate_part))
    other = swap_chip(scaled)
    near, far_side = call(
        halves_kernel,
        [((rows, cells), jnp.float32), field],
        [SMEM, VMEM, VMEM],
        [place, own, mate_part],
    )
    far = swap_chip(far_side)
    (gathered,) = call(
        pair_kernel,
        [((2, rows, cells), jnp.bfloat16)],
        [VMEM, VMEM],
        [scaled, other],
        cost=10.0,
    )
    far, gathered = lax.optimization_barrier((far, gathered))
    mate = swap_core(gathered)
    act_out, sent = call(
        output_kernel,
        [field, field],
        [SMEM] * 3 + [VMEM] * 8,
        [
            place,
            plan,
            timesteps,
            near,
            far,
            arrived,
            entry_latent,
            skips,
            time_gain,
            returned,
            reward_head,
        ],
    )
    mirror_in = lax.ppermute(sent, "section", [(s, sections - 1 - s) for s in range(sections)])

    mate, act_out = lax.optimization_barrier((mate, act_out))
    (cot_out,) = call(
        gradient_kernel,
        [field],
        [SMEM] * 2 + [VMEM] * 8,
        [place, plan, stored, returned, reward_head, skips, scaled, other, mate, weight],
        scratch=[pltpu.VMEM((full, cells), jnp.bfloat16)],
        cost=30.0,
    )
    mirror_in, cot_out = lax.optimization_barrier((mirror_in, cot_out))
    return (act_out[None], cot_out[None], mirror_in[None])


def solution(mesh):
    placed = (
        P("section", "ch", None),
        P("section", "ch", None),
        P("ch", None),
        P("ch", None),
        P("section", None, "ch", None),
        P("section", None, "ch", None),
        P("section", None, "ch", None),
        P(None, "ch"),
        P("section", None),
        P("section", None),
    )
    return jax.shard_map(
        local,
        mesh=mesh,
        in_specs=placed,
        out_specs=(P("section", "ch", None), P("section", "ch", None), P("section", "ch", None)),
        check_vma=False,
    )
```

time: 174 us -> 80.8 us (0.46)
  the two profiles are of different devices: /device:TPU:1 before, /device:TPU:3 now
where the time goes in v2:
time: 80.8 us; the launch traced here: 80.5 us
  starting transfers between devices  38.6 us (48%)
  waiting for transfers between devices  28.3 us (35%)
  Pallas kernels  10.1 us (12%)
  local copies, waits for them, and re-layouts  2.52 us (3%)
  between operations  0.9 us (1%)
    ppermute x1, waiting for transfers between devices, local(): lax.ppermute(sent, 'section', [(s, sections - 1 - s) for s in range(secti...  18.9 us
    ppermute x2, starting transfers between devices, shifted(): return lax.ppermute(block, axis, route)  15.6 us
    ppermute x1, starting transfers between devices, local(): lax.ppermute(sent, 'section', [(s, sections - 1 - s) for s in range(secti...  11 us
    pallas_call x8, Pallas kernels, call(): pl.pallas_call(kernel, out_shape=[jax.ShapeDtypeStruct(shape, kind) for s...  10.1 us
    ppermute x2, waiting for transfers between devices, swap_chip(): return lax.ppermute(block, 'ch', [(0, 2), (2, 0), (1, 3), (3, 1)])  8.05 us
    ppermute x2, starting transfers between devices, swap_core(): return lax.ppermute(block, 'ch', [(0, 1), (1, 0), (2, 3), (3, 2)])  6.47 us
    ppermute x2, starting transfers between devices, swap_chip(): return lax.ppermute(block, 'ch', [(0, 2), (2, 0), (1, 3), (3, 1)])  5.53 us
    unnamed x19, local copies, waits for them, and re-layouts  2.43 us
  transfers between devices with their start and end apart: 7, of which 4 were waited for; matrix products, arithmetic and copies ran while one was open for 0% of the time, Pallas kernels for 13%

profile of v2, /device:TPU:3, one launch (start us, length us, event | category | flops | bytes accessed | tf_op | source)
XLA Modules:
  0.0 80.5 jit_solution(4348495930209166058)
XLA Ops:
  0.6 4.8 %collective-permute-start.1 = (bf16[320,384]{1,0:T(8,128)(2,1)}, bf16[320,384]{1,0:T(8,128)(2,1)S(1)}, u32[]{:S(2)}, u32[]{:S(2)}) collective-permute-start(bf16[320,384]{1,0:T(8,128)(2,1)} %bitcast.20), channel_id=1, source_target_pairs={{0,4},{4,8},{8,12},{12,16},{16,20},{20,24},{24,28},{28,32},{32,36}... | collective-permute-start | bytes 737288 | tf_op jit(solution)/shard_map/ppermute | solution.py:22
  5.5 10.8 %collective-permute-start = (bf16[320,384]{1,0:T(8,128)(2,1)}, bf16[320,384]{1,0:T(8,128)(2,1)S(1)}, u32[]{:S(2)}, u32[]{:S(2)}) collective-permute-start(bf16[320,384]{1,0:T(8,128)(2,1)} %bitcast.21), channel_id=1, source_target_pairs={{4,0},{8,4},{12,8},{16,12},{20,16},{24,20},{28,24},{32,28},{36,32}... | collective-permute-start | bytes 737288 | tf_op jit(solution)/shard_map/ppermute | solution.py:22
  16.3 0.0 copy-start
  16.3 1.7 %copy-done = bf16[1,3,320,1280]{3,2,1,0:T(8,128)(2,1)S(1)} copy-done((bf16[1,3,320,1280]{3,2,1,0:T(8,128)(2,1)S(1)}, bf16[1,3,320,1280]{3,2,1,0:T(8,128)(2,1)}, u32[]{:S(2)}) %copy-start) | copy-done | bytes 2457624
  18.0 0.8 %transpose_kernel.1.weight_ref = bf16[1280,960]{1,0:T(8,128)(2,1)S(1)} custom-call(bf16[960,1280]{1,0:T(8,128)(2,1)S(1)} %bitcast.13), custom_call_target="tpu_custom_call" | custom-call | tf_op jit(solution)/shard_map/transpose_kernel/pallas_call | solution.py:193
  18.9 0.1 stack.31.place_ref
  19.0 1.3 %collective-permute-done.1.arrived_ref = bf16[320,384]{1,0:T(8,128)(2,1)S(1)} collective-permute-done((bf16[320,384]{1,0:T(8,128)(2,1)}, bf16[320,384]{1,0:T(8,128)(2,1)S(1)}, u32[]{:S(2)}, u32[]{:S(2)}) %collective-permute-start.1) | collective-permute-done | bytes 245792 | tf_op jit(solution)/shard_map/ppermute | solution.py:22
  20.2 1.9 %forward_kernel.1 = (f32[2,320,384]{2,1,0:T(8,128)S(1)}, bf16[960,384]{1,0:T(8,128)(2,1)S(1)}) custom-call(s32[5]{0:T(128)S(1)} %stack.31.place_ref, bf16[320,384]{1,0:T(8,128)(2,1)S(1)} %collective-permute-done.1.arrived_ref, bf16[320,384]{1,0:T(8,128)(2,1)S(1)} %copy-done.3, bf16[1280,960]{1,0:T(8,128)(2,1)S(1)} %transpose_kernel.1.weight_ref), custom_call_target="tpu_custom_call" | custom-call | tf_op jit(solution)/shard_map/forward_kernel/pallas_call | solution.py:193
  22.1 0.0 copy-start.2
  22.2 3.4 %collective-permute-start.2 = (f32[2,320,384]{2,1,0:T(8,128)S(1)}, f32[2,320,384]{2,1,0:T(8,128)S(1)}, u32[]{:S(2)}, u32[]{:S(2)}) collective-permute-start(f32[2,320,384]{2,1,0:T(8,128)S(1)} %get-tuple-element.26), channel_id=1, source_target_pairs={{0,1},{1,0},{2,3},{3,2},{4,5},{5,4},{6,7},{7,6},{8,9},{9,8},{10,11... | collective-permute-start | bytes 2949128 | tf_op jit(solution)/shard_map/ppermute | solution.py:26
  25.6 1.4 %own_kernel.1.own_ref = f32[2,320,384]{2,1,0:T(8,128)S(1)} custom-call(s32[5]{0:T(128)S(1)} %stack.31.place_ref, bf16[1280,960]{1,0:T(8,128)(2,1)S(1)} %transpose_kernel.1.weight_ref, bf16[960,384]{1,0:T(8,128)(2,1)S(1)} %get-tuple-element.23.stacked_ref), custom_call_target="tpu_custom_call" | custom-call | tf_op jit(solution)/shard_map/own_kernel/pallas_call | solution.py:193
  27.0 0.7 scaled_kernel.1.scaled_ref
  27.7 0.0 collective-permute-done.2.mate_ref
  27.7 2.3 %collective-permute-start.4 = (bf16[320,384]{1,0:T(8,128)(2,1)S(1)}, bf16[320,384]{1,0:T(8,128)(2,1)S(1)}, u32[]{:S(2)}, u32[]{:S(2)}) collective-permute-start(bf16[320,384]{1,0:T(8,128)(2,1)S(1)} %scaled_kernel.1.scaled_ref), channel_id=1, source_target_pairs={{0,2},{2,0},{1,3},{3,1},{4,6},{6,4},{5,7},{7,5},{8,10},{10,8},{9,1... | collective-permute-start | bytes 737288 | tf_op jit(solution)/shard_map/ppermute | solution.py:30
  30.0 0.6 halves_kernel.1
  30.7 3.2 %collective-permute-start.3 = (bf16[320,384]{1,0:T(8,128)(2,1)S(1)}, bf16[320,384]{1,0:T(8,128)(2,1)S(1)}, u32[]{:S(2)}, u32[]{:S(2)}) collective-permute-start(bf16[320,384]{1,0:T(8,128)(2,1)S(1)} %get-tuple-element.28), channel_id=1, source_target_pairs={{0,2},{2,0},{1,3},{3,1},{4,6},{6,4},{5,7},{7,5},{8,10},{10,8},{9,1... | collective-permute-start | bytes 737288 | tf_op jit(solution)/shard_map/ppermute | solution.py:30
  34.0 2.8 %collective-permute-done.4.other_ref = bf16[320,384]{1,0:T(8,128)(2,1)S(1)} collective-permute-done((bf16[320,384]{1,0:T(8,128)(2,1)S(1)}, bf16[320,384]{1,0:T(8,128)(2,1)S(1)}, u32[]{:S(2)}, u32[]{:S(2)}) %collective-permute-start.4) | collective-permute-done | bytes 245792 | tf_op jit(solution)/shard_map/ppermute | solution.py:30
  36.8 5.2 %collective-permute-done.3.far_ref = bf16[320,384]{1,0:T(8,128)(2,1)S(1)} collective-permute-done((bf16[320,384]{1,0:T(8,128)(2,1)S(1)}, bf16[320,384]{1,0:T(8,128)(2,1)S(1)}, u32[]{:S(2)}, u32[]{:S(2)}) %collective-permute-start.3) | collective-permute-done | bytes 245792 | tf_op jit(solution)/shard_map/ppermute | solution.py:30
  42.0 3.1 %collective-permute-start.5 = (bf16[2,320,384]{2,1,0:T(8,128)(2,1)S(1)}, bf16[2,320,384]{2,1,0:T(8,128)(2,1)S(1)}, u32[]{:S(2)}, u32[]{:S(2)}) collective-permute-start(bf16[2,320,384]{2,1,0:T(8,128)(2,1)S(1)} %pair_kernel.1), channel_id=1, source_target_pairs={{0,1},{1,0},{2,3},{3,2},{4,5},{5,4},{6,7},{7,6},{8,9},{9,8},{10,11... | collective-permute-start | bytes 1474568 | tf_op jit(solution)/shard_map/ppermute | solution.py:26
  45.2 1.5 %output_kernel.1 = (bf16[320,384]{1,0:T(8,128)(2,1)}, bf16[320,384]{1,0:T(8,128)(2,1)S(1)}) custom-call(s32[5]{0:T(128)S(1)} %stack.31.place_ref, s32[1,2]{1,0:T(1,128)S(1)} %copy-done.7, s32[1,2]{1,0:T(1,128)S(1)} %copy-done.6, f32[320,384]{1,0:T(8,128)S(1)} %get-tuple-element.31.near_ref, bf16[320,384]{1,0:T(8,128)(2,1)S(1)} %collective-permute-done.3.far_ref, ...), custom_call_target="tpu_custom_call" | custom-call | tf_op jit(solution)/shard_map/output_kernel/pallas_call | solution.py:193
  46.7 11.0 %collective-permute-start.6 = (bf16[320,384]{1,0:T(8,128)(2,1)S(1)}, bf16[320,384]{1,0:T(8,128)(2,1)S(1)}, u32[]{:S(2)}, u32[]{:S(2)}) collective-permute-start(bf16[320,384]{1,0:T(8,128)(2,1)S(1)} %get-tuple-element.35), channel_id=1, source_target_pairs={{0,508},{4,504},{8,500},{12,496},{16,492},{20,488},{24,484},{28,48... | collective-permute-start | bytes 737288 | tf_op jit(solution)/shard_map/ppermute | solution.py:288
  57.7 3.1 %gradient_kernel.1 = bf16[320,384]{1,0:T(8,128)(2,1)} custom-call(s32[5]{0:T(128)S(1)} %stack.31.place_ref, s32[1,2]{1,0:T(1,128)S(1)} %copy-done.7, bf16[2,320,384]{2,1,0:T(8,128)(2,1)S(1)} %bitcast.18, bf16[320,384]{1,0:T(8,128)(2,1)S(1)} %collective-permute-done.returned_ref, bf16[320,384]{1,0:T(8,128)(2,1)S(1)} %copy-done.4, ...), custom_call_target="tpu_custom_call" | custom-call | flops 30000001024 | bytes 30000000 | tf_op jit(solution)/shard_map/gradient_kernel/pallas_call | solution.py:193
  60.8 18.9 %collective-permute-done.6 = bf16[320,384]{1,0:T(8,128)(2,1)S(1)} collective-permute-done((bf16[320,384]{1,0:T(8,128)(2,1)S(1)}, bf16[320,384]{1,0:T(8,128)(2,1)S(1)}, u32[]{:S(2)}, u32[]{:S(2)}) %collective-permute-start.6) | collective-permute-done | bytes 245792 | tf_op jit(solution)/shard_map/ppermute | solution.py:288
  79.8 0.7 copy.14
  (18 shorter events, 0.1 us)
Async XLA Ops:
  0.6 19.6 %collective-permute-start.1 = (bf16[320,384]{1,0:T(8,128)(2,1)}, bf16[320,384]{1,0:T(8,128)(2,1)S(1)}, u32[]{:S(2)}, u32[]{:S(2)}) collective-permute-start(bf16[320,384]{1,0:T(8,128)(2,1)} %bitcast.20), channel_id=1, source_target_pairs={{0,4},{4,8},{8,12},{12,16},{16,20},{20,24},{24,28},{28,32},{32,36}... | collective-permute-start | bytes 737288 | tf_op jit(solution)/shard_map/ppermute | solution.py:22
  5.5 16.7 %collective-permute-start = (bf16[320,384]{1,0:T(8,128)(2,1)}, bf16[320,384]{1,0:T(8,128)(2,1)S(1)}, u32[]{:S(2)}, u32[]{:S(2)}) collective-permute-start(bf16[320,384]{1,0:T(8,128)(2,1)} %bitcast.21), channel_id=1, source_target_pairs={{4,0},{8,4},{12,8},{16,12},{20,16},{24,20},{28,24},{32,28},{36,32}... | collective-permute-start | bytes 737288 | tf_op jit(solution)/shard_map/ppermute | solution.py:22
  16.3 1.7 %copy-start = (bf16[1,3,320,1280]{3,2,1,0:T(8,128)(2,1)S(1)}, bf16[1,3,320,1280]{3,2,1,0:T(8,128)(2,1)}, u32[]{:S(2)}) copy-start(bf16[1,3,320,1280]{3,2,1,0:T(8,128)(2,1)} %param.16) | copy-start | bytes 7372804
  18.0 2.2 %copy-start.3 = (bf16[320,384]{1,0:T(8,128)(2,1)S(1)}, bf16[320,384]{1,0:T(8,128)(2,1)}, u32[]{:S(2)}) copy-start(bf16[320,384]{1,0:T(8,128)(2,1)} %entry_ref.3) | copy-start | bytes 737284
  22.1 4.8 %copy-start.2 = (bf16[1,2,320,384]{3,2,1,0:T(8,128)(2,1)S(1)}, bf16[1,2,320,384]{3,2,1,0:T(8,128)(2,1)}, u32[]{:S(2)}) copy-start(bf16[1,2,320,384]{3,2,1,0:T(8,128)(2,1)} %param.15) | copy-start | bytes 1474564
  22.1 4.8 %copy-start.4 = (bf16[320,384]{1,0:T(8,128)(2,1)S(1)}, bf16[320,384]{1,0:T(8,128)(2,1)}, u32[]{:S(2)}) copy-start(bf16[320,384]{1,0:T(8,128)(2,1)} %reward_ref.5) | copy-start | bytes 737284
  22.1 4.8 %copy-start.5 = (f32[25,320]{1,0:T(8,128)S(1)}, f32[25,320]{1,0:T(8,128)}, u32[]{:S(2)}) copy-start(f32[25,320]{1,0:T(8,128)} %gain_ref.3) | copy-start | bytes 96004
  22.1 4.8 %copy-start.6 = (s32[1,2]{1,0:T(1,128)S(1)}, s32[1,2]{1,0:T(1,128)}, u32[]{:S(2)}) copy-start(s32[1,2]{1,0:T(1,128)} %stamps_ref.3) | copy-start | bytes 28
  22.2 4.8 %copy-start.7 = (s32[1,2]{1,0:T(1,128)S(1)}, s32[1,2]{1,0:T(1,128)}, u32[]{:S(2)}) copy-start(s32[1,2]{1,0:T(1,128)} %plan_ref.5) | copy-start | bytes 28
  22.2 5.5 %collective-permute-start.2 = (f32[2,320,384]{2,1,0:T(8,128)S(1)}, f32[2,320,384]{2,1,0:T(8,128)S(1)}, u32[]{:S(2)}, u32[]{:S(2)}) collective-permute-start(f32[2,320,384]{2,1,0:T(8,128)S(1)} %get-tuple-element.26), channel_id=1, source_target_pairs={{0,1},{1,0},{2,3},{3,2},{4,5},{5,4},{6,7},{7,6},{8,9},{9,8},{10,11... | collective-permute-start | bytes 2949128 | tf_op jit(solution)/shard_map/ppermute | solution.py:26
  27.7 9.1 %collective-permute-start.4 = (bf16[320,384]{1,0:T(8,128)(2,1)S(1)}, bf16[320,384]{1,0:T(8,128)(2,1)S(1)}, u32[]{:S(2)}, u32[]{:S(2)}) collective-permute-start(bf16[320,384]{1,0:T(8,128)(2,1)S(1)} %scaled_kernel.1.scaled_ref), channel_id=1, source_target_pairs={{0,2},{2,0},{1,3},{3,1},{4,6},{6,4},{5,7},{7,5},{8,10},{10,8},{9,1... | collective-permute-start | bytes 737288 | tf_op jit(solution)/shard_map/ppermute | solution.py:30
  30.7 27.0 %copy-start.1 = (bf16[1,3,320,1280]{3,2,1,0:T(8,128)(2,1)S(1)}, bf16[1,3,320,1280]{3,2,1,0:T(8,128)(2,1)}, u32[]{:S(2)}) copy-start(bf16[1,3,320,1280]{3,2,1,0:T(8,128)(2,1)} %param.16) | copy-start | bytes 7372804
  30.7 27.0 %copy-start.8 = (bf16[1,2,320,384]{3,2,1,0:T(8,128)(2,1)S(1)}, bf16[1,2,320,384]{3,2,1,0:T(8,128)(2,1)}, u32[]{:S(2)}) copy-start(bf16[1,2,320,384]{3,2,1,0:T(8,128)(2,1)} %param.14) | copy-start | bytes 1474564
  30.7 11.3 %collective-permute-start.3 = (bf16[320,384]{1,0:T(8,128)(2,1)S(1)}, bf16[320,384]{1,0:T(8,128)(2,1)S(1)}, u32[]{:S(2)}, u32[]{:S(2)}) collective-permute-start(bf16[320,384]{1,0:T(8,128)(2,1)S(1)} %get-tuple-element.28), channel_id=1, source_target_pairs={{0,2},{2,0},{1,3},{3,1},{4,6},{6,4},{5,7},{7,5},{8,10},{10,8},{9,1... | collective-permute-start | bytes 737288 | tf_op jit(solution)/shard_map/ppermute | solution.py:30
  42.0 15.6 %collective-permute-start.5 = (bf16[2,320,384]{2,1,0:T(8,128)(2,1)S(1)}, bf16[2,320,384]{2,1,0:T(8,128)(2,1)S(1)}, u32[]{:S(2)}, u32[]{:S(2)}) collective-permute-start(bf16[2,320,384]{2,1,0:T(8,128)(2,1)S(1)} %pair_kernel.1), channel_id=1, source_target_pairs={{0,1},{1,0},{2,3},{3,2},{4,5},{5,4},{6,7},{7,6},{8,9},{9,8},{10,11... | collective-permute-start | bytes 1474568 | tf_op jit(solution)/shard_map/ppermute | solution.py:26
  46.7 33.1 %collective-permute-start.6 = (bf16[320,384]{1,0:T(8,128)(2,1)S(1)}, bf16[320,384]{1,0:T(8,128)(2,1)S(1)}, u32[]{:S(2)}, u32[]{:S(2)}) collective-permute-start(bf16[320,384]{1,0:T(8,128)(2,1)S(1)} %get-tuple-element.35), channel_id=1, source_target_pairs={{0,508},{4,504},{8,500},{12,496},{16,492},{20,488},{24,484},{28,48... | collective-permute-start | bytes 737288 | tf_op jit(solution)/shard_map/ppermute | solution.py:288

commit v3 on v2

--- a/solution.py
+++ b/solution.py
@@ -127,36 +127,39 @@
     entry_ref,
     skip_ref,
     gain_ref,
-    returned_ref,
-    reward_ref,
     out_ref,
-    sent_ref,
 ):
     x_in = jnp.where(place_ref[0] == 0, entry_ref[...], arrived_ref[...]).astype(jnp.float32)
-    encoder = place_ref[4] == 1
-    skip = jnp.where(encoder, 0.0, skip_ref[plan_ref[0, 0]].astype(jnp.float32))
+    skip = jnp.where(place_ref[4] == 1, 0.0, skip_ref[plan_ref[0, 0]].astype(jnp.float32))
     conv_sum = near_ref[...] + far_ref[...].astype(jnp.float32)
     act_out = (x_in + conv_sum * column(gain_ref, stamps_ref[0, 0]) + skip).astype(jnp.bfloat16)
-    cot_in = jnp.where(place_ref[3] == 1, reward_ref[...], returned_ref[...])
     out_ref[...] = act_out
-    sent_ref[...] = jnp.where(encoder, act_out, cot_in)
-
-
-def pair_kernel(scaled_ref, other_ref, pair_ref):
-    pair_ref[0] = scaled_ref[...]
-    pair_ref[1] = other_ref[...]
+
+
+def choose_kernel(place_ref, cot_ref, act_ref, reward_ref, out_ref):
+    cot = jnp.where(place_ref[0] == 0, reward_ref[...], cot_ref[...])
+    out_ref[...] = jnp.where(place_ref[4] == 1, cot, act_ref[...])
+
+
+def saved_kernel(plan_ref, stored_ref, normed_ref, factor_ref):
+    normed, factor = normalize(stored_ref[plan_ref[0, 1]].astype(jnp.float32))
+    normed_ref[...] = normed
+    factor_ref[...] = jnp.broadcast_to(factor, factor_ref.shape)
 
 
 def gradient_kernel(
     place_ref,
     plan_ref,
-    stored_ref,
+    normed_ref,
+    factor_ref,
     returned_ref,
     reward_ref,
     skip_ref,
     scaled_ref,
     other_ref,
     mate_ref,
+    mate_low_ref,
+    mate_high_ref,
     weight_ref,
     out_ref,
     whole_ref,
@@ -164,15 +167,17 @@
     rows = scaled_ref.shape[0]
     core, chip = place_ref[1], place_ref[2]
 
-    def put(chip, core, block):
-        whole_ref[pl.ds(pl.multiple_of((chip * 2 + core) * rows, rows), rows), :] = block
+    def put(chip, core, block, skipped=0):
+        start = pl.multiple_of((chip * 2 + core) * rows + skipped, 32)
+        whole_ref[pl.ds(start, block.shape[0]), :] = block
 
     put(chip, core, scaled_ref[...])
     put(1 - chip, core, other_ref[...])
-    put(chip, 1 - core, mate_ref[0])
-    put(1 - chip, 1 - core, mate_ref[1])
+    put(chip, 1 - core, mate_ref[...])
+    put(1 - chip, 1 - core, mate_low_ref[...])
+    put(1 - chip, 1 - core, mate_high_ref[...], rows // 2)
     _, cot_total = cotangent(place_ref, plan_ref, returned_ref, reward_ref, skip_ref)
-    normed, factor = normalize(stored_ref[plan_ref[0, 1]].astype(jnp.float32))
+    normed = normed_ref[...]
     sigmoid = 1.0 / (1.0 + jnp.exp(-normed))
     slope = sigmoid * (1.0 + normed * (1.0 - sigmoid))
     folded = jnp.dot(weight_ref[...], whole_ref[...], preferred_element_type=jnp.float32)
@@ -183,7 +188,7 @@
     )
     d_normed = by_group(d_acted * slope)
     grouped = by_group(normed)
-    result = factor * (
+    result = factor_ref[:, :1, :1] * (
         d_normed - group_mean(d_normed) - grouped * group_mean(d_normed * grouped)
     )
     out_ref[...] = (cot_total + result.reshape(cot_total.shape)).astype(jnp.bfloat16)
@@ -230,8 +235,11 @@
     pair = ((2, rows, cells), jnp.float32)
 
     arrived = shifted(act_carried[0], "section", 1)
-    returned = shifted(cot_carried[0], "section", -1)
-    (turned,) = call(transpose_kernel, [((full, 3 * rows), jnp.bfloat16)], [VMEM], [weight])
+    (turned,) = call(transpose_kernel, [((full, 3 * rows), jnp.bfloat16)], [VMEM], [weight], cost=20.0)
+    cotangents, turned = lax.optimization_barrier((cot_carried[0], turned))
+    mirrored_cot = lax.ppermute(
+        cotangents, "section", [(sections - s, s) for s in range(1, sections // 2)]
+    )
 
     mate_side, stacked = call(
         forward_kernel,
@@ -239,64 +247,63 @@
         [SMEM, VMEM, VMEM, VMEM],
         [place, arrived, entry_latent, turned],
     )
-    returned, mate_side = lax.optimization_barrier((returned, mate_side))
     mate_part = swap_core(mate_side)
-    (own,) = call(own_kernel, [pair], [SMEM, VMEM, VMEM], [place, turned, stacked])
-    returned, own = lax.optimization_barrier((returned, own))
+    cotangents, mate_side = lax.optimization_barrier((cotangents, mate_side))
+    returned = shifted(cotangents, "section", -1)
+    (own,) = call(own_kernel, [pair], [SMEM, VMEM, VMEM], [place, turned, stacked], cost=20.0)
+    near, far_side = call(
+        halves_kernel,
+        [((rows, cells), jnp.float32), field],
+        [SMEM, VMEM, VMEM],
+        [place, own, mate_part],
+    )
+    far = swap_chip(far_side)
+    returned, far_side = lax.optimization_barrier((returned, far_side))
     (scaled,) = call(
         scaled_kernel,
         [field],
         [SMEM] * 3 + [VMEM] * 4,
         [place, plan, timesteps, returned, reward_head, skips, time_gain],
     )
-    scaled, mate_part = lax.optimization_barrier((scaled, mate_part))
     other = swap_chip(scaled)
-    near, far_side = call(
-        halves_kernel,
-        [((rows, cells), jnp.float32), field],
-        [SMEM, VMEM, VMEM],
-        [place, own, mate_part],
-    )
-    far = swap_chip(far_side)
-    (gathered,) = call(
-        pair_kernel,
-        [((2, rows, cells), jnp.bfloat16)],
-        [VMEM, VMEM],
-        [scaled, other],
-        cost=10.0,
-    )
-    far, gathered = lax.optimization_barrier((far, gathered))
-    mate = swap_core(gathered)
-    act_out, sent = call(
+    stored, far_side = lax.optimization_barrier((stored, far_side))
+    saved_normed, saved_factor = call(
+        saved_kernel,
+        [((rows, cells), jnp.float32), ((rows // WIDTH, 8, 128), jnp.float32)],
+        [SMEM, VMEM],
+        [plan, stored],
+        cost=20.0,
+    )
+    far, scaled, saved_normed = lax.optimization_barrier((far, scaled, saved_normed))
+    (act_out,) = call(
         output_kernel,
-        [field, field],
-        [SMEM] * 3 + [VMEM] * 8,
-        [
-            place,
-            plan,
-            timesteps,
-            near,
-            far,
-            arrived,
-            entry_latent,
-            skips,
-            time_gain,
-            returned,
-            reward_head,
-        ],
-    )
-    mirror_in = lax.ppermute(sent, "section", [(s, sections - 1 - s) for s in range(sections)])
-
-    mate, act_out = lax.optimization_barrier((mate, act_out))
+        [field],
+        [SMEM] * 3 + [VMEM] * 6,
+        [place, plan, timesteps, near, far, arrived, entry_latent, skips, time_gain],
+    )
+    mirrored_act = lax.ppermute(
+        act_out, "section", [(s, sections - 1 - s) for s in range(sections // 2)]
+    )
+
+    other, scaled, act_out = lax.optimization_barrier((other, scaled, act_out))
+    half = rows // 2
+    mates = [swap_core(part) for part in (scaled, other[:half], other[half:])]
     (cot_out,) = call(
         gradient_kernel,
         [field],
-        [SMEM] * 2 + [VMEM] * 8,
-        [place, plan, stored, returned, reward_head, skips, scaled, other, mate, weight],
+        [SMEM] * 2 + [VMEM] * 11,
+        [place, plan, saved_normed, saved_factor, returned, reward_head, skips, scaled, other, *mates, weight],
         scratch=[pltpu.VMEM((full, cells), jnp.bfloat16)],
-        cost=30.0,
-    )
-    mirror_in, cot_out = lax.optimization_barrier((mirror_in, cot_out))
+    )
+    mirrored_cot, mirrored_act, cot_out = lax.optimization_barrier(
+        (mirrored_cot, mirrored_act, cot_out)
+    )
+    (mirror_in,) = call(
+        choose_kernel,
+        [field],
+        [SMEM] + [VMEM] * 3,
+        [place, mirrored_cot, mirrored_act, reward_head],
+    )
     return (act_out[None], cot_out[None], mirror_in[None])
 
 

time: 80.8 us -> 79.8 us (0.988)
  the two profiles are of different devices: /device:TPU:3 before, /device:TPU:1 now
where the time goes in v3:
time: 79.8 us; the launch traced here: 79.2 us
  starting transfers between devices  51.1 us (64%)
  waiting for transfers between devices  13.3 us (17%)
  Pallas kernels  12.1 us (15%)
  local copies, waits for them, and re-layouts  1.85 us (2%)
  between operations  0.91 us (1%)
    ppermute x1, starting transfers between devices, local(): lax.ppermute(act_out, 'section', [(s, sections - 1 - s) for s in range(se...  26.3 us
    ppermute x4, starting transfers between devices, swap_core(): return lax.ppermute(block, 'ch', [(0, 1), (1, 0), (2, 3), (3, 2)])  12.7 us
    pallas_call x9, Pallas kernels, call(): pl.pallas_call(kernel, out_shape=[jax.ShapeDtypeStruct(shape, kind) for s...  12.1 us
    ppermute x2, starting transfers between devices, shifted(): return lax.ppermute(block, axis, route)  6.95 us
    ppermute x2, waiting for transfers between devices, shifted(): return lax.ppermute(block, axis, route)  6.44 us
    ppermute x2, starting transfers between devices, swap_chip(): return lax.ppermute(block, 'ch', [(0, 2), (2, 0), (1, 3), (3, 1)])  4.48 us
    ppermute x1, waiting for transfers between devices, local(): lax.ppermute(act_out, 'section', [(s, sections - 1 - s) for s in range(se...  3.37 us
    ppermute x2, waiting for transfers between devices, swap_chip(): return lax.ppermute(block, 'ch', [(0, 2), (2, 0), (1, 3), (3, 1)])  2.49 us
  transfers between devices with their start and end apart: 10, of which 5 were waited for; matrix products, arithmetic and copies ran while one was open for 0% of the time, Pallas kernels for 14%

profile of v3, /device:TPU:1, one launch (start us, length us, event | category | flops | bytes accessed | tf_op | source)
XLA Modules:
  0.0 79.2 jit_solution(13619238880506267054)
XLA Ops:
  0.6 5.7 %collective-permute-start = (bf16[320,384]{1,0:T(8,128)(2,1)}, bf16[320,384]{1,0:T(8,128)(2,1)S(1)}, u32[]{:S(2)}, u32[]{:S(2)}) collective-permute-start(bf16[320,384]{1,0:T(8,128)(2,1)} %bitcast.22), channel_id=1, source_target_pairs={{0,4},{4,8},{8,12},{12,16},{16,20},{20,24},{24,28},{28,32},{32,36}... | collective-permute-start | bytes 737288 | tf_op jit(solution)/shard_map/ppermute | solution.py:22
  6.3 1.7 %copy-done.1 = bf16[1,3,320,1280]{3,2,1,0:T(8,128)(2,1)S(1)} copy-done((bf16[1,3,320,1280]{3,2,1,0:T(8,128)(2,1)S(1)}, bf16[1,3,320,1280]{3,2,1,0:T(8,128)(2,1)}, u32[]{:S(2)}) %copy-start.1) | copy-done | bytes 2457624
  8.0 0.8 %transpose_kernel.1.weight_ref = bf16[1280,960]{1,0:T(8,128)(2,1)S(1)} custom-call(bf16[960,1280]{1,0:T(8,128)(2,1)S(1)} %bitcast.16), custom_call_target="tpu_custom_call" | custom-call | flops 20000000000 | bytes 20000000 | tf_op jit(solution)/shard_map/transpose_kernel/pallas_call | solution.py:198
  8.8 0.7 collective-permute-start.5
  9.7 1.9 %forward_kernel.1 = (f32[2,320,384]{2,1,0:T(8,128)S(1)}, bf16[960,384]{1,0:T(8,128)(2,1)S(1)}) custom-call(s32[5]{0:T(128)S(1)} %stack.31.place_ref, bf16[320,384]{1,0:T(8,128)(2,1)S(1)} %collective-permute-done.arrived_ref, bf16[320,384]{1,0:T(8,128)(2,1)S(1)} %copy-done.4, bf16[1280,960]{1,0:T(8,128)(2,1)S(1)} %transpose_kernel.1.weight_ref), custom_call_target="tpu_custom_call" | custom-call | tf_op jit(solution)/shard_map/forward_kernel/pallas_call | solution.py:198
  11.6 5.0 %collective-permute-start.2 = (f32[2,320,384]{2,1,0:T(8,128)S(1)}, f32[2,320,384]{2,1,0:T(8,128)S(1)}, u32[]{:S(2)}, u32[]{:S(2)}) collective-permute-start(f32[2,320,384]{2,1,0:T(8,128)S(1)} %get-tuple-element.24), channel_id=1, source_target_pairs={{0,1},{1,0},{2,3},{3,2},{4,5},{5,4},{6,7},{7,6},{8,9},{9,8},{10,11... | collective-permute-start | bytes 2949128 | tf_op jit(solution)/shard_map/ppermute | solution.py:26
  16.6 1.3 %collective-permute-start.1 = (bf16[320,384]{1,0:T(8,128)(2,1)}, bf16[320,384]{1,0:T(8,128)(2,1)S(1)}, u32[]{:S(2)}, u32[]{:S(2)}) collective-permute-start(bf16[320,384]{1,0:T(8,128)(2,1)} %bitcast.5), channel_id=1, source_target_pairs={{4,0},{8,4},{12,8},{16,12},{20,16},{24,20},{28,24},{32,28},{36,32}... | collective-permute-start | bytes 737288 | tf_op jit(solution)/shard_map/ppermute | solution.py:22
  18.0 1.4 %own_kernel.1.own_ref = f32[2,320,384]{2,1,0:T(8,128)S(1)} custom-call(s32[5]{0:T(128)S(1)} %stack.31.place_ref, bf16[1280,960]{1,0:T(8,128)(2,1)S(1)} %transpose_kernel.1.weight_ref, bf16[960,384]{1,0:T(8,128)(2,1)S(1)} %get-tuple-element.26.stacked_ref), custom_call_target="tpu_custom_call" | custom-call | flops 20000000000 | bytes 20000000 | tf_op jit(solution)/shard_map/own_kernel/pallas_call | solution.py:198
  19.4 0.6 halves_kernel.1
  20.0 2.2 %collective-permute-start.4 = (bf16[320,384]{1,0:T(8,128)(2,1)S(1)}, bf16[320,384]{1,0:T(8,128)(2,1)S(1)}, u32[]{:S(2)}, u32[]{:S(2)}) collective-permute-start(bf16[320,384]{1,0:T(8,128)(2,1)S(1)} %get-tuple-element.27), channel_id=1, source_target_pairs={{0,2},{2,0},{1,3},{3,1},{4,6},{6,4},{5,7},{7,5},{8,10},{10,8},{9,1... | collective-permute-start | bytes 737288 | tf_op jit(solution)/shard_map/ppermute | solution.py:30
  22.3 6.4 %collective-permute-done.1.returned_ref = bf16[320,384]{1,0:T(8,128)(2,1)S(1)} collective-permute-done((bf16[320,384]{1,0:T(8,128)(2,1)}, bf16[320,384]{1,0:T(8,128)(2,1)S(1)}, u32[]{:S(2)}, u32[]{:S(2)}) %collective-permute-start.1) | collective-permute-done | bytes 245792 | tf_op jit(solution)/shard_map/ppermute | solution.py:22
  28.7 0.7 scaled_kernel.1.scaled_ref
  29.4 2.2 %collective-permute-start.3 = (bf16[320,384]{1,0:T(8,128)(2,1)S(1)}, bf16[320,384]{1,0:T(8,128)(2,1)S(1)}, u32[]{:S(2)}, u32[]{:S(2)}) collective-permute-start(bf16[320,384]{1,0:T(8,128)(2,1)S(1)} %scaled_kernel.1.scaled_ref), channel_id=1, source_target_pairs={{0,2},{2,0},{1,3},{3,1},{4,6},{6,4},{5,7},{7,5},{8,10},{10,8},{9,1... | collective-permute-start | bytes 737288 | tf_op jit(solution)/shard_map/ppermute | solution.py:30
  31.6 0.8 %saved_kernel.1 = (f32[320,384]{1,0:T(8,128)S(1)}, f32[8,8,128]{2,1,0:T(8,128)S(1)}) custom-call(s32[1,2]{1,0:T(1,128)S(1)} %copy-done.6, bf16[2,320,384]{2,1,0:T(8,128)(2,1)S(1)} %bitcast.18), custom_call_target="tpu_custom_call" | custom-call | flops 20000000000 | bytes 20000000 | tf_op jit(solution)/shard_map/saved_kernel/pallas_call | solution.py:198
  32.4 2.5 %collective-permute-done.4.far_ref = bf16[320,384]{1,0:T(8,128)(2,1)S(1)} collective-permute-done((bf16[320,384]{1,0:T(8,128)(2,1)S(1)}, bf16[320,384]{1,0:T(8,128)(2,1)S(1)}, u32[]{:S(2)}, u32[]{:S(2)}) %collective-permute-start.4) | collective-permute-done | bytes 245792 | tf_op jit(solution)/shard_map/ppermute | solution.py:30
  34.9 1.4 %output_kernel.1 = bf16[320,384]{1,0:T(8,128)(2,1)} custom-call(s32[5]{0:T(128)S(1)} %stack.31.place_ref, s32[1,2]{1,0:T(1,128)S(1)} %copy-done.6, s32[1,2]{1,0:T(1,128)S(1)} %copy-done.7, f32[320,384]{1,0:T(8,128)S(1)} %get-tuple-element.31.near_ref, bf16[320,384]{1,0:T(8,128)(2,1)S(1)} %collective-permute-done.4.far_ref, ...), custom_call_target="tpu_custom_call" | custom-call | tf_op jit(solution)/shard_map/output_kernel/pallas_call | solution.py:198
  36.4 26.3 %collective-permute-start.6 = (bf16[320,384]{1,0:T(8,128)(2,1)}, bf16[320,384]{1,0:T(8,128)(2,1)S(1)}, u32[]{:S(2)}, u32[]{:S(2)}) collective-permute-start(bf16[320,384]{1,0:T(8,128)(2,1)} %output_kernel.1), channel_id=1, source_target_pairs={{0,508},{4,504},{8,500},{12,496},{16,492},{20,488},{24,484},{28,48... | collective-permute-start | bytes 737288 | tf_op jit(solution)/shard_map/ppermute | solution.py:284
  62.6 3.4 %collective-permute-start.7 = (bf16[320,384]{1,0:T(8,128)(2,1)S(1)}, bf16[320,384]{1,0:T(8,128)(2,1)S(1)}, u32[]{:S(2)}, u32[]{:S(2)}) collective-permute-start(bf16[320,384]{1,0:T(8,128)(2,1)S(1)} %scaled_kernel.1.scaled_ref), channel_id=1, source_target_pairs={{0,1},{1,0},{2,3},{3,2},{4,5},{5,4},{6,7},{7,6},{8,9},{9,8},{10,11... | collective-permute-start | bytes 737288 | tf_op jit(solution)/shard_map/ppermute | solution.py:26
  66.1 1.9 %collective-permute-start.8 = (bf16[160,384]{1,0:T(8,128)(2,1)S(1)}, bf16[160,384]{1,0:T(8,128)(2,1)S(1)}, u32[]{:S(2)}, u32[]{:S(2)}) collective-permute-start(bf16[160,384]{1,0:T(8,128)(2,1)S(1)} %get-tuple-element.42), channel_id=1, source_target_pairs={{0,1},{1,0},{2,3},{3,2},{4,5},{5,4},{6,7},{7,6},{8,9},{9,8},{10,11... | collective-permute-start | bytes 368648 | tf_op jit(solution)/shard_map/ppermute | solution.py:26
  68.0 2.4 %collective-permute-start.9 = (bf16[160,384]{1,0:T(8,128)(2,1)S(1)}, bf16[160,384]{1,0:T(8,128)(2,1)S(1)}, u32[]{:S(2)}, u32[]{:S(2)}) collective-permute-start(bf16[160,384]{1,0:T(8,128)(2,1)S(1)} %get-tuple-element.41), channel_id=1, source_target_pairs={{0,1},{1,0},{2,3},{3,2},{4,5},{5,4},{6,7},{7,6},{8,9},{9,8},{10,11... | collective-permute-start | bytes 368648 | tf_op jit(solution)/shard_map/ppermute | solution.py:26
  70.4 0.9 %collective-permute-done.9.mate_high_ref = bf16[160,384]{1,0:T(8,128)(2,1)S(1)} collective-permute-done((bf16[160,384]{1,0:T(8,128)(2,1)S(1)}, bf16[160,384]{1,0:T(8,128)(2,1)S(1)}, u32[]{:S(2)}, u32[]{:S(2)}) %collective-permute-start.9) | collective-permute-done | bytes 122912 | tf_op jit(solution)/shard_map/ppermute | solution.py:26
  71.4 3.2 %gradient_kernel.1 = bf16[320,384]{1,0:T(8,128)(2,1)} custom-call(s32[5]{0:T(128)S(1)} %stack.31.place_ref, s32[1,2]{1,0:T(1,128)S(1)} %copy-done.6, f32[320,384]{1,0:T(8,128)S(1)} %get-tuple-element.34.normed_ref, f32[8,8,128]{2,1,0:T(8,128)S(1)} %get-tuple-element.35.factor_ref, bf16[320,384]{1,0:T(8,128)(2,1)S(1)} %collective-permute-done.1.returned_ref, ...), custom_call_target="tpu_custom_call" | custom-call | tf_op jit(solution)/shard_map/gradient_kernel/pallas_call | solution.py:198
  74.6 3.4 %collective-permute-done.6.act_ref = bf16[320,384]{1,0:T(8,128)(2,1)S(1)} collective-permute-done((bf16[320,384]{1,0:T(8,128)(2,1)}, bf16[320,384]{1,0:T(8,128)(2,1)S(1)}, u32[]{:S(2)}, u32[]{:S(2)}) %collective-permute-start.6) | collective-permute-done | bytes 245792 | tf_op jit(solution)/shard_map/ppermute | solution.py:284
  78.0 1.3 %choose_kernel.1 = bf16[320,384]{1,0:T(8,128)(2,1)} custom-call(s32[5]{0:T(128)S(1)} %stack.31.place_ref, bf16[320,384]{1,0:T(8,128)(2,1)S(1)} %collective-permute-done.5.cot_ref, bf16[320,384]{1,0:T(8,128)(2,1)S(1)} %collective-permute-done.6.act_ref, bf16[320,384]{1,0:T(8,128)(2,1)S(1)} %copy-done.3), custom_call_target="tpu_custom_call" | custom-call | tf_op jit(solution)/shard_map/choose_kernel/pallas_call | solution.py:198
  (25 shorter events, 0.3 us)
Async XLA Ops:
  0.6 9.1 %collective-permute-start = (bf16[320,384]{1,0:T(8,128)(2,1)}, bf16[320,384]{1,0:T(8,128)(2,1)S(1)}, u32[]{:S(2)}, u32[]{:S(2)}) collective-permute-start(bf16[320,384]{1,0:T(8,128)(2,1)} %bitcast.22), channel_id=1, source_target_pairs={{0,4},{4,8},{8,12},{12,16},{16,20},{20,24},{24,28},{28,32},{32,36}... | collective-permute-start | bytes 737288 | tf_op jit(solution)/shard_map/ppermute | solution.py:22
  6.3 1.7 %copy-start.1 = (bf16[1,3,320,1280]{3,2,1,0:T(8,128)(2,1)S(1)}, bf16[1,3,320,1280]{3,2,1,0:T(8,128)(2,1)}, u32[]{:S(2)}) copy-start(bf16[1,3,320,1280]{3,2,1,0:T(8,128)(2,1)} %param.16) | copy-start | bytes 7372804
  8.0 1.7 %copy-start.4 = (bf16[320,384]{1,0:T(8,128)(2,1)S(1)}, bf16[320,384]{1,0:T(8,128)(2,1)}, u32[]{:S(2)}) copy-start(bf16[320,384]{1,0:T(8,128)(2,1)} %entry_ref.3) | copy-start | bytes 737284
  8.8 65.7 %collective-permute-start.5 = (bf16[320,384]{1,0:T(8,128)(2,1)}, bf16[320,384]{1,0:T(8,128)(2,1)S(1)}, u32[]{:S(2)}, u32[]{:S(2)}) collective-permute-start(bf16[320,384]{1,0:T(8,128)(2,1)} %bitcast.5), channel_id=1, source_target_pairs={{508,4},{504,8},{500,12},{496,16},{492,20},{488,24},{484,28},{480,... | collective-permute-start | bytes 737288 | tf_op jit(solution)/shard_map/ppermute | solution.py:240
  11.6 7.8 %collective-permute-start.2 = (f32[2,320,384]{2,1,0:T(8,128)S(1)}, f32[2,320,384]{2,1,0:T(8,128)S(1)}, u32[]{:S(2)}, u32[]{:S(2)}) collective-permute-start(f32[2,320,384]{2,1,0:T(8,128)S(1)} %get-tuple-element.24), channel_id=1, source_target_pairs={{0,1},{1,0},{2,3},{3,2},{4,5},{5,4},{6,7},{7,6},{8,9},{9,8},{10,11... | collective-permute-start | bytes 2949128 | tf_op jit(solution)/shard_map/ppermute | solution.py:26
  16.6 12.0 %collective-permute-start.1 = (bf16[320,384]{1,0:T(8,128)(2,1)}, bf16[320,384]{1,0:T(8,128)(2,1)S(1)}, u32[]{:S(2)}, u32[]{:S(2)}) collective-permute-start(bf16[320,384]{1,0:T(8,128)(2,1)} %bitcast.5), channel_id=1, source_target_pairs={{4,0},{8,4},{12,8},{16,12},{20,16},{24,20},{28,24},{32,28},{36,32}... | collective-permute-start | bytes 737288 | tf_op jit(solution)/shard_map/ppermute | solution.py:22
  17.9 10.7 %copy-start = (bf16[1,2,320,384]{3,2,1,0:T(8,128)(2,1)S(1)}, bf16[1,2,320,384]{3,2,1,0:T(8,128)(2,1)}, u32[]{:S(2)}) copy-start(bf16[1,2,320,384]{3,2,1,0:T(8,128)(2,1)} %param.15) | copy-start | bytes 1474564
  17.9 10.7 %copy-start.3 = (bf16[320,384]{1,0:T(8,128)(2,1)S(1)}, bf16[320,384]{1,0:T(8,128)(2,1)}, u32[]{:S(2)}) copy-start(bf16[320,384]{1,0:T(8,128)(2,1)} %reward_ref.5) | copy-start | bytes 737284
  17.9 10.7 %copy-start.5 = (f32[25,320]{1,0:T(8,128)S(1)}, f32[25,320]{1,0:T(8,128)}, u32[]{:S(2)}) copy-start(f32[25,320]{1,0:T(8,128)} %gain_ref.3) | copy-start | bytes 96004
  17.9 10.7 %copy-start.6 = (s32[1,2]{1,0:T(1,128)S(1)}, s32[1,2]{1,0:T(1,128)}, u32[]{:S(2)}) copy-start(s32[1,2]{1,0:T(1,128)} %plan_ref.7) | copy-start | bytes 28
  18.0 10.7 %copy-start.7 = (s32[1,2]{1,0:T(1,128)S(1)}, s32[1,2]{1,0:T(1,128)}, u32[]{:S(2)}) copy-start(s32[1,2]{1,0:T(1,128)} %stamps_ref.3) | copy-start | bytes 28
  19.4 12.2 %copy-start.8 = (bf16[1,2,320,384]{3,2,1,0:T(8,128)(2,1)S(1)}, bf16[1,2,320,384]{3,2,1,0:T(8,128)(2,1)}, u32[]{:S(2)}) copy-start(bf16[1,2,320,384]{3,2,1,0:T(8,128)(2,1)} %param.14) | copy-start | bytes 1474564
  20.0 14.9 %collective-permute-start.4 = (bf16[320,384]{1,0:T(8,128)(2,1)S(1)}, bf16[320,384]{1,0:T(8,128)(2,1)S(1)}, u32[]{:S(2)}, u32[]{:S(2)}) collective-permute-start(bf16[320,384]{1,0:T(8,128)(2,1)S(1)} %get-tuple-element.27), channel_id=1, source_target_pairs={{0,2},{2,0},{1,3},{3,1},{4,6},{6,4},{5,7},{7,5},{8,10},{10,8},{9,1... | collective-permute-start | bytes 737288 | tf_op jit(solution)/shard_map/ppermute | solution.py:30
  29.4 33.3 %collective-permute-start.3 = (bf16[320,384]{1,0:T(8,128)(2,1)S(1)}, bf16[320,384]{1,0:T(8,128)(2,1)S(1)}, u32[]{:S(2)}, u32[]{:S(2)}) collective-permute-start(bf16[320,384]{1,0:T(8,128)(2,1)S(1)} %scaled_kernel.1.scaled_ref), channel_id=1, source_target_pairs={{0,2},{2,0},{1,3},{3,1},{4,6},{6,4},{5,7},{7,5},{8,10},{10,8},{9,1... | collective-permute-start | bytes 737288 | tf_op jit(solution)/shard_map/ppermute | solution.py:30
  32.4 38.9 %copy-start.2 = (bf16[1,3,320,1280]{3,2,1,0:T(8,128)(2,1)S(1)}, bf16[1,3,320,1280]{3,2,1,0:T(8,128)(2,1)}, u32[]{:S(2)}) copy-start(bf16[1,3,320,1280]{3,2,1,0:T(8,128)(2,1)} %param.16) | copy-start | bytes 7372804
  36.4 41.6 %collective-permute-start.6 = (bf16[320,384]{1,0:T(8,128)(2,1)}, bf16[320,384]{1,0:T(8,128)(2,1)S(1)}, u32[]{:S(2)}, u32[]{:S(2)}) collective-permute-start(bf16[320,384]{1,0:T(8,128)(2,1)} %output_kernel.1), channel_id=1, source_target_pairs={{0,508},{4,504},{8,500},{12,496},{16,492},{20,488},{24,484},{28,48... | collective-permute-start | bytes 737288 | tf_op jit(solution)/shard_map/ppermute | solution.py:284
  62.6 8.7 %collective-permute-start.7 = (bf16[320,384]{1,0:T(8,128)(2,1)S(1)}, bf16[320,384]{1,0:T(8,128)(2,1)S(1)}, u32[]{:S(2)}, u32[]{:S(2)}) collective-permute-start(bf16[320,384]{1,0:T(8,128)(2,1)S(1)} %scaled_kernel.1.scaled_ref), channel_id=1, source_target_pairs={{0,1},{1,0},{2,3},{3,2},{4,5},{5,4},{6,7},{7,6},{8,9},{9,8},{10,11... | collective-permute-start | bytes 737288 | tf_op jit(solution)/shard_map/ppermute | solution.py:26
  66.1 4.3 %collective-permute-start.8 = (bf16[160,384]{1,0:T(8,128)(2,1)S(1)}, bf16[160,384]{1,0:T(8,128)(2,1)S(1)}, u32[]{:S(2)}, u32[]{:S(2)}) collective-permute-start(bf16[160,384]{1,0:T(8,128)(2,1)S(1)} %get-tuple-element.42), channel_id=1, source_target_pairs={{0,1},{1,0},{2,3},{3,2},{4,5},{5,4},{6,7},{7,6},{8,9},{9,8},{10,11... | collective-permute-start | bytes 368648 | tf_op jit(solution)/shard_map/ppermute | solution.py:26
  68.0 3.4 %collective-permute-start.9 = (bf16[160,384]{1,0:T(8,128)(2,1)S(1)}, bf16[160,384]{1,0:T(8,128)(2,1)S(1)}, u32[]{:S(2)}, u32[]{:S(2)}) collective-permute-start(bf16[160,384]{1,0:T(8,128)(2,1)S(1)} %get-tuple-element.41), channel_id=1, source_target_pairs={{0,1},{1,0},{2,3},{3,2},{4,5},{5,4},{6,7},{7,6},{8,9},{9,8},{10,11... | collective-permute-start | bytes 368648 | tf_op jit(solution)/shard_map/ppermute | solution.py:26

commit v4 on v3

--- a/solution.py
+++ b/solution.py
@@ -96,19 +96,28 @@
     own_side(place_ref[1], weight_ref, stacked_ref, own_ref)
 
 
-def cotangent(place_ref, plan_ref, returned_ref, reward_ref, skip_ref):
-    last = place_ref[3] == 1
-    cot_in = jnp.where(last, reward_ref[...], returned_ref[...])
-    skip = skip_ref[plan_ref[0, 1]].astype(jnp.float32)
-    skip = jnp.where(place_ref[4] == 1, skip, 0.0)
-    return cot_in, cot_in.astype(jnp.float32) + skip
-
-
-def scaled_kernel(
-    place_ref, plan_ref, stamps_ref, returned_ref, reward_ref, skip_ref, gain_ref, scaled_ref
+def prepare_kernel(
+    place_ref, plan_ref, stamps_ref, skip_ref, gain_ref, columns_ref, added_ref, extra_ref
 ):
-    _, cot_total = cotangent(place_ref, plan_ref, returned_ref, reward_ref, skip_ref)
-    scaled_ref[...] = (cot_total * column(gain_ref, stamps_ref[0, 1])).astype(jnp.bfloat16)
+    for way in range(2):
+        columns_ref[way] = jnp.broadcast_to(
+            column(gain_ref, stamps_ref[0, way]), columns_ref.shape[1:]
+        )
+    encoder = place_ref[4] == 1
+    added = skip_ref[plan_ref[0, 0]]
+    extra = skip_ref[plan_ref[0, 1]]
+    added_ref[...] = jnp.where(encoder, jnp.zeros_like(added), added)
+    extra_ref[...] = jnp.where(encoder, extra, jnp.zeros_like(extra))
+
+
+def cotangent(place_ref, returned_ref, reward_ref, extra_ref):
+    cot_in = jnp.where(place_ref[3] == 1, reward_ref[...], returned_ref[...])
+    return cot_in.astype(jnp.float32) + extra_ref[...].astype(jnp.float32)
+
+
+def scaled_kernel(place_ref, returned_ref, reward_ref, extra_ref, columns_ref, scaled_ref):
+    cot_total = cotangent(place_ref, returned_ref, reward_ref, extra_ref)
+    scaled_ref[...] = (cot_total * columns_ref[1][:, :1]).astype(jnp.bfloat16)
 
 
 def halves_kernel(place_ref, own_ref, mate_ref, near_ref, far_ref):
@@ -118,27 +127,31 @@
 
 
 def output_kernel(
-    place_ref,
-    plan_ref,
-    stamps_ref,
-    near_ref,
-    far_ref,
-    arrived_ref,
-    entry_ref,
-    skip_ref,
-    gain_ref,
-    out_ref,
+    place_ref, near_ref, far_ref, arrived_ref, entry_ref, added_ref, columns_ref, out_ref
 ):
     x_in = jnp.where(place_ref[0] == 0, entry_ref[...], arrived_ref[...]).astype(jnp.float32)
-    skip = jnp.where(place_ref[4] == 1, 0.0, skip_ref[plan_ref[0, 0]].astype(jnp.float32))
     conv_sum = near_ref[...] + far_ref[...].astype(jnp.float32)
-    act_out = (x_in + conv_sum * column(gain_ref, stamps_ref[0, 0]) + skip).astype(jnp.bfloat16)
-    out_ref[...] = act_out
-
-
-def choose_kernel(place_ref, cot_ref, act_ref, reward_ref, out_ref):
-    cot = jnp.where(place_ref[0] == 0, reward_ref[...], cot_ref[...])
-    out_ref[...] = jnp.where(place_ref[4] == 1, cot, act_ref[...])
+    act_out = x_in + conv_sum * columns_ref[0][:, :1] + added_ref[...].astype(jnp.float32)
+    out_ref[...] = act_out.astype(jnp.bfloat16)
+
+
+def choose_kernel(place_ref, cot_ref, act_ref, reward_ref, out_ref, sem):
+    def put(chosen_ref):
+        copy = pltpu.make_async_copy(chosen_ref, out_ref, sem)
+        copy.start()
+        copy.wait()
+
+    @pl.when(place_ref[0] == 0)
+    def _():
+        put(reward_ref)
+
+    @pl.when((place_ref[4] == 1) & (place_ref[0] != 0))
+    def _():
+        put(cot_ref)
+
+    @pl.when(place_ref[4] == 0)
+    def _():
+        put(act_ref)
 
 
 def saved_kernel(plan_ref, stored_ref, normed_ref, factor_ref):
@@ -149,12 +162,11 @@
 
 def gradient_kernel(
     place_ref,
-    plan_ref,
     normed_ref,
     factor_ref,
     returned_ref,
     reward_ref,
-    skip_ref,
+    extra_ref,
     scaled_ref,
     other_ref,
     mate_ref,
@@ -176,7 +188,7 @@
     put(chip, 1 - core, mate_ref[...])
     put(1 - chip, 1 - core, mate_low_ref[...])
     put(1 - chip, 1 - core, mate_high_ref[...], rows // 2)
-    _, cot_total = cotangent(place_ref, plan_ref, returned_ref, reward_ref, skip_ref)
+    cot_total = cotangent(place_ref, returned_ref, reward_ref, extra_ref)
     normed = normed_ref[...]
     sigmoid = 1.0 / (1.0 + jnp.exp(-normed))
     slope = sigmoid * (1.0 + normed * (1.0 - sigmoid))
@@ -194,12 +206,12 @@
     out_ref[...] = (cot_total + result.reshape(cot_total.shape)).astype(jnp.bfloat16)
 
 
-def call(kernel, outs, specs, args, scratch=(), cost=0.0, limit=16):
+def call(kernel, outs, specs, args, scratch=(), cost=0.0, limit=16, where=VMEM):
     return pl.pallas_call(
         kernel,
         out_shape=[jax.ShapeDtypeStruct(shape, kind) for shape, kind in outs],
         in_specs=specs,
-        out_specs=[VMEM] * len(outs),
+        out_specs=[where] * len(outs),
         scratch_shapes=list(scratch),
         compiler_params=pltpu.CompilerParams(vmem_limit_bytes=limit * 2**20),
         cost_estimate=pl.CostEstimate(
@@ -236,7 +248,15 @@
 
     arrived = shifted(act_carried[0], "section", 1)
     (turned,) = call(transpose_kernel, [((full, 3 * rows), jnp.bfloat16)], [VMEM], [weight], cost=20.0)
-    cotangents, turned = lax.optimization_barrier((cot_carried[0], turned))
+    turned, skips, time_gain = lax.optimization_barrier((turned, skips, time_gain))
+    gains, added, extra = call(
+        prepare_kernel,
+        [((2, rows, 128), jnp.float32), field, field],
+        [SMEM] * 3 + [VMEM] * 2,
+        [place, plan, timesteps, skips, time_gain],
+        cost=20.0,
+    )
+    cotangents, gains, turned = lax.optimization_barrier((cot_carried[0], gains, turned))
     mirrored_cot = lax.ppermute(
         cotangents, "section", [(sections - s, s) for s in range(1, sections // 2)]
     )
@@ -262,8 +282,8 @@
     (scaled,) = call(
         scaled_kernel,
         [field],
-        [SMEM] * 3 + [VMEM] * 4,
-        [place, plan, timesteps, returned, reward_head, skips, time_gain],
+        [SMEM] + [VMEM] * 4,
+        [place, returned, reward_head, extra, gains],
     )
     other = swap_chip(scaled)
     stored, far_side = lax.optimization_barrier((stored, far_side))
@@ -278,8 +298,8 @@
     (act_out,) = call(
         output_kernel,
         [field],
-        [SMEM] * 3 + [VMEM] * 6,
-        [place, plan, timesteps, near, far, arrived, entry_latent, skips, time_gain],
+        [SMEM] + [VMEM] * 6,
+        [place, near, far, arrived, entry_latent, added, gains],
     )
     mirrored_act = lax.ppermute(
         act_out, "section", [(s, sections - 1 - s) for s in range(sections // 2)]
@@ -291,8 +311,19 @@
     (cot_out,) = call(
         gradient_kernel,
         [field],
-        [SMEM] * 2 + [VMEM] * 11,
-        [place, plan, saved_normed, saved_factor, returned, reward_head, skips, scaled, other, *mates, weight],
+        [SMEM] + [VMEM] * 11,
+        [
+            place,
+            saved_normed,
+            saved_factor,
+            returned,
+            reward_head,
+            extra,
+            scaled,
+            other,
+            *mates,
+            weight,
+        ],
         scratch=[pltpu.VMEM((full, cells), jnp.bfloat16)],
     )
     mirrored_cot, mirrored_act, cot_out = lax.optimization_barrier(
@@ -303,6 +334,8 @@
         [field],
         [SMEM] + [VMEM] * 3,
         [place, mirrored_cot, mirrored_act, reward_head],
+        scratch=[pltpu.SemaphoreType.DMA],
+        where=pl.BlockSpec(memory_space=pl.ANY),
     )
     return (act_out[None], cot_out[None], mirror_in[None])
 

time: 79.8 us -> 80.6 us (1.010)
  the two profiles are of different devices: /device:TPU:1 before, /device:TPU:7 now
where the time goes in v4:
time: 80.6 us; the launch traced here: 80.2 us
  waiting for transfers between devices  35.1 us (44%)
  starting transfers between devices  29.3 us (36%)
  Pallas kernels  12.7 us (16%)
  local copies, waits for them, and re-layouts  2.13 us (3%)
  between operations  0.89 us (1%)
    ppermute x2, waiting for transfers between devices, shifted(): return lax.ppermute(block, axis, route)  16.1 us
    ppermute x1, waiting for transfers between devices, local(): lax.ppermute(act_out, 'section', [(s, sections - 1 - s) for s in range(se...  15 us
    pallas_call x10, Pallas kernels, call(): pl.pallas_call(kernel, out_shape=[jax.ShapeDtypeStruct(shape, kind) for s...  12.7 us
    ppermute x4, starting transfers between devices, swap_core(): return lax.ppermute(block, 'ch', [(0, 1), (1, 0), (2, 3), (3, 2)])  11.1 us
    ppermute x2, starting transfers between devices, shifted(): return lax.ppermute(block, axis, route)  9.27 us
    ppermute x2, starting transfers between devices, swap_chip(): return lax.ppermute(block, 'ch', [(0, 2), (2, 0), (1, 3), (3, 1)])  4.61 us
    ppermute x2, waiting for transfers between devices, swap_chip(): return lax.ppermute(block, 'ch', [(0, 2), (2, 0), (1, 3), (3, 1)])  3.1 us
    ppermute x1, starting transfers between devices, local(): lax.ppermute(cotangents, 'section', [(sections - s, s) for s in range(1,...  3.03 us
  transfers between devices with their start and end apart: 10, of which 6 were waited for; matrix products, arithmetic and copies ran while one was open for 0% of the time, Pallas kernels for 14%

profile of v4, /device:TPU:7, one launch (start us, length us, event | category | flops | bytes accessed | tf_op | source)
XLA Modules:
  0.0 80.2 jit_solution(16173670291927457578)
XLA Ops:
  0.6 4.8 %collective-permute-start = (bf16[320,384]{1,0:T(8,128)(2,1)}, bf16[320,384]{1,0:T(8,128)(2,1)S(1)}, u32[]{:S(2)}, u32[]{:S(2)}) collective-permute-start(bf16[320,384]{1,0:T(8,128)(2,1)} %bitcast.20), channel_id=1, source_target_pairs={{0,4},{4,8},{8,12},{12,16},{16,20},{20,24},{24,28},{28,32},{32,36}... | collective-permute-start | bytes 737288 | tf_op jit(solution)/shard_map/ppermute | solution.py:22
  5.5 1.7 %copy-done = bf16[1,3,320,1280]{3,2,1,0:T(8,128)(2,1)S(1)} copy-done((bf16[1,3,320,1280]{3,2,1,0:T(8,128)(2,1)S(1)}, bf16[1,3,320,1280]{3,2,1,0:T(8,128)(2,1)}, u32[]{:S(2)}) %copy-start) | copy-done | bytes 2457624
  7.2 0.8 %transpose_kernel.1.weight_ref = bf16[1280,960]{1,0:T(8,128)(2,1)S(1)} custom-call(bf16[960,1280]{1,0:T(8,128)(2,1)S(1)} %bitcast.13), custom_call_target="tpu_custom_call" | custom-call | flops 20000000000 | bytes 20000000 | tf_op jit(solution)/shard_map/transpose_kernel/pallas_call | solution.py:210
  9.2 3.0 %collective-permute-start.5 = (bf16[320,384]{1,0:T(8,128)(2,1)S(1)}, bf16[320,384]{1,0:T(8,128)(2,1)S(1)}, u32[]{:S(2)}, u32[]{:S(2)}) collective-permute-start(bf16[320,384]{1,0:T(8,128)(2,1)S(1)} %bitcast.21), channel_id=1, source_target_pairs={{508,4},{504,8},{500,12},{496,16},{492,20},{488,24},{484,28},{480,... | collective-permute-start | bytes 737288 | tf_op jit(solution)/shard_map/ppermute | solution.py:260
  12.2 8.3 %collective-permute-done.arrived_ref = bf16[320,384]{1,0:T(8,128)(2,1)S(1)} collective-permute-done((bf16[320,384]{1,0:T(8,128)(2,1)}, bf16[320,384]{1,0:T(8,128)(2,1)S(1)}, u32[]{:S(2)}, u32[]{:S(2)}) %collective-permute-start) | collective-permute-done | bytes 245792 | tf_op jit(solution)/shard_map/ppermute | solution.py:22
  20.5 1.9 %forward_kernel.1 = (f32[2,320,384]{2,1,0:T(8,128)S(1)}, bf16[960,384]{1,0:T(8,128)(2,1)S(1)}) custom-call(s32[5]{0:T(128)S(1)} %stack.31.place_ref, bf16[320,384]{1,0:T(8,128)(2,1)S(1)} %collective-permute-done.arrived_ref, bf16[320,384]{1,0:T(8,128)(2,1)S(1)} %copy-done.3, bf16[1280,960]{1,0:T(8,128)(2,1)S(1)} %transpose_kernel.1.weight_ref), custom_call_target="tpu_custom_call" | custom-call | tf_op jit(solution)/shard_map/forward_kernel/pallas_call | solution.py:210
  22.4 3.6 %collective-permute-start.2 = (f32[2,320,384]{2,1,0:T(8,128)S(1)}, f32[2,320,384]{2,1,0:T(8,128)S(1)}, u32[]{:S(2)}, u32[]{:S(2)}) collective-permute-start(f32[2,320,384]{2,1,0:T(8,128)S(1)} %get-tuple-element.35), channel_id=1, source_target_pairs={{0,1},{1,0},{2,3},{3,2},{4,5},{5,4},{6,7},{7,6},{8,9},{9,8},{10,11... | collective-permute-start | bytes 2949128 | tf_op jit(solution)/shard_map/ppermute | solution.py:26
  26.0 4.4 %collective-permute-start.1 = (bf16[320,384]{1,0:T(8,128)(2,1)S(1)}, bf16[320,384]{1,0:T(8,128)(2,1)S(1)}, u32[]{:S(2)}, u32[]{:S(2)}) collective-permute-start(bf16[320,384]{1,0:T(8,128)(2,1)S(1)} %bitcast.22), channel_id=1, source_target_pairs={{4,0},{8,4},{12,8},{16,12},{20,16},{24,20},{28,24},{32,28},{36,32}... | collective-permute-start | bytes 737288 | tf_op jit(solution)/shard_map/ppermute | solution.py:22
  30.4 1.4 %own_kernel.1.own_ref = f32[2,320,384]{2,1,0:T(8,128)S(1)} custom-call(s32[5]{0:T(128)S(1)} %stack.31.place_ref, bf16[1280,960]{1,0:T(8,128)(2,1)S(1)} %transpose_kernel.1.weight_ref, bf16[960,384]{1,0:T(8,128)(2,1)S(1)} %get-tuple-element.37.stacked_ref), custom_call_target="tpu_custom_call" | custom-call | flops 20000000000 | bytes 20000000 | tf_op jit(solution)/shard_map/own_kernel/pallas_call | solution.py:210
  32.5 2.3 %collective-permute-start.4 = (bf16[320,384]{1,0:T(8,128)(2,1)S(1)}, bf16[320,384]{1,0:T(8,128)(2,1)S(1)}, u32[]{:S(2)}, u32[]{:S(2)}) collective-permute-start(bf16[320,384]{1,0:T(8,128)(2,1)S(1)} %get-tuple-element.38), channel_id=1, source_target_pairs={{0,2},{2,0},{1,3},{3,1},{4,6},{6,4},{5,7},{7,5},{8,10},{10,8},{9,1... | collective-permute-start | bytes 737288 | tf_op jit(solution)/shard_map/ppermute | solution.py:30
  34.8 7.8 %collective-permute-done.1.returned_ref = bf16[320,384]{1,0:T(8,128)(2,1)S(1)} collective-permute-done((bf16[320,384]{1,0:T(8,128)(2,1)S(1)}, bf16[320,384]{1,0:T(8,128)(2,1)S(1)}, u32[]{:S(2)}, u32[]{:S(2)}) %collective-permute-start.1) | collective-permute-done | bytes 245792 | tf_op jit(solution)/shard_map/ppermute | solution.py:22
  43.3 2.3 %collective-permute-start.3 = (bf16[320,384]{1,0:T(8,128)(2,1)S(1)}, bf16[320,384]{1,0:T(8,128)(2,1)S(1)}, u32[]{:S(2)}, u32[]{:S(2)}) collective-permute-start(bf16[320,384]{1,0:T(8,128)(2,1)S(1)} %scaled_kernel.1.scaled_ref), channel_id=1, source_target_pairs={{0,2},{2,0},{1,3},{3,1},{4,6},{6,4},{5,7},{7,5},{8,10},{10,8},{9,1... | collective-permute-start | bytes 737288 | tf_op jit(solution)/shard_map/ppermute | solution.py:30
  45.6 0.8 %saved_kernel.1 = (f32[320,384]{1,0:T(8,128)S(1)}, f32[8,8,128]{2,1,0:T(8,128)S(1)}) custom-call(s32[1,2]{1,0:T(1,128)S(1)} %copy-done.8, bf16[2,320,384]{2,1,0:T(8,128)(2,1)S(1)} %bitcast.16), custom_call_target="tpu_custom_call" | custom-call | flops 20000000000 | bytes 20000000 | tf_op jit(solution)/shard_map/saved_kernel/pallas_call | solution.py:210
  46.4 0.9 %collective-permute-done.4.far_ref = bf16[320,384]{1,0:T(8,128)(2,1)S(1)} collective-permute-done((bf16[320,384]{1,0:T(8,128)(2,1)S(1)}, bf16[320,384]{1,0:T(8,128)(2,1)S(1)}, u32[]{:S(2)}, u32[]{:S(2)}) %collective-permute-start.4) | collective-permute-done | bytes 245792 | tf_op jit(solution)/shard_map/ppermute | solution.py:30
  47.3 1.4 %output_kernel.1 = bf16[320,384]{1,0:T(8,128)(2,1)} custom-call(s32[5]{0:T(128)S(1)} %stack.31.place_ref, f32[320,384]{1,0:T(8,128)S(1)} %get-tuple-element.44.near_ref, bf16[320,384]{1,0:T(8,128)(2,1)S(1)} %collective-permute-done.4.far_ref, bf16[320,384]{1,0:T(8,128)(2,1)S(1)} %collective-permute-done.arrived_ref, bf16[320,384]{1,0:T(8,128)(2,1)S(1)} %copy-done.3, ...), custom_call_target="tpu_custom_call" | custom-call | tf_op jit(solution)/shard_map/output_kernel/pallas_call | solution.py:210
  48.7 1.3 %collective-permute-start.6 = (bf16[320,384]{1,0:T(8,128)(2,1)}, bf16[320,384]{1,0:T(8,128)(2,1)S(1)}, u32[]{:S(2)}, u32[]{:S(2)}) collective-permute-start(bf16[320,384]{1,0:T(8,128)(2,1)} %output_kernel.1), channel_id=1, source_target_pairs={{0,508},{4,504},{8,500},{12,496},{16,492},{20,488},{24,484},{28,48... | collective-permute-start | bytes 737288 | tf_op jit(solution)/shard_map/ppermute | solution.py:304
  50.0 2.2 %collective-permute-done.3.other_ref = bf16[320,384]{1,0:T(8,128)(2,1)S(1)} collective-permute-done((bf16[320,384]{1,0:T(8,128)(2,1)S(1)}, bf16[320,384]{1,0:T(8,128)(2,1)S(1)}, u32[]{:S(2)}, u32[]{:S(2)}) %collective-permute-start.3) | collective-permute-done | bytes 245792 | tf_op jit(solution)/shard_map/ppermute | solution.py:30
  52.2 3.2 %collective-permute-start.7 = (bf16[320,384]{1,0:T(8,128)(2,1)S(1)}, bf16[320,384]{1,0:T(8,128)(2,1)S(1)}, u32[]{:S(2)}, u32[]{:S(2)}) collective-permute-start(bf16[320,384]{1,0:T(8,128)(2,1)S(1)} %scaled_kernel.1.scaled_ref), channel_id=1, source_target_pairs={{0,1},{1,0},{2,3},{3,2},{4,5},{5,4},{6,7},{7,6},{8,9},{9,8},{10,11... | collective-permute-start | bytes 737288 | tf_op jit(solution)/shard_map/ppermute | solution.py:26
  55.5 1.9 %collective-permute-start.8 = (bf16[160,384]{1,0:T(8,128)(2,1)S(1)}, bf16[160,384]{1,0:T(8,128)(2,1)S(1)}, u32[]{:S(2)}, u32[]{:S(2)}) collective-permute-start(bf16[160,384]{1,0:T(8,128)(2,1)S(1)} %get-tuple-element.56), channel_id=1, source_target_pairs={{0,1},{1,0},{2,3},{3,2},{4,5},{5,4},{6,7},{7,6},{8,9},{9,8},{10,11... | collective-permute-start | bytes 368648 | tf_op jit(solution)/shard_map/ppermute | solution.py:26
  57.4 2.4 %collective-permute-start.9 = (bf16[160,384]{1,0:T(8,128)(2,1)S(1)}, bf16[160,384]{1,0:T(8,128)(2,1)S(1)}, u32[]{:S(2)}, u32[]{:S(2)}) collective-permute-start(bf16[160,384]{1,0:T(8,128)(2,1)S(1)} %get-tuple-element.55), channel_id=1, source_target_pairs={{0,1},{1,0},{2,3},{3,2},{4,5},{5,4},{6,7},{7,6},{8,9},{9,8},{10,11... | collective-permute-start | bytes 368648 | tf_op jit(solution)/shard_map/ppermute | solution.py:26
  59.8 0.9 %collective-permute-done.9.mate_high_ref = bf16[160,384]{1,0:T(8,128)(2,1)S(1)} collective-permute-done((bf16[160,384]{1,0:T(8,128)(2,1)S(1)}, bf16[160,384]{1,0:T(8,128)(2,1)S(1)}, u32[]{:S(2)}, u32[]{:S(2)}) %collective-permute-start.9) | collective-permute-done | bytes 122912 | tf_op jit(solution)/shard_map/ppermute | solution.py:26
  60.8 3.2 %gradient_kernel.1 = bf16[320,384]{1,0:T(8,128)(2,1)} custom-call(s32[5]{0:T(128)S(1)} %stack.31.place_ref, f32[320,384]{1,0:T(8,128)S(1)} %get-tuple-element.48.normed_ref, f32[8,8,128]{2,1,0:T(8,128)S(1)} %get-tuple-element.49.factor_ref, bf16[320,384]{1,0:T(8,128)(2,1)S(1)} %collective-permute-done.1.returned_ref, bf16[320,384]{1,0:T(8,128)(2,1)S(1)} %copy-done.2, ...), custom_call_target="tpu_custom_call" | custom-call | tf_op jit(solution)/shard_map/gradient_kernel/pallas_call | solution.py:210
  63.9 15.0 %collective-permute-done.6.act_ref = bf16[320,384]{1,0:T(8,128)(2,1)S(1)} collective-permute-done((bf16[320,384]{1,0:T(8,128)(2,1)}, bf16[320,384]{1,0:T(8,128)(2,1)S(1)}, u32[]{:S(2)}, u32[]{:S(2)}) %collective-permute-start.6) | collective-permute-done | bytes 245792 | tf_op jit(solution)/shard_map/ppermute | solution.py:304
  78.9 1.3 %choose_kernel.1 = bf16[320,384]{1,0:T(8,128)(2,1)} custom-call(s32[5]{0:T(128)S(1)} %stack.31.place_ref, bf16[320,384]{1,0:T(8,128)(2,1)S(1)} %collective-permute-done.5.cot_ref, bf16[320,384]{1,0:T(8,128)(2,1)S(1)} %collective-permute-done.6.act_ref, bf16[320,384]{1,0:T(8,128)(2,1)S(1)} %copy-done.2), custom_call_target="tpu_custom_call" | custom-call | tf_op jit(solution)/shard_map/choose_kernel/pallas_call | solution.py:210
  (28 shorter events, 2.5 us)
Async XLA Ops:
  0.6 19.9 %collective-permute-start = (bf16[320,384]{1,0:T(8,128)(2,1)}, bf16[320,384]{1,0:T(8,128)(2,1)S(1)}, u32[]{:S(2)}, u32[]{:S(2)}) collective-permute-start(bf16[320,384]{1,0:T(8,128)(2,1)} %bitcast.20), channel_id=1, source_target_pairs={{0,4},{4,8},{8,12},{12,16},{16,20},{20,24},{24,28},{28,32},{32,36}... | collective-permute-start | bytes 737288 | tf_op jit(solution)/shard_map/ppermute | solution.py:22
  5.5 1.7 %copy-start = (bf16[1,3,320,1280]{3,2,1,0:T(8,128)(2,1)S(1)}, bf16[1,3,320,1280]{3,2,1,0:T(8,128)(2,1)}, u32[]{:S(2)}) copy-start(bf16[1,3,320,1280]{3,2,1,0:T(8,128)(2,1)} %param.16) | copy-start | bytes 7372804
  7.2 1.0 %copy-start.4 = (bf16[1,2,320,384]{3,2,1,0:T(8,128)(2,1)S(1)}, bf16[1,2,320,384]{3,2,1,0:T(8,128)(2,1)}, u32[]{:S(2)}) copy-start(bf16[1,2,320,384]{3,2,1,0:T(8,128)(2,1)} %param.15) | copy-start | bytes 1474564
  7.2 1.0 %copy-start.6 = (f32[25,320]{1,0:T(8,128)S(1)}, f32[25,320]{1,0:T(8,128)}, u32[]{:S(2)}) copy-start(f32[25,320]{1,0:T(8,128)} %gain_ref) | copy-start | bytes 96004
  7.2 1.0 %copy-start.7 = (s32[1,2]{1,0:T(1,128)S(1)}, s32[1,2]{1,0:T(1,128)}, u32[]{:S(2)}) copy-start(s32[1,2]{1,0:T(1,128)} %stamps_ref.1) | copy-start | bytes 28
  7.2 1.0 %copy-start.8 = (s32[1,2]{1,0:T(1,128)S(1)}, s32[1,2]{1,0:T(1,128)}, u32[]{:S(2)}) copy-start(s32[1,2]{1,0:T(1,128)} %plan_ref.3) | copy-start | bytes 28
  8.2 0.9 %copy-start.9 = (bf16[1,320,384]{2,1,0:T(8,128)(2,1)S(1)}, bf16[1,320,384]{2,1,0:T(8,128)(2,1)}, u32[]{:S(2)}) copy-start(bf16[1,320,384]{2,1,0:T(8,128)(2,1)} %param.11) | copy-start | bytes 737284
  8.2 12.3 %copy-start.3 = (bf16[320,384]{1,0:T(8,128)(2,1)S(1)}, bf16[320,384]{1,0:T(8,128)(2,1)}, u32[]{:S(2)}) copy-start(bf16[320,384]{1,0:T(8,128)(2,1)} %entry_ref.3) | copy-start | bytes 737284
  9.2 54.8 %collective-permute-start.5 = (bf16[320,384]{1,0:T(8,128)(2,1)S(1)}, bf16[320,384]{1,0:T(8,128)(2,1)S(1)}, u32[]{:S(2)}, u32[]{:S(2)}) collective-permute-start(bf16[320,384]{1,0:T(8,128)(2,1)S(1)} %bitcast.21), channel_id=1, source_target_pairs={{508,4},{504,8},{500,12},{496,16},{492,20},{488,24},{484,28},{480,... | collective-permute-start | bytes 737288 | tf_op jit(solution)/shard_map/ppermute | solution.py:260
  22.4 9.4 %collective-permute-start.2 = (f32[2,320,384]{2,1,0:T(8,128)S(1)}, f32[2,320,384]{2,1,0:T(8,128)S(1)}, u32[]{:S(2)}, u32[]{:S(2)}) collective-permute-start(f32[2,320,384]{2,1,0:T(8,128)S(1)} %get-tuple-element.35), channel_id=1, source_target_pairs={{0,1},{1,0},{2,3},{3,2},{4,5},{5,4},{6,7},{7,6},{8,9},{9,8},{10,11... | collective-permute-start | bytes 2949128 | tf_op jit(solution)/shard_map/ppermute | solution.py:26
  26.0 16.6 %collective-permute-start.1 = (bf16[320,384]{1,0:T(8,128)(2,1)S(1)}, bf16[320,384]{1,0:T(8,128)(2,1)S(1)}, u32[]{:S(2)}, u32[]{:S(2)}) collective-permute-start(bf16[320,384]{1,0:T(8,128)(2,1)S(1)} %bitcast.22), channel_id=1, source_target_pairs={{4,0},{8,4},{12,8},{16,12},{20,16},{24,20},{28,24},{32,28},{36,32}... | collective-permute-start | bytes 737288 | tf_op jit(solution)/shard_map/ppermute | solution.py:22
  30.4 12.2 %copy-start.2 = (bf16[320,384]{1,0:T(8,128)(2,1)S(1)}, bf16[320,384]{1,0:T(8,128)(2,1)}, u32[]{:S(2)}) copy-start(bf16[320,384]{1,0:T(8,128)(2,1)} %reward_ref.5) | copy-start | bytes 737284
  31.8 13.8 %copy-start.5 = (bf16[1,2,320,384]{3,2,1,0:T(8,128)(2,1)S(1)}, bf16[1,2,320,384]{3,2,1,0:T(8,128)(2,1)}, u32[]{:S(2)}) copy-start(bf16[1,2,320,384]{3,2,1,0:T(8,128)(2,1)} %param.14) | copy-start | bytes 1474564
  32.5 14.8 %collective-permute-start.4 = (bf16[320,384]{1,0:T(8,128)(2,1)S(1)}, bf16[320,384]{1,0:T(8,128)(2,1)S(1)}, u32[]{:S(2)}, u32[]{:S(2)}) collective-permute-start(bf16[320,384]{1,0:T(8,128)(2,1)S(1)} %get-tuple-element.38), channel_id=1, source_target_pairs={{0,2},{2,0},{1,3},{3,1},{4,6},{6,4},{5,7},{7,5},{8,10},{10,8},{9,1... | collective-permute-start | bytes 737288 | tf_op jit(solution)/shard_map/ppermute | solution.py:30
  43.3 9.0 %collective-permute-start.3 = (bf16[320,384]{1,0:T(8,128)(2,1)S(1)}, bf16[320,384]{1,0:T(8,128)(2,1)S(1)}, u32[]{:S(2)}, u32[]{:S(2)}) collective-permute-start(bf16[320,384]{1,0:T(8,128)(2,1)S(1)} %scaled_kernel.1.scaled_ref), channel_id=1, source_target_pairs={{0,2},{2,0},{1,3},{3,1},{4,6},{6,4},{5,7},{7,5},{8,10},{10,8},{9,1... | collective-permute-start | bytes 737288 | tf_op jit(solution)/shard_map/ppermute | solution.py:30
  46.4 14.4 %copy-start.1 = (bf16[1,3,320,1280]{3,2,1,0:T(8,128)(2,1)S(1)}, bf16[1,3,320,1280]{3,2,1,0:T(8,128)(2,1)}, u32[]{:S(2)}) copy-start(bf16[1,3,320,1280]{3,2,1,0:T(8,128)(2,1)} %param.16) | copy-start | bytes 7372804
  48.7 30.2 %collective-permute-start.6 = (bf16[320,384]{1,0:T(8,128)(2,1)}, bf16[320,384]{1,0:T(8,128)(2,1)S(1)}, u32[]{:S(2)}, u32[]{:S(2)}) collective-permute-start(bf16[320,384]{1,0:T(8,128)(2,1)} %output_kernel.1), channel_id=1, source_target_pairs={{0,508},{4,504},{8,500},{12,496},{16,492},{20,488},{24,484},{28,48... | collective-permute-start | bytes 737288 | tf_op jit(solution)/shard_map/ppermute | solution.py:304
  52.2 8.6 %collective-permute-start.7 = (bf16[320,384]{1,0:T(8,128)(2,1)S(1)}, bf16[320,384]{1,0:T(8,128)(2,1)S(1)}, u32[]{:S(2)}, u32[]{:S(2)}) collective-permute-start(bf16[320,384]{1,0:T(8,128)(2,1)S(1)} %scaled_kernel.1.scaled_ref), channel_id=1, source_target_pairs={{0,1},{1,0},{2,3},{3,2},{4,5},{5,4},{6,7},{7,6},{8,9},{9,8},{10,11... | collective-permute-start | bytes 737288 | tf_op jit(solution)/shard_map/ppermute | solution.py:26
  55.5 4.3 %collective-permute-start.8 = (bf16[160,384]{1,0:T(8,128)(2,1)S(1)}, bf16[160,384]{1,0:T(8,128)(2,1)S(1)}, u32[]{:S(2)}, u32[]{:S(2)}) collective-permute-start(bf16[160,384]{1,0:T(8,128)(2,1)S(1)} %get-tuple-element.56), channel_id=1, source_target_pairs={{0,1},{1,0},{2,3},{3,2},{4,5},{5,4},{6,7},{7,6},{8,9},{9,8},{10,11... | collective-permute-start | bytes 368648 | tf_op jit(solution)/shard_map/ppermute | solution.py:26
  57.4 3.4 %collective-permute-start.9 = (bf16[160,384]{1,0:T(8,128)(2,1)S(1)}, bf16[160,384]{1,0:T(8,128)(2,1)S(1)}, u32[]{:S(2)}, u32[]{:S(2)}) collective-permute-start(bf16[160,384]{1,0:T(8,128)(2,1)S(1)} %get-tuple-element.55), channel_id=1, source_target_pairs={{0,1},{1,0},{2,3},{3,2},{4,5},{5,4},{6,7},{7,6},{8,9},{9,8},{10,11... | collective-permute-start | bytes 368648 | tf_op jit(solution)/shard_map/ppermute | solution.py:26

commit v5 on v4

--- a/solution.py
+++ b/solution.py
@@ -127,37 +127,38 @@
 
 
 def output_kernel(
-    place_ref, near_ref, far_ref, arrived_ref, entry_ref, added_ref, columns_ref, out_ref
+    place_ref,
+    near_ref,
+    far_ref,
+    arrived_ref,
+    entry_ref,
+    added_ref,
+    columns_ref,
+    returned_ref,
+    reward_ref,
+    out_ref,
+    sent_ref,
 ):
     x_in = jnp.where(place_ref[0] == 0, entry_ref[...], arrived_ref[...]).astype(jnp.float32)
     conv_sum = near_ref[...] + far_ref[...].astype(jnp.float32)
     act_out = x_in + conv_sum * columns_ref[0][:, :1] + added_ref[...].astype(jnp.float32)
-    out_ref[...] = act_out.astype(jnp.bfloat16)
-
-
-def choose_kernel(place_ref, cot_ref, act_ref, reward_ref, out_ref, sem):
-    def put(chosen_ref):
-        copy = pltpu.make_async_copy(chosen_ref, out_ref, sem)
-        copy.start()
-        copy.wait()
-
-    @pl.when(place_ref[0] == 0)
-    def _():
-        put(reward_ref)
-
-    @pl.when((place_ref[4] == 1) & (place_ref[0] != 0))
-    def _():
-        put(cot_ref)
-
-    @pl.when(place_ref[4] == 0)
-    def _():
-        put(act_ref)
+    act_out = act_out.astype(jnp.bfloat16)
+    out_ref[...] = act_out
+    cot_in = jnp.where(place_ref[3] == 1, reward_ref[...], returned_ref[...])
+    sent_ref[...] = jnp.where(place_ref[4] == 1, act_out, cot_in)
 
 
 def saved_kernel(plan_ref, stored_ref, normed_ref, factor_ref):
     normed, factor = normalize(stored_ref[plan_ref[0, 1]].astype(jnp.float32))
     normed_ref[...] = normed
     factor_ref[...] = jnp.broadcast_to(factor, factor_ref.shape)
+
+
+def split_kernel(scaled_ref, other_ref, *part_refs):
+    half = part_refs[0].shape[0]
+    for i, part_ref in enumerate(part_refs):
+        source_ref = (scaled_ref, other_ref)[i // 2]
+        part_ref[...] = source_ref[i % 2 * half : (i % 2 + 1) * half, :]
 
 
 def gradient_kernel(
@@ -169,9 +170,10 @@
     extra_ref,
     scaled_ref,
     other_ref,
-    mate_ref,
     mate_low_ref,
     mate_high_ref,
+    other_low_ref,
+    other_high_ref,
     weight_ref,
     out_ref,
     whole_ref,
@@ -185,9 +187,10 @@
 
     put(chip, core, scaled_ref[...])
     put(1 - chip, core, other_ref[...])
-    put(chip, 1 - core, mate_ref[...])
-    put(1 - chip, 1 - core, mate_low_ref[...])
-    put(1 - chip, 1 - core, mate_high_ref[...], rows // 2)
+    put(chip, 1 - core, mate_low_ref[...])
+    put(chip, 1 - core, mate_high_ref[...], rows // 2)
+    put(1 - chip, 1 - core, other_low_ref[...])
+    put(1 - chip, 1 - core, other_high_ref[...], rows // 2)
     cot_total = cotangent(place_ref, returned_ref, reward_ref, extra_ref)
     normed = normed_ref[...]
     sigmoid = 1.0 / (1.0 + jnp.exp(-normed))
@@ -206,12 +209,12 @@
     out_ref[...] = (cot_total + result.reshape(cot_total.shape)).astype(jnp.bfloat16)
 
 
-def call(kernel, outs, specs, args, scratch=(), cost=0.0, limit=16, where=VMEM):
+def call(kernel, outs, specs, args, scratch=(), cost=0.0, limit=16):
     return pl.pallas_call(
         kernel,
         out_shape=[jax.ShapeDtypeStruct(shape, kind) for shape, kind in outs],
         in_specs=specs,
-        out_specs=[where] * len(outs),
+        out_specs=[VMEM] * len(outs),
         scratch_shapes=list(scratch),
         compiler_params=pltpu.CompilerParams(vmem_limit_bytes=limit * 2**20),
         cost_estimate=pl.CostEstimate(
@@ -256,10 +259,7 @@
         [place, plan, timesteps, skips, time_gain],
         cost=20.0,
     )
-    cotangents, gains, turned = lax.optimization_barrier((cot_carried[0], gains, turned))
-    mirrored_cot = lax.ppermute(
-        cotangents, "section", [(sections - s, s) for s in range(1, sections // 2)]
-    )
+    gains, turned = lax.optimization_barrier((gains, turned))
 
     mate_side, stacked = call(
         forward_kernel,
@@ -268,7 +268,7 @@
         [place, arrived, entry_latent, turned],
     )
     mate_part = swap_core(mate_side)
-    cotangents, mate_side = lax.optimization_barrier((cotangents, mate_side))
+    cotangents, mate_side = lax.optimization_barrier((cot_carried[0], mate_side))
     returned = shifted(cotangents, "section", -1)
     (own,) = call(own_kernel, [pair], [SMEM, VMEM, VMEM], [place, turned, stacked], cost=20.0)
     near, far_side = call(
@@ -295,23 +295,26 @@
         cost=20.0,
     )
     far, scaled, saved_normed = lax.optimization_barrier((far, scaled, saved_normed))
-    (act_out,) = call(
+    act_out, sent = call(
         output_kernel,
-        [field],
-        [SMEM] + [VMEM] * 6,
-        [place, near, far, arrived, entry_latent, added, gains],
-    )
-    mirrored_act = lax.ppermute(
-        act_out, "section", [(s, sections - 1 - s) for s in range(sections // 2)]
-    )
+        [field, field],
+        [SMEM] + [VMEM] * 8,
+        [place, near, far, arrived, entry_latent, added, gains, returned, reward_head],
+    )
+    mirror_in = lax.ppermute(sent, "section", [(s, sections - 1 - s) for s in range(sections)])
 
     other, scaled, act_out = lax.optimization_barrier((other, scaled, act_out))
-    half = rows // 2
-    mates = [swap_core(part) for part in (scaled, other[:half], other[half:])]
+    parts = call(
+        split_kernel,
+        [((rows // 2, cells), jnp.bfloat16)] * 4,
+        [VMEM] * 2,
+        [scaled, other],
+    )
+    mates = [swap_core(part) for part in parts]
     (cot_out,) = call(
         gradient_kernel,
         [field],
-        [SMEM] + [VMEM] * 11,
+        [SMEM] + [VMEM] * 12,
         [
             place,
             saved_normed,
@@ -326,17 +329,7 @@
         ],
         scratch=[pltpu.VMEM((full, cells), jnp.bfloat16)],
     )
-    mirrored_cot, mirrored_act, cot_out = lax.optimization_barrier(
-        (mirrored_cot, mirrored_act, cot_out)
-    )
-    (mirror_in,) = call(
-        choose_kernel,
-        [field],
-        [SMEM] + [VMEM] * 3,
-        [place, mirrored_cot, mirrored_act, reward_head],
-        scratch=[pltpu.SemaphoreType.DMA],
-        where=pl.BlockSpec(memory_space=pl.ANY),
-    )
+    mirror_in, cot_out = lax.optimization_barrier((mirror_in, cot_out))
     return (act_out[None], cot_out[None], mirror_in[None])
 
 

time: 80.6 us -> 73.4 us (0.911)
  the two profiles are of different devices: /device:TPU:7 before, /device:TPU:1 now
where the time goes in v5:
time: 73.4 us; the launch traced here: 73 us
  starting transfers between devices  40 us (54%)
  waiting for transfers between devices  17.7 us (24%)
  Pallas kernels  11.6 us (16%)
  local copies, waits for them, and re-layouts  2.78 us (4%)
  between operations  0.92 us (1%)
    ppermute x5, starting transfers between devices, swap_core(): return lax.ppermute(block, 'ch', [(0, 1), (1, 0), (2, 3), (3, 2)])  14.4 us
    ppermute x1, starting transfers between devices, local(): lax.ppermute(sent, 'section', [(s, sections - 1 - s) for s in range(secti...  14.2 us
    pallas_call x10, Pallas kernels, call(): pl.pallas_call(kernel, out_shape=[jax.ShapeDtypeStruct(shape, kind) for s...  11.6 us
    ppermute x1, waiting for transfers between devices, local(): lax.ppermute(sent, 'section', [(s, sections - 1 - s) for s in range(secti...  7.3 us
    ppermute x2, starting transfers between devices, shifted(): return lax.ppermute(block, axis, route)  6.95 us
    ppermute x2, waiting for transfers between devices, shifted(): return lax.ppermute(block, axis, route)  6.19 us
    ppermute x2, starting transfers between devices, swap_chip(): return lax.ppermute(block, 'ch', [(0, 2), (2, 0), (1, 3), (3, 1)])  4.47 us
    ppermute x2, waiting for transfers between devices, swap_chip(): return lax.ppermute(block, 'ch', [(0, 2), (2, 0), (1, 3), (3, 1)])  2.89 us
  transfers between devices with their start and end apart: 10, of which 4 were waited for; matrix products, arithmetic and copies ran while one was open for 0% of the time, Pallas kernels for 13%

profile of v5, /device:TPU:1, one launch (start us, length us, event | category | flops | bytes accessed | tf_op | source)
XLA Modules:
  0.0 73.0 jit_solution(2230349063199650464)
XLA Ops:
  0.6 5.7 %collective-permute-start = (bf16[320,384]{1,0:T(8,128)(2,1)}, bf16[320,384]{1,0:T(8,128)(2,1)S(1)}, u32[]{:S(2)}, u32[]{:S(2)}) collective-permute-start(bf16[320,384]{1,0:T(8,128)(2,1)} %bitcast.19), channel_id=1, source_target_pairs={{0,4},{4,8},{8,12},{12,16},{16,20},{20,24},{24,28},{28,32},{32,36}... | collective-permute-start | bytes 737288 | tf_op jit(solution)/shard_map/ppermute | solution.py:22
  6.3 1.7 %copy-done = bf16[1,3,320,1280]{3,2,1,0:T(8,128)(2,1)S(1)} copy-done((bf16[1,3,320,1280]{3,2,1,0:T(8,128)(2,1)S(1)}, bf16[1,3,320,1280]{3,2,1,0:T(8,128)(2,1)}, u32[]{:S(2)}) %copy-start) | copy-done | bytes 2457624
  8.0 0.8 %transpose_kernel.1.weight_ref = bf16[1280,960]{1,0:T(8,128)(2,1)S(1)} custom-call(bf16[960,1280]{1,0:T(8,128)(2,1)S(1)} %bitcast.13), custom_call_target="tpu_custom_call" | custom-call | flops 20000000000 | bytes 20000000 | tf_op jit(solution)/shard_map/transpose_kernel/pallas_call | solution.py:213
  9.1 0.7 prepare_kernel.1
  10.0 1.9 %forward_kernel.1 = (f32[2,320,384]{2,1,0:T(8,128)S(1)}, bf16[960,384]{1,0:T(8,128)(2,1)S(1)}) custom-call(s32[5]{0:T(128)S(1)} %stack.31.place_ref, bf16[320,384]{1,0:T(8,128)(2,1)S(1)} %collective-permute-done.arrived_ref, bf16[320,384]{1,0:T(8,128)(2,1)S(1)} %copy-done.3, bf16[1280,960]{1,0:T(8,128)(2,1)S(1)} %transpose_kernel.1.weight_ref), custom_call_target="tpu_custom_call" | custom-call | tf_op jit(solution)/shard_map/forward_kernel/pallas_call | solution.py:213
  11.9 4.7 %collective-permute-start.2 = (f32[2,320,384]{2,1,0:T(8,128)S(1)}, f32[2,320,384]{2,1,0:T(8,128)S(1)}, u32[]{:S(2)}, u32[]{:S(2)}) collective-permute-start(f32[2,320,384]{2,1,0:T(8,128)S(1)} %get-tuple-element.38), channel_id=1, source_target_pairs={{0,1},{1,0},{2,3},{3,2},{4,5},{5,4},{6,7},{7,6},{8,9},{9,8},{10,11... | collective-permute-start | bytes 2949128 | tf_op jit(solution)/shard_map/ppermute | solution.py:26
  16.6 1.3 %collective-permute-start.1 = (bf16[320,384]{1,0:T(8,128)(2,1)S(1)}, bf16[320,384]{1,0:T(8,128)(2,1)S(1)}, u32[]{:S(2)}, u32[]{:S(2)}) collective-permute-start(bf16[320,384]{1,0:T(8,128)(2,1)S(1)} %bitcast.20), channel_id=1, source_target_pairs={{4,0},{8,4},{12,8},{16,12},{20,16},{24,20},{28,24},{32,28},{36,32}... | collective-permute-start | bytes 737288 | tf_op jit(solution)/shard_map/ppermute | solution.py:22
  17.9 1.4 %own_kernel.1.own_ref = f32[2,320,384]{2,1,0:T(8,128)S(1)} custom-call(s32[5]{0:T(128)S(1)} %stack.31.place_ref, bf16[1280,960]{1,0:T(8,128)(2,1)S(1)} %transpose_kernel.1.weight_ref, bf16[960,384]{1,0:T(8,128)(2,1)S(1)} %get-tuple-element.40.stacked_ref), custom_call_target="tpu_custom_call" | custom-call | flops 20000000000 | bytes 20000000 | tf_op jit(solution)/shard_map/own_kernel/pallas_call | solution.py:213
  20.0 2.2 %collective-permute-start.4 = (bf16[320,384]{1,0:T(8,128)(2,1)S(1)}, bf16[320,384]{1,0:T(8,128)(2,1)S(1)}, u32[]{:S(2)}, u32[]{:S(2)}) collective-permute-start(bf16[320,384]{1,0:T(8,128)(2,1)S(1)} %get-tuple-element.41), channel_id=1, source_target_pairs={{0,2},{2,0},{1,3},{3,1},{4,6},{6,4},{5,7},{7,5},{8,10},{10,8},{9,1... | collective-permute-start | bytes 737288 | tf_op jit(solution)/shard_map/ppermute | solution.py:30
  22.2 6.2 %collective-permute-done.1.returned_ref = bf16[320,384]{1,0:T(8,128)(2,1)S(1)} collective-permute-done((bf16[320,384]{1,0:T(8,128)(2,1)S(1)}, bf16[320,384]{1,0:T(8,128)(2,1)S(1)}, u32[]{:S(2)}, u32[]{:S(2)}) %collective-permute-start.1) | collective-permute-done | bytes 245792 | tf_op jit(solution)/shard_map/ppermute | solution.py:22
  28.4 0.7 scaled_kernel.1.scaled_ref
  29.1 2.2 %collective-permute-start.3 = (bf16[320,384]{1,0:T(8,128)(2,1)S(1)}, bf16[320,384]{1,0:T(8,128)(2,1)S(1)}, u32[]{:S(2)}, u32[]{:S(2)}) collective-permute-start(bf16[320,384]{1,0:T(8,128)(2,1)S(1)} %scaled_kernel.1.scaled_ref), channel_id=1, source_target_pairs={{0,2},{2,0},{1,3},{3,1},{4,6},{6,4},{5,7},{7,5},{8,10},{10,8},{9,1... | collective-permute-start | bytes 737288 | tf_op jit(solution)/shard_map/ppermute | solution.py:30
  31.4 0.8 %saved_kernel.1 = (f32[320,384]{1,0:T(8,128)S(1)}, f32[8,8,128]{2,1,0:T(8,128)S(1)}) custom-call(s32[1,2]{1,0:T(1,128)S(1)} %copy-done.8, bf16[2,320,384]{2,1,0:T(8,128)(2,1)S(1)} %bitcast.16), custom_call_target="tpu_custom_call" | custom-call | flops 20000000000 | bytes 20000000 | tf_op jit(solution)/shard_map/saved_kernel/pallas_call | solution.py:213
  32.2 2.9 %collective-permute-done.4.far_ref = bf16[320,384]{1,0:T(8,128)(2,1)S(1)} collective-permute-done((bf16[320,384]{1,0:T(8,128)(2,1)S(1)}, bf16[320,384]{1,0:T(8,128)(2,1)S(1)}, u32[]{:S(2)}, u32[]{:S(2)}) %collective-permute-start.4) | collective-permute-done | bytes 245792 | tf_op jit(solution)/shard_map/ppermute | solution.py:30
  35.1 1.5 %output_kernel.1 = (bf16[320,384]{1,0:T(8,128)(2,1)}, bf16[320,384]{1,0:T(8,128)(2,1)S(1)}) custom-call(s32[5]{0:T(128)S(1)} %stack.31.place_ref, f32[320,384]{1,0:T(8,128)S(1)} %get-tuple-element.47.near_ref, bf16[320,384]{1,0:T(8,128)(2,1)S(1)} %collective-permute-done.4.far_ref, bf16[320,384]{1,0:T(8,128)(2,1)S(1)} %collective-permute-done.arrived_ref, ...), custom_call_target="tpu_custom_call" | custom-call | tf_op jit(solution)/shard_map/output_kernel/pallas_call | solution.py:213
  36.6 14.2 %collective-permute-start.5 = (bf16[320,384]{1,0:T(8,128)(2,1)S(1)}, bf16[320,384]{1,0:T(8,128)(2,1)S(1)}, u32[]{:S(2)}, u32[]{:S(2)}) collective-permute-start(bf16[320,384]{1,0:T(8,128)(2,1)S(1)} %get-tuple-element.52), channel_id=1, source_target_pairs={{0,508},{4,504},{8,500},{12,496},{16,492},{20,488},{24,484},{28,48... | collective-permute-start | bytes 737288 | tf_op jit(solution)/shard_map/ppermute | solution.py:304
  50.9 3.4 %collective-permute-start.6 = (bf16[160,384]{1,0:T(8,128)(2,1)S(1)}, bf16[160,384]{1,0:T(8,128)(2,1)S(1)}, u32[]{:S(2)}, u32[]{:S(2)}) collective-permute-start(bf16[160,384]{1,0:T(8,128)(2,1)S(1)} %get-tuple-element.57), channel_id=1, source_target_pairs={{0,1},{1,0},{2,3},{3,2},{4,5},{5,4},{6,7},{7,6},{8,9},{9,8},{10,11... | collective-permute-start | bytes 368648 | tf_op jit(solution)/shard_map/ppermute | solution.py:26
  54.2 1.9 %collective-permute-start.7 = (bf16[160,384]{1,0:T(8,128)(2,1)S(1)}, bf16[160,384]{1,0:T(8,128)(2,1)S(1)}, u32[]{:S(2)}, u32[]{:S(2)}) collective-permute-start(bf16[160,384]{1,0:T(8,128)(2,1)S(1)} %get-tuple-element.58), channel_id=1, source_target_pairs={{0,1},{1,0},{2,3},{3,2},{4,5},{5,4},{6,7},{7,6},{8,9},{9,8},{10,11... | collective-permute-start | bytes 368648 | tf_op jit(solution)/shard_map/ppermute | solution.py:26
  56.2 2.4 %collective-permute-start.8 = (bf16[160,384]{1,0:T(8,128)(2,1)S(1)}, bf16[160,384]{1,0:T(8,128)(2,1)S(1)}, u32[]{:S(2)}, u32[]{:S(2)}) collective-permute-start(bf16[160,384]{1,0:T(8,128)(2,1)S(1)} %get-tuple-element.59), channel_id=1, source_target_pairs={{0,1},{1,0},{2,3},{3,2},{4,5},{5,4},{6,7},{7,6},{8,9},{9,8},{10,11... | collective-permute-start | bytes 368648 | tf_op jit(solution)/shard_map/ppermute | solution.py:26
  58.6 1.9 %collective-permute-start.9 = (bf16[160,384]{1,0:T(8,128)(2,1)S(1)}, bf16[160,384]{1,0:T(8,128)(2,1)S(1)}, u32[]{:S(2)}, u32[]{:S(2)}) collective-permute-start(bf16[160,384]{1,0:T(8,128)(2,1)S(1)} %get-tuple-element.60), channel_id=1, source_target_pairs={{0,1},{1,0},{2,3},{3,2},{4,5},{5,4},{6,7},{7,6},{8,9},{9,8},{10,11... | collective-permute-start | bytes 368648 | tf_op jit(solution)/shard_map/ppermute | solution.py:26
  60.5 1.3 %collective-permute-done.9.other_high_ref = bf16[160,384]{1,0:T(8,128)(2,1)S(1)} collective-permute-done((bf16[160,384]{1,0:T(8,128)(2,1)S(1)}, bf16[160,384]{1,0:T(8,128)(2,1)S(1)}, u32[]{:S(2)}, u32[]{:S(2)}) %collective-permute-start.9) | collective-permute-done | bytes 122912 | tf_op jit(solution)/shard_map/ppermute | solution.py:26
  61.8 3.2 %gradient_kernel.1 = bf16[320,384]{1,0:T(8,128)(2,1)} custom-call(s32[5]{0:T(128)S(1)} %stack.31.place_ref, f32[320,384]{1,0:T(8,128)S(1)} %get-tuple-element.53.normed_ref, f32[8,8,128]{2,1,0:T(8,128)S(1)} %get-tuple-element.54.factor_ref, bf16[320,384]{1,0:T(8,128)(2,1)S(1)} %collective-permute-done.1.returned_ref, bf16[320,384]{1,0:T(8,128)(2,1)S(1)} %copy-done.2, ...), custom_call_target="tpu_custom_call" | custom-call | tf_op jit(solution)/shard_map/gradient_kernel/pallas_call | solution.py:213
  65.0 7.3 %collective-permute-done.5 = bf16[320,384]{1,0:T(8,128)(2,1)S(1)} collective-permute-done((bf16[320,384]{1,0:T(8,128)(2,1)S(1)}, bf16[320,384]{1,0:T(8,128)(2,1)S(1)}, u32[]{:S(2)}, u32[]{:S(2)}) %collective-permute-start.5) | collective-permute-done | bytes 245792 | tf_op jit(solution)/shard_map/ppermute | solution.py:304
  72.3 0.7 copy.14
  (28 shorter events, 1.1 us)
Async XLA Ops:
  0.6 9.2 %collective-permute-start = (bf16[320,384]{1,0:T(8,128)(2,1)}, bf16[320,384]{1,0:T(8,128)(2,1)S(1)}, u32[]{:S(2)}, u32[]{:S(2)}) collective-permute-start(bf16[320,384]{1,0:T(8,128)(2,1)} %bitcast.19), channel_id=1, source_target_pairs={{0,4},{4,8},{8,12},{12,16},{16,20},{20,24},{24,28},{28,32},{32,36}... | collective-permute-start | bytes 737288 | tf_op jit(solution)/shard_map/ppermute | solution.py:22
  6.3 1.7 %copy-start = (bf16[1,3,320,1280]{3,2,1,0:T(8,128)(2,1)S(1)}, bf16[1,3,320,1280]{3,2,1,0:T(8,128)(2,1)}, u32[]{:S(2)}) copy-start(bf16[1,3,320,1280]{3,2,1,0:T(8,128)(2,1)} %param.16) | copy-start | bytes 7372804
  8.0 1.0 %copy-start.4 = (bf16[1,2,320,384]{3,2,1,0:T(8,128)(2,1)S(1)}, bf16[1,2,320,384]{3,2,1,0:T(8,128)(2,1)}, u32[]{:S(2)}) copy-start(bf16[1,2,320,384]{3,2,1,0:T(8,128)(2,1)} %param.15) | copy-start | bytes 1474564
  8.0 1.0 %copy-start.6 = (f32[25,320]{1,0:T(8,128)S(1)}, f32[25,320]{1,0:T(8,128)}, u32[]{:S(2)}) copy-start(f32[25,320]{1,0:T(8,128)} %gain_ref) | copy-start | bytes 96004
  8.0 1.0 %copy-start.7 = (s32[1,2]{1,0:T(1,128)S(1)}, s32[1,2]{1,0:T(1,128)}, u32[]{:S(2)}) copy-start(s32[1,2]{1,0:T(1,128)} %stamps_ref.1) | copy-start | bytes 28
  8.0 1.0 %copy-start.8 = (s32[1,2]{1,0:T(1,128)S(1)}, s32[1,2]{1,0:T(1,128)}, u32[]{:S(2)}) copy-start(s32[1,2]{1,0:T(1,128)} %plan_ref.3) | copy-start | bytes 28
  9.1 0.9 %copy-start.3 = (bf16[320,384]{1,0:T(8,128)(2,1)S(1)}, bf16[320,384]{1,0:T(8,128)(2,1)}, u32[]{:S(2)}) copy-start(bf16[320,384]{1,0:T(8,128)(2,1)} %entry_ref.3) | copy-start | bytes 737284
  9.8 6.8 %copy-start.9 = (bf16[1,320,384]{2,1,0:T(8,128)(2,1)S(1)}, bf16[1,320,384]{2,1,0:T(8,128)(2,1)}, u32[]{:S(2)}) copy-start(bf16[1,320,384]{2,1,0:T(8,128)(2,1)} %param.11) | copy-start | bytes 737284
  11.9 7.5 %collective-permute-start.2 = (f32[2,320,384]{2,1,0:T(8,128)S(1)}, f32[2,320,384]{2,1,0:T(8,128)S(1)}, u32[]{:S(2)}, u32[]{:S(2)}) collective-permute-start(f32[2,320,384]{2,1,0:T(8,128)S(1)} %get-tuple-element.38), channel_id=1, source_target_pairs={{0,1},{1,0},{2,3},{3,2},{4,5},{5,4},{6,7},{7,6},{8,9},{9,8},{10,11... | collective-permute-start | bytes 2949128 | tf_op jit(solution)/shard_map/ppermute | solution.py:26
  16.6 11.8 %collective-permute-start.1 = (bf16[320,384]{1,0:T(8,128)(2,1)S(1)}, bf16[320,384]{1,0:T(8,128)(2,1)S(1)}, u32[]{:S(2)}, u32[]{:S(2)}) collective-permute-start(bf16[320,384]{1,0:T(8,128)(2,1)S(1)} %bitcast.20), channel_id=1, source_target_pairs={{4,0},{8,4},{12,8},{16,12},{20,16},{24,20},{28,24},{32,28},{36,32}... | collective-permute-start | bytes 737288 | tf_op jit(solution)/shard_map/ppermute | solution.py:22
  17.9 10.5 %copy-start.2 = (bf16[320,384]{1,0:T(8,128)(2,1)S(1)}, bf16[320,384]{1,0:T(8,128)(2,1)}, u32[]{:S(2)}) copy-start(bf16[320,384]{1,0:T(8,128)(2,1)} %reward_ref.5) | copy-start | bytes 737284
  19.3 12.0 %copy-start.5 = (bf16[1,2,320,384]{3,2,1,0:T(8,128)(2,1)S(1)}, bf16[1,2,320,384]{3,2,1,0:T(8,128)(2,1)}, u32[]{:S(2)}) copy-start(bf16[1,2,320,384]{3,2,1,0:T(8,128)(2,1)} %param.14) | copy-start | bytes 1474564
  20.0 15.1 %collective-permute-start.4 = (bf16[320,384]{1,0:T(8,128)(2,1)S(1)}, bf16[320,384]{1,0:T(8,128)(2,1)S(1)}, u32[]{:S(2)}, u32[]{:S(2)}) collective-permute-start(bf16[320,384]{1,0:T(8,128)(2,1)S(1)} %get-tuple-element.41), channel_id=1, source_target_pairs={{0,2},{2,0},{1,3},{3,1},{4,6},{6,4},{5,7},{7,5},{8,10},{10,8},{9,1... | collective-permute-start | bytes 737288 | tf_op jit(solution)/shard_map/ppermute | solution.py:30
  29.1 21.7 %collective-permute-start.3 = (bf16[320,384]{1,0:T(8,128)(2,1)S(1)}, bf16[320,384]{1,0:T(8,128)(2,1)S(1)}, u32[]{:S(2)}, u32[]{:S(2)}) collective-permute-start(bf16[320,384]{1,0:T(8,128)(2,1)S(1)} %scaled_kernel.1.scaled_ref), channel_id=1, source_target_pairs={{0,2},{2,0},{1,3},{3,1},{4,6},{6,4},{5,7},{7,5},{8,10},{10,8},{9,1... | collective-permute-start | bytes 737288 | tf_op jit(solution)/shard_map/ppermute | solution.py:30
  32.2 29.6 %copy-start.1 = (bf16[1,3,320,1280]{3,2,1,0:T(8,128)(2,1)S(1)}, bf16[1,3,320,1280]{3,2,1,0:T(8,128)(2,1)}, u32[]{:S(2)}) copy-start(bf16[1,3,320,1280]{3,2,1,0:T(8,128)(2,1)} %param.16) | copy-start | bytes 7372804
  36.6 35.8 %collective-permute-start.5 = (bf16[320,384]{1,0:T(8,128)(2,1)S(1)}, bf16[320,384]{1,0:T(8,128)(2,1)S(1)}, u32[]{:S(2)}, u32[]{:S(2)}) collective-permute-start(bf16[320,384]{1,0:T(8,128)(2,1)S(1)} %get-tuple-element.52), channel_id=1, source_target_pairs={{0,508},{4,504},{8,500},{12,496},{16,492},{20,488},{24,484},{28,48... | collective-permute-start | bytes 737288 | tf_op jit(solution)/shard_map/ppermute | solution.py:304
  50.9 9.7 %collective-permute-start.6 = (bf16[160,384]{1,0:T(8,128)(2,1)S(1)}, bf16[160,384]{1,0:T(8,128)(2,1)S(1)}, u32[]{:S(2)}, u32[]{:S(2)}) collective-permute-start(bf16[160,384]{1,0:T(8,128)(2,1)S(1)} %get-tuple-element.57), channel_id=1, source_target_pairs={{0,1},{1,0},{2,3},{3,2},{4,5},{5,4},{6,7},{7,6},{8,9},{9,8},{10,11... | collective-permute-start | bytes 368648 | tf_op jit(solution)/shard_map/ppermute | solution.py:26
  54.2 6.3 %collective-permute-start.7 = (bf16[160,384]{1,0:T(8,128)(2,1)S(1)}, bf16[160,384]{1,0:T(8,128)(2,1)S(1)}, u32[]{:S(2)}, u32[]{:S(2)}) collective-permute-start(bf16[160,384]{1,0:T(8,128)(2,1)S(1)} %get-tuple-element.58), channel_id=1, source_target_pairs={{0,1},{1,0},{2,3},{3,2},{4,5},{5,4},{6,7},{7,6},{8,9},{9,8},{10,11... | collective-permute-start | bytes 368648 | tf_op jit(solution)/shard_map/ppermute | solution.py:26
  56.2 4.4 %collective-permute-start.8 = (bf16[160,384]{1,0:T(8,128)(2,1)S(1)}, bf16[160,384]{1,0:T(8,128)(2,1)S(1)}, u32[]{:S(2)}, u32[]{:S(2)}) collective-permute-start(bf16[160,384]{1,0:T(8,128)(2,1)S(1)} %get-tuple-element.59), channel_id=1, source_target_pairs={{0,1},{1,0},{2,3},{3,2},{4,5},{5,4},{6,7},{7,6},{8,9},{9,8},{10,11... | collective-permute-start | bytes 368648 | tf_op jit(solution)/shard_map/ppermute | solution.py:26
  58.6 3.2 %collective-permute-start.9 = (bf16[160,384]{1,0:T(8,128)(2,1)S(1)}, bf16[160,384]{1,0:T(8,128)(2,1)S(1)}, u32[]{:S(2)}, u32[]{:S(2)}) collective-permute-start(bf16[160,384]{1,0:T(8,128)(2,1)S(1)} %get-tuple-element.60), channel_id=1, source_target_pairs={{0,1},{1,0},{2,3},{3,2},{4,5},{5,4},{6,7},{7,6},{8,9},{9,8},{10,11... | collective-permute-start | bytes 368648 | tf_op jit(solution)/shard_map/ppermute | solution.py:26

commit v6 on v5

--- a/solution.py
+++ b/solution.py
@@ -134,7 +134,7 @@
     entry_ref,
     added_ref,
     columns_ref,
-    returned_ref,
+    cot_ref,
     reward_ref,
     out_ref,
     sent_ref,
@@ -144,8 +144,10 @@
     act_out = x_in + conv_sum * columns_ref[0][:, :1] + added_ref[...].astype(jnp.float32)
     act_out = act_out.astype(jnp.bfloat16)
     out_ref[...] = act_out
-    cot_in = jnp.where(place_ref[3] == 1, reward_ref[...], returned_ref[...])
-    sent_ref[...] = jnp.where(place_ref[4] == 1, act_out, cot_in)
+    cot_in = jnp.where(place_ref[5] == 1, reward_ref[...], cot_ref[...])
+    rows = out_ref.shape[0]
+    sent_ref[rows:, :] = jnp.zeros((sent_ref.shape[0] - rows, sent_ref.shape[1]), jnp.bfloat16)
+    sent_ref[:rows, :] = jnp.where(place_ref[4] == 1, act_out, cot_in)
 
 
 def saved_kernel(plan_ref, stored_ref, normed_ref, factor_ref):
@@ -154,43 +156,15 @@
     factor_ref[...] = jnp.broadcast_to(factor, factor_ref.shape)
 
 
-def split_kernel(scaled_ref, other_ref, *part_refs):
-    half = part_refs[0].shape[0]
-    for i, part_ref in enumerate(part_refs):
-        source_ref = (scaled_ref, other_ref)[i // 2]
-        part_ref[...] = source_ref[i % 2 * half : (i % 2 + 1) * half, :]
-
-
 def gradient_kernel(
-    place_ref,
-    normed_ref,
-    factor_ref,
-    returned_ref,
-    reward_ref,
-    extra_ref,
-    scaled_ref,
-    other_ref,
-    mate_low_ref,
-    mate_high_ref,
-    other_low_ref,
-    other_high_ref,
-    weight_ref,
-    out_ref,
-    whole_ref,
+    place_ref, normed_ref, factor_ref, returned_ref, reward_ref, extra_ref, *refs
 ):
-    rows = scaled_ref.shape[0]
-    core, chip = place_ref[1], place_ref[2]
-
-    def put(chip, core, block, skipped=0):
-        start = pl.multiple_of((chip * 2 + core) * rows + skipped, 32)
-        whole_ref[pl.ds(start, block.shape[0]), :] = block
-
-    put(chip, core, scaled_ref[...])
-    put(1 - chip, core, other_ref[...])
-    put(chip, 1 - core, mate_low_ref[...])
-    put(chip, 1 - core, mate_high_ref[...], rows // 2)
-    put(1 - chip, 1 - core, other_low_ref[...])
-    put(1 - chip, 1 - core, other_high_ref[...], rows // 2)
+    *part_refs, weight_ref, out_ref, whole_ref = refs
+    rows = out_ref.shape[0]
+    ch = place_ref[1] + 2 * place_ref[2]
+    for k in range(4):
+        start = jnp.bitwise_xor(ch, k) * rows
+        whole_ref[pl.ds(pl.multiple_of(start, rows), rows), :] = part_refs[k][...]
     cot_total = cotangent(place_ref, returned_ref, reward_ref, extra_ref)
     normed = normed_ref[...]
     sigmoid = 1.0 / (1.0 + jnp.exp(-normed))
@@ -245,7 +219,8 @@
     stored, skips = stored_inputs[0], skip_buffer[0]
     last = (section == sections - 1).astype(jnp.int32)
     encoder = (section < sections // 2).astype(jnp.int32)
-    place = jnp.stack([section, ch % 2, ch // 2, last, encoder])
+    middle = (section == sections // 2).astype(jnp.int32)
+    place = jnp.stack([section, ch % 2, ch // 2, last, encoder, middle])
     field = ((rows, cells), jnp.bfloat16)
     pair = ((2, rows, cells), jnp.float32)
 
@@ -268,8 +243,6 @@
         [place, arrived, entry_latent, turned],
     )
     mate_part = swap_core(mate_side)
-    cotangents, mate_side = lax.optimization_barrier((cot_carried[0], mate_side))
-    returned = shifted(cotangents, "section", -1)
     (own,) = call(own_kernel, [pair], [SMEM, VMEM, VMEM], [place, turned, stacked], cost=20.0)
     near, far_side = call(
         halves_kernel,
@@ -278,14 +251,8 @@
         [place, own, mate_part],
     )
     far = swap_chip(far_side)
-    returned, far_side = lax.optimization_barrier((returned, far_side))
-    (scaled,) = call(
-        scaled_kernel,
-        [field],
-        [SMEM] + [VMEM] * 4,
-        [place, returned, reward_head, extra, gains],
-    )
-    other = swap_chip(scaled)
+    cotangents, far_side = lax.optimization_barrier((cot_carried[0], far_side))
+    returned = shifted(cotangents, "section", -1)
     stored, far_side = lax.optimization_barrier((stored, far_side))
     saved_normed, saved_factor = call(
         saved_kernel,
@@ -294,27 +261,30 @@
         [plan, stored],
         cost=20.0,
     )
-    far, scaled, saved_normed = lax.optimization_barrier((far, scaled, saved_normed))
+    far, saved_normed = lax.optimization_barrier((far, saved_normed))
     act_out, sent = call(
         output_kernel,
-        [field, field],
+        [field, ((rows + 16, cells), jnp.bfloat16)],
         [SMEM] + [VMEM] * 8,
-        [place, near, far, arrived, entry_latent, added, gains, returned, reward_head],
-    )
-    mirror_in = lax.ppermute(sent, "section", [(s, sections - 1 - s) for s in range(sections)])
-
-    other, scaled, act_out = lax.optimization_barrier((other, scaled, act_out))
-    parts = call(
-        split_kernel,
-        [((rows // 2, cells), jnp.bfloat16)] * 4,
-        [VMEM] * 2,
-        [scaled, other],
-    )
-    mates = [swap_core(part) for part in parts]
+        [place, near, far, arrived, entry_latent, added, gains, cot_carried[0], reward_head],
+    )
+    half = sections // 2
+    route = [(s, sections - 1 - s) for s in range(half)]
+    route += [(s, (sections - s) % half) for s in range(half, sections)]
+    mirror_in = lax.ppermute(sent, "section", route)[:rows]
+
+    returned, act_out = lax.optimization_barrier((returned, act_out))
+    (scaled,) = call(
+        scaled_kernel,
+        [field],
+        [SMEM] + [VMEM] * 4,
+        [place, returned, reward_head, extra, gains],
+    )
+    gathered = [lax.ppermute(scaled, "ch", [(c, c ^ k) for c in range(4)]) for k in (1, 2, 3)]
     (cot_out,) = call(
         gradient_kernel,
         [field],
-        [SMEM] + [VMEM] * 12,
+        [SMEM] + [VMEM] * 10,
         [
             place,
             saved_normed,
@@ -323,8 +293,7 @@
             reward_head,
             extra,
             scaled,
-            other,
-            *mates,
+            *gathered,
             weight,
         ],
         scratch=[pltpu.VMEM((full, cells), jnp.bfloat16)],

time: 73.4 us -> 74.3 us (1.012)
  the two profiles are of different devices: /device:TPU:1 before, /device:TPU:121 now
where the time goes in v6:
time: 74.3 us; the launch traced here: 74 us
  starting transfers between devices  45 us (61%)
  waiting for transfers between devices  13.8 us (19%)
  Pallas kernels  11.6 us (16%)
  local copies, waits for them, and re-layouts  2.61 us (4%)
  between operations  0.87 us (1%)
    ppermute x1, starting transfers between devices, local(): mirror_in = lax.ppermute(sent, 'section', route)[:rows]  21.3 us
    pallas_call x9, Pallas kernels, call(): pl.pallas_call(kernel, out_shape=[jax.ShapeDtypeStruct(shape, kind) for s...  11.6 us
    ppermute x3, waiting for transfers between devices, local(): lax.ppermute(scaled, 'ch', [(c, c ^ k) for c in range(4)])  9.36 us
    ppermute x2, starting transfers between devices, shifted(): return lax.ppermute(block, axis, route)  9.03 us
    ppermute x3, starting transfers between devices, local(): lax.ppermute(scaled, 'ch', [(c, c ^ k) for c in range(4)])  8.85 us
    ppermute x1, starting transfers between devices, swap_core(): return lax.ppermute(block, 'ch', [(0, 1), (1, 0), (2, 3), (3, 2)])  3.46 us
    ppermute x1, starting transfers between devices, swap_chip(): return lax.ppermute(block, 'ch', [(0, 2), (2, 0), (1, 3), (3, 1)])  2.37 us
    ppermute x1, waiting for transfers between devices, swap_chip(): return lax.ppermute(block, 'ch', [(0, 2), (2, 0), (1, 3), (3, 1)])  2.21 us
  transfers between devices with their start and end apart: 8, of which 5 were waited for; matrix products, arithmetic and copies ran while one was open for 0% of the time, Pallas kernels for 12%

profile of v6, /device:TPU:121, one launch (start us, length us, event | category | flops | bytes accessed | tf_op | source)
XLA Modules:
  0.0 74.0 jit_solution(18088029629960503984)
XLA Ops:
  0.6 5.4 %collective-permute-start = (bf16[320,384]{1,0:T(8,128)(2,1)}, bf16[320,384]{1,0:T(8,128)(2,1)S(1)}, u32[]{:S(2)}, u32[]{:S(2)}) collective-permute-start(bf16[320,384]{1,0:T(8,128)(2,1)} %bitcast.22), channel_id=1, source_target_pairs={{0,4},{4,8},{8,12},{12,16},{16,20},{20,24},{24,28},{28,32},{32,36}... | collective-permute-start | bytes 737288 | tf_op jit(solution)/shard_map/ppermute | solution.py:22
  6.1 1.7 %copy-done = bf16[1,3,320,1280]{3,2,1,0:T(8,128)(2,1)S(1)} copy-done((bf16[1,3,320,1280]{3,2,1,0:T(8,128)(2,1)S(1)}, bf16[1,3,320,1280]{3,2,1,0:T(8,128)(2,1)}, u32[]{:S(2)}) %copy-start) | copy-done | bytes 2457624
  7.8 0.8 %transpose_kernel.1.weight_ref = bf16[1280,960]{1,0:T(8,128)(2,1)S(1)} custom-call(bf16[960,1280]{1,0:T(8,128)(2,1)S(1)} %bitcast.14), custom_call_target="tpu_custom_call" | custom-call | flops 20000000000 | bytes 20000000 | tf_op jit(solution)/shard_map/transpose_kernel/pallas_call | solution.py:187
  8.8 0.7 prepare_kernel.1
  9.5 1.5 %collective-permute-done.arrived_ref = bf16[320,384]{1,0:T(8,128)(2,1)S(1)} collective-permute-done((bf16[320,384]{1,0:T(8,128)(2,1)}, bf16[320,384]{1,0:T(8,128)(2,1)S(1)}, u32[]{:S(2)}, u32[]{:S(2)}) %collective-permute-start) | collective-permute-done | bytes 245792 | tf_op jit(solution)/shard_map/ppermute | solution.py:22
  11.1 1.9 %forward_kernel.1 = (f32[2,320,384]{2,1,0:T(8,128)S(1)}, bf16[960,384]{1,0:T(8,128)(2,1)S(1)}) custom-call(s32[6]{0:T(128)S(1)} %stack.39.place_ref, bf16[320,384]{1,0:T(8,128)(2,1)S(1)} %collective-permute-done.arrived_ref, bf16[320,384]{1,0:T(8,128)(2,1)S(1)} %copy-done.3, bf16[1280,960]{1,0:T(8,128)(2,1)S(1)} %transpose_kernel.1.weight_ref), custom_call_target="tpu_custom_call" | custom-call | tf_op jit(solution)/shard_map/forward_kernel/pallas_call | solution.py:187
  12.9 3.5 %collective-permute-start.1 = (f32[2,320,384]{2,1,0:T(8,128)S(1)}, f32[2,320,384]{2,1,0:T(8,128)S(1)}, u32[]{:S(2)}, u32[]{:S(2)}) collective-permute-start(f32[2,320,384]{2,1,0:T(8,128)S(1)} %get-tuple-element.32), channel_id=1, source_target_pairs={{0,1},{1,0},{2,3},{3,2},{4,5},{5,4},{6,7},{7,6},{8,9},{9,8},{10,11... | collective-permute-start | bytes 2949128 | tf_op jit(solution)/shard_map/ppermute | solution.py:26
  16.4 1.4 %own_kernel.1.own_ref = f32[2,320,384]{2,1,0:T(8,128)S(1)} custom-call(s32[6]{0:T(128)S(1)} %stack.39.place_ref, bf16[1280,960]{1,0:T(8,128)(2,1)S(1)} %transpose_kernel.1.weight_ref, bf16[960,384]{1,0:T(8,128)(2,1)S(1)} %get-tuple-element.31.stacked_ref), custom_call_target="tpu_custom_call" | custom-call | flops 20000000000 | bytes 20000000 | tf_op jit(solution)/shard_map/own_kernel/pallas_call | solution.py:187
  17.8 0.7 %collective-permute-done.1.mate_ref = f32[2,320,384]{2,1,0:T(8,128)S(1)} collective-permute-done((f32[2,320,384]{2,1,0:T(8,128)S(1)}, f32[2,320,384]{2,1,0:T(8,128)S(1)}, u32[]{:S(2)}, u32[]{:S(2)}) %collective-permute-start.1) | collective-permute-done | bytes 983072 | tf_op jit(solution)/shard_map/ppermute | solution.py:26
  18.6 0.6 halves_kernel.1
  19.2 2.4 %collective-permute-start.3 = (bf16[320,384]{1,0:T(8,128)(2,1)S(1)}, bf16[320,384]{1,0:T(8,128)(2,1)S(1)}, u32[]{:S(2)}, u32[]{:S(2)}) collective-permute-start(bf16[320,384]{1,0:T(8,128)(2,1)S(1)} %get-tuple-element.33), channel_id=1, source_target_pairs={{0,2},{2,0},{1,3},{3,1},{4,6},{6,4},{5,7},{7,5},{8,10},{10,8},{9,1... | collective-permute-start | bytes 737288 | tf_op jit(solution)/shard_map/ppermute | solution.py:30
  21.6 3.6 %collective-permute-start.2 = (bf16[320,384]{1,0:T(8,128)(2,1)S(1)}, bf16[320,384]{1,0:T(8,128)(2,1)S(1)}, u32[]{:S(2)}, u32[]{:S(2)}) collective-permute-start(bf16[320,384]{1,0:T(8,128)(2,1)S(1)} %bitcast.16), channel_id=1, source_target_pairs={{4,0},{8,4},{12,8},{16,12},{20,16},{24,20},{28,24},{32,28},{36,32}... | collective-permute-start | bytes 737288 | tf_op jit(solution)/shard_map/ppermute | solution.py:22
  25.2 0.8 %saved_kernel.1 = (f32[320,384]{1,0:T(8,128)S(1)}, f32[8,8,128]{2,1,0:T(8,128)S(1)}) custom-call(s32[1,2]{1,0:T(1,128)S(1)} %copy-done.9, bf16[2,320,384]{2,1,0:T(8,128)(2,1)S(1)} %bitcast.19), custom_call_target="tpu_custom_call" | custom-call | flops 20000000000 | bytes 20000000 | tf_op jit(solution)/shard_map/saved_kernel/pallas_call | solution.py:187
  26.1 2.2 %collective-permute-done.3.far_ref = bf16[320,384]{1,0:T(8,128)(2,1)S(1)} collective-permute-done((bf16[320,384]{1,0:T(8,128)(2,1)S(1)}, bf16[320,384]{1,0:T(8,128)(2,1)S(1)}, u32[]{:S(2)}, u32[]{:S(2)}) %collective-permute-start.3) | collective-permute-done | bytes 245792 | tf_op jit(solution)/shard_map/ppermute | solution.py:30
  28.3 1.5 %output_kernel.1 = (bf16[320,384]{1,0:T(8,128)(2,1)}, bf16[336,384]{1,0:T(8,128)(2,1)S(1)}) custom-call(s32[6]{0:T(128)S(1)} %stack.39.place_ref, f32[320,384]{1,0:T(8,128)S(1)} %get-tuple-element.35.near_ref, bf16[320,384]{1,0:T(8,128)(2,1)S(1)} %collective-permute-done.3.far_ref, bf16[320,384]{1,0:T(8,128)(2,1)S(1)} %collective-permute-done.arrived_ref, ...), custom_call_target="tpu_custom_call" | custom-call | tf_op jit(solution)/shard_map/output_kernel/pallas_call | solution.py:187
  29.8 21.3 %collective-permute-start.4 = (bf16[336,384]{1,0:T(8,128)(2,1)S(1)}, bf16[336,384]{1,0:T(8,128)(2,1)S(1)}, u32[]{:S(2)}, u32[]{:S(2)}) collective-permute-start(bf16[336,384]{1,0:T(8,128)(2,1)S(1)} %get-tuple-element.42), channel_id=1, source_target_pairs={{0,508},{4,504},{8,500},{12,496},{16,492},{20,488},{24,484},{28,48... | collective-permute-start | bytes 774152 | tf_op jit(solution)/shard_map/ppermute | solution.py:274
  51.1 0.7 scaled_kernel.1.refs_0_
  51.8 3.4 %collective-permute-start.5 = (bf16[320,384]{1,0:T(8,128)(2,1)S(1)}, bf16[320,384]{1,0:T(8,128)(2,1)S(1)}, u32[]{:S(2)}, u32[]{:S(2)}) collective-permute-start(bf16[320,384]{1,0:T(8,128)(2,1)S(1)} %scaled_kernel.1.refs_0_), channel_id=1, source_target_pairs={{0,1},{1,0},{2,3},{3,2},{4,5},{5,4},{6,7},{7,6},{8,9},{9,8},{10,11... | collective-permute-start | bytes 737288 | tf_op jit(solution)/shard_map/ppermute | solution.py:283
  55.2 1.9 %collective-permute-start.6 = (bf16[320,384]{1,0:T(8,128)(2,1)S(1)}, bf16[320,384]{1,0:T(8,128)(2,1)S(1)}, u32[]{:S(2)}, u32[]{:S(2)}) collective-permute-start(bf16[320,384]{1,0:T(8,128)(2,1)S(1)} %scaled_kernel.1.refs_0_), channel_id=1, source_target_pairs={{0,2},{1,3},{2,0},{3,1},{4,6},{5,7},{6,4},{7,5},{8,10},{9,11},{10,... | collective-permute-start | bytes 737288 | tf_op jit(solution)/shard_map/ppermute | solution.py:283
  57.1 3.5 %collective-permute-start.7 = (bf16[320,384]{1,0:T(8,128)(2,1)S(1)}, bf16[320,384]{1,0:T(8,128)(2,1)S(1)}, u32[]{:S(2)}, u32[]{:S(2)}) collective-permute-start(bf16[320,384]{1,0:T(8,128)(2,1)S(1)} %scaled_kernel.1.refs_0_), channel_id=1, source_target_pairs={{0,3},{1,2},{2,1},{3,0},{4,7},{5,6},{6,5},{7,4},{8,11},{9,10},{10,... | collective-permute-start | bytes 737288 | tf_op jit(solution)/shard_map/ppermute | solution.py:283
  60.7 4.0 %collective-permute-done.6.refs_2_ = bf16[320,384]{1,0:T(8,128)(2,1)S(1)} collective-permute-done((bf16[320,384]{1,0:T(8,128)(2,1)S(1)}, bf16[320,384]{1,0:T(8,128)(2,1)S(1)}, u32[]{:S(2)}, u32[]{:S(2)}) %collective-permute-start.6) | collective-permute-done | bytes 245792 | tf_op jit(solution)/shard_map/ppermute | solution.py:283
  64.7 5.4 %collective-permute-done.7.refs_3_ = bf16[320,384]{1,0:T(8,128)(2,1)S(1)} collective-permute-done((bf16[320,384]{1,0:T(8,128)(2,1)S(1)}, bf16[320,384]{1,0:T(8,128)(2,1)S(1)}, u32[]{:S(2)}, u32[]{:S(2)}) %collective-permute-start.7) | collective-permute-done | bytes 245792 | tf_op jit(solution)/shard_map/ppermute | solution.py:283
  70.0 3.2 %gradient_kernel.1 = bf16[320,384]{1,0:T(8,128)(2,1)} custom-call(s32[6]{0:T(128)S(1)} %stack.39.place_ref, f32[320,384]{1,0:T(8,128)S(1)} %get-tuple-element.43.normed_ref, f32[8,8,128]{2,1,0:T(8,128)S(1)} %get-tuple-element.44.factor_ref, bf16[320,384]{1,0:T(8,128)(2,1)S(1)} %collective-permute-done.2.returned_ref, bf16[320,384]{1,0:T(8,128)(2,1)S(1)} %copy-done.2, ...), custom_call_target="tpu_custom_call" | custom-call | tf_op jit(solution)/shard_map/gradient_kernel/pallas_call | solution.py:187
  73.2 0.7 slice.4
  (23 shorter events, 0.2 us)
Async XLA Ops:
  0.6 10.4 %collective-permute-start = (bf16[320,384]{1,0:T(8,128)(2,1)}, bf16[320,384]{1,0:T(8,128)(2,1)S(1)}, u32[]{:S(2)}, u32[]{:S(2)}) collective-permute-start(bf16[320,384]{1,0:T(8,128)(2,1)} %bitcast.22), channel_id=1, source_target_pairs={{0,4},{4,8},{8,12},{12,16},{16,20},{20,24},{24,28},{28,32},{32,36}... | collective-permute-start | bytes 737288 | tf_op jit(solution)/shard_map/ppermute | solution.py:22
  6.1 1.7 %copy-start = (bf16[1,3,320,1280]{3,2,1,0:T(8,128)(2,1)S(1)}, bf16[1,3,320,1280]{3,2,1,0:T(8,128)(2,1)}, u32[]{:S(2)}) copy-start(bf16[1,3,320,1280]{3,2,1,0:T(8,128)(2,1)} %param.16) | copy-start | bytes 7372804
  7.8 1.0 %copy-start.5 = (bf16[1,2,320,384]{3,2,1,0:T(8,128)(2,1)S(1)}, bf16[1,2,320,384]{3,2,1,0:T(8,128)(2,1)}, u32[]{:S(2)}) copy-start(bf16[1,2,320,384]{3,2,1,0:T(8,128)(2,1)} %param.15) | copy-start | bytes 1474564
  7.8 1.0 %copy-start.7 = (f32[25,320]{1,0:T(8,128)S(1)}, f32[25,320]{1,0:T(8,128)}, u32[]{:S(2)}) copy-start(f32[25,320]{1,0:T(8,128)} %gain_ref) | copy-start | bytes 96004
  7.8 1.0 %copy-start.8 = (s32[1,2]{1,0:T(1,128)S(1)}, s32[1,2]{1,0:T(1,128)}, u32[]{:S(2)}) copy-start(s32[1,2]{1,0:T(1,128)} %stamps_ref.1) | copy-start | bytes 28
  7.8 1.0 %copy-start.9 = (s32[1,2]{1,0:T(1,128)S(1)}, s32[1,2]{1,0:T(1,128)}, u32[]{:S(2)}) copy-start(s32[1,2]{1,0:T(1,128)} %plan_ref.3) | copy-start | bytes 28
  8.8 2.2 %copy-start.3 = (bf16[320,384]{1,0:T(8,128)(2,1)S(1)}, bf16[320,384]{1,0:T(8,128)(2,1)}, u32[]{:S(2)}) copy-start(bf16[320,384]{1,0:T(8,128)(2,1)} %entry_ref.3) | copy-start | bytes 737284
  12.9 5.6 %collective-permute-start.1 = (f32[2,320,384]{2,1,0:T(8,128)S(1)}, f32[2,320,384]{2,1,0:T(8,128)S(1)}, u32[]{:S(2)}, u32[]{:S(2)}) collective-permute-start(f32[2,320,384]{2,1,0:T(8,128)S(1)} %get-tuple-element.32), channel_id=1, source_target_pairs={{0,1},{1,0},{2,3},{3,2},{4,5},{5,4},{6,7},{7,6},{8,9},{9,8},{10,11... | collective-permute-start | bytes 2949128 | tf_op jit(solution)/shard_map/ppermute | solution.py:26
  16.4 5.2 %copy-start.4 = (bf16[1,320,384]{2,1,0:T(8,128)(2,1)S(1)}, bf16[1,320,384]{2,1,0:T(8,128)(2,1)}, u32[]{:S(2)}) copy-start(bf16[1,320,384]{2,1,0:T(8,128)(2,1)} %param.11) | copy-start | bytes 737284
  16.4 8.8 %copy-start.6 = (bf16[1,2,320,384]{3,2,1,0:T(8,128)(2,1)S(1)}, bf16[1,2,320,384]{3,2,1,0:T(8,128)(2,1)}, u32[]{:S(2)}) copy-start(bf16[1,2,320,384]{3,2,1,0:T(8,128)(2,1)} %param.14) | copy-start | bytes 1474564
  19.2 9.1 %collective-permute-start.3 = (bf16[320,384]{1,0:T(8,128)(2,1)S(1)}, bf16[320,384]{1,0:T(8,128)(2,1)S(1)}, u32[]{:S(2)}, u32[]{:S(2)}) collective-permute-start(bf16[320,384]{1,0:T(8,128)(2,1)S(1)} %get-tuple-element.33), channel_id=1, source_target_pairs={{0,2},{2,0},{1,3},{3,1},{4,6},{6,4},{5,7},{7,5},{8,10},{10,8},{9,1... | collective-permute-start | bytes 737288 | tf_op jit(solution)/shard_map/ppermute | solution.py:30
  21.6 6.7 %copy-start.2 = (bf16[320,384]{1,0:T(8,128)(2,1)S(1)}, bf16[320,384]{1,0:T(8,128)(2,1)}, u32[]{:S(2)}) copy-start(bf16[320,384]{1,0:T(8,128)(2,1)} %reward_ref.5) | copy-start | bytes 737284
  21.6 29.5 %collective-permute-start.2 = (bf16[320,384]{1,0:T(8,128)(2,1)S(1)}, bf16[320,384]{1,0:T(8,128)(2,1)S(1)}, u32[]{:S(2)}, u32[]{:S(2)}) collective-permute-start(bf16[320,384]{1,0:T(8,128)(2,1)S(1)} %bitcast.16), channel_id=1, source_target_pairs={{4,0},{8,4},{12,8},{16,12},{20,16},{24,20},{28,24},{32,28},{36,32}... | collective-permute-start | bytes 737288 | tf_op jit(solution)/shard_map/ppermute | solution.py:22
  26.1 44.0 %copy-start.1 = (bf16[1,3,320,1280]{3,2,1,0:T(8,128)(2,1)S(1)}, bf16[1,3,320,1280]{3,2,1,0:T(8,128)(2,1)}, u32[]{:S(2)}) copy-start(bf16[1,3,320,1280]{3,2,1,0:T(8,128)(2,1)} %param.16) | copy-start | bytes 7372804
  29.8 43.5 %collective-permute-start.4 = (bf16[336,384]{1,0:T(8,128)(2,1)S(1)}, bf16[336,384]{1,0:T(8,128)(2,1)S(1)}, u32[]{:S(2)}, u32[]{:S(2)}) collective-permute-start(bf16[336,384]{1,0:T(8,128)(2,1)S(1)} %get-tuple-element.42), channel_id=1, source_target_pairs={{0,508},{4,504},{8,500},{12,496},{16,492},{20,488},{24,484},{28,48... | collective-permute-start | bytes 774152 | tf_op jit(solution)/shard_map/ppermute | solution.py:274
  51.8 8.9 %collective-permute-start.5 = (bf16[320,384]{1,0:T(8,128)(2,1)S(1)}, bf16[320,384]{1,0:T(8,128)(2,1)S(1)}, u32[]{:S(2)}, u32[]{:S(2)}) collective-permute-start(bf16[320,384]{1,0:T(8,128)(2,1)S(1)} %scaled_kernel.1.refs_0_), channel_id=1, source_target_pairs={{0,1},{1,0},{2,3},{3,2},{4,5},{5,4},{6,7},{7,6},{8,9},{9,8},{10,11... | collective-permute-start | bytes 737288 | tf_op jit(solution)/shard_map/ppermute | solution.py:283
  55.2 9.5 %collective-permute-start.6 = (bf16[320,384]{1,0:T(8,128)(2,1)S(1)}, bf16[320,384]{1,0:T(8,128)(2,1)S(1)}, u32[]{:S(2)}, u32[]{:S(2)}) collective-permute-start(bf16[320,384]{1,0:T(8,128)(2,1)S(1)} %scaled_kernel.1.refs_0_), channel_id=1, source_target_pairs={{0,2},{1,3},{2,0},{3,1},{4,6},{5,7},{6,4},{7,5},{8,10},{9,11},{10,... | collective-permute-start | bytes 737288 | tf_op jit(solution)/shard_map/ppermute | solution.py:283
  57.1 12.9 %collective-permute-start.7 = (bf16[320,384]{1,0:T(8,128)(2,1)S(1)}, bf16[320,384]{1,0:T(8,128)(2,1)S(1)}, u32[]{:S(2)}, u32[]{:S(2)}) collective-permute-start(bf16[320,384]{1,0:T(8,128)(2,1)S(1)} %scaled_kernel.1.refs_0_), channel_id=1, source_target_pairs={{0,3},{1,2},{2,1},{3,0},{4,7},{5,6},{6,5},{7,4},{8,11},{9,10},{10,... | collective-permute-start | bytes 737288 | tf_op jit(solution)/shard_map/ppermute | solution.py:283

commit v7 on v5

--- a/solution.py
+++ b/solution.py
@@ -134,7 +134,7 @@
     entry_ref,
     added_ref,
     columns_ref,
-    returned_ref,
+    cot_ref,
     reward_ref,
     out_ref,
     sent_ref,
@@ -144,7 +144,7 @@
     act_out = x_in + conv_sum * columns_ref[0][:, :1] + added_ref[...].astype(jnp.float32)
     act_out = act_out.astype(jnp.bfloat16)
     out_ref[...] = act_out
-    cot_in = jnp.where(place_ref[3] == 1, reward_ref[...], returned_ref[...])
+    cot_in = jnp.where(place_ref[5] == 1, reward_ref[...], cot_ref[...])
     sent_ref[...] = jnp.where(place_ref[4] == 1, act_out, cot_in)
 
 
@@ -245,7 +245,8 @@
     stored, skips = stored_inputs[0], skip_buffer[0]
     last = (section == sections - 1).astype(jnp.int32)
     encoder = (section < sections // 2).astype(jnp.int32)
-    place = jnp.stack([section, ch % 2, ch // 2, last, encoder])
+    middle = (section == sections // 2).astype(jnp.int32)
+    place = jnp.stack([section, ch % 2, ch // 2, last, encoder, middle])
     field = ((rows, cells), jnp.bfloat16)
     pair = ((2, rows, cells), jnp.float32)
 
@@ -259,7 +260,8 @@
         [place, plan, timesteps, skips, time_gain],
         cost=20.0,
     )
-    gains, turned = lax.optimization_barrier((gains, turned))
+    cotangents, gains, turned = lax.optimization_barrier((cot_carried[0], gains, turned))
+    returned = shifted(cotangents, "section", -1)
 
     mate_side, stacked = call(
         forward_kernel,
@@ -268,8 +270,6 @@
         [place, arrived, entry_latent, turned],
     )
     mate_part = swap_core(mate_side)
-    cotangents, mate_side = lax.optimization_barrier((cot_carried[0], mate_side))
-    returned = shifted(cotangents, "section", -1)
     (own,) = call(own_kernel, [pair], [SMEM, VMEM, VMEM], [place, turned, stacked], cost=20.0)
     near, far_side = call(
         halves_kernel,
@@ -299,9 +299,12 @@
         output_kernel,
         [field, field],
         [SMEM] + [VMEM] * 8,
-        [place, near, far, arrived, entry_latent, added, gains, returned, reward_head],
-    )
-    mirror_in = lax.ppermute(sent, "section", [(s, sections - 1 - s) for s in range(sections)])
+        [place, near, far, arrived, entry_latent, added, gains, cot_carried[0], reward_head],
+    )
+    half = sections // 2
+    route = [(s, sections - 1 - s) for s in range(half)]
+    route += [(s, (sections - s) % half) for s in range(half, sections)]
+    mirror_in = lax.ppermute(sent, "section", route)
 
     other, scaled, act_out = lax.optimization_barrier((other, scaled, act_out))
     parts = call(

time: 73.4 us -> 67.7 us (0.922)
  waiting for transfers between devices: 17.7 us -> 9.28 us
  starting transfers between devices: 40 us -> 42.6 us
    ppermute x2, waiting for transfers between devices: 6.19 us -> 0.01 us  [shifted(): return lax.ppermute(block, axis, route)]
    ppermute x1, waiting for transfers between devices: 7.3 us -> 5 us  [local(): mirror_in = lax.ppermute(sent, 'section', route)]
    ppermute x1, starting transfers between devices: 14.2 us -> 15.5 us  [local(): mirror_in = lax.ppermute(sent, 'section', route)]
    ppermute x2, starting transfers between devices: 4.47 us -> 5.28 us  [swap_chip(): return lax.ppermute(block, 'ch', [(0, 2), (2, 0), (1, 3), (3, 1)])]
    ppermute x5, waiting for transfers between devices: 1.28 us -> 2.03 us  [swap_core(): return lax.ppermute(block, 'ch', [(0, 1), (1, 0), (2, 3), (3, 2)])]
  transfers between devices with their start and end apart: 10 -> 10, of which waited for: 4 -> 4; matrix products, arithmetic and copies ran while one was open for 0% -> 0% of each run, Pallas kernels for 13% -> 17%
where the time goes in v7:
time: 67.7 us; the launch traced here: 67.3 us
  starting transfers between devices  42.6 us (63%)
  Pallas kernels  11.7 us (17%)
  waiting for transfers between devices  9.28 us (14%)
  local copies, waits for them, and re-layouts  2.79 us (4%)
  between operations  0.93 us (1%)
    ppermute x1, starting transfers between devices, local(): mirror_in = lax.ppermute(sent, 'section', route)  15.5 us
    ppermute x5, starting transfers between devices, swap_core(): return lax.ppermute(block, 'ch', [(0, 1), (1, 0), (2, 3), (3, 2)])  14.9 us
    pallas_call x10, Pallas kernels, call(): pl.pallas_call(kernel, out_shape=[jax.ShapeDtypeStruct(shape, kind) for s...  11.7 us
    ppermute x2, starting transfers between devices, shifted(): return lax.ppermute(block, axis, route)  6.94 us
    ppermute x2, starting transfers between devices, swap_chip(): return lax.ppermute(block, 'ch', [(0, 2), (2, 0), (1, 3), (3, 1)])  5.28 us
    ppermute x1, waiting for transfers between devices, local(): mirror_in = lax.ppermute(sent, 'section', route)  5 us
    unnamed x21, local copies, waits for them, and re-layouts  2.7 us
    ppermute x2, waiting for transfers between devices, swap_chip(): return lax.ppermute(block, 'ch', [(0, 2), (2, 0), (1, 3), (3, 1)])  2.25 us
  transfers between devices with their start and end apart: 10, of which 4 were waited for; matrix products, arithmetic and copies ran while one was open for 0% of the time, Pallas kernels for 17%

profile of v7, /device:TPU:1, one launch (start us, length us, event | category | flops | bytes accessed | tf_op | source)
XLA Modules:
  0.0 67.3 jit_solution(6502865082530239989)
XLA Ops:
  0.6 5.7 %collective-permute-start.1 = (bf16[320,384]{1,0:T(8,128)(2,1)}, bf16[320,384]{1,0:T(8,128)(2,1)S(1)}, u32[]{:S(2)}, u32[]{:S(2)}) collective-permute-start(bf16[320,384]{1,0:T(8,128)(2,1)} %bitcast.22), channel_id=1, source_target_pairs={{0,4},{4,8},{8,12},{12,16},{16,20},{20,24},{24,28},{28,32},{32,36}... | collective-permute-start | bytes 737288 | tf_op jit(solution)/shard_map/ppermute | solution.py:22
  6.3 1.7 %copy-done = bf16[1,3,320,1280]{3,2,1,0:T(8,128)(2,1)S(1)} copy-done((bf16[1,3,320,1280]{3,2,1,0:T(8,128)(2,1)S(1)}, bf16[1,3,320,1280]{3,2,1,0:T(8,128)(2,1)}, u32[]{:S(2)}) %copy-start) | copy-done | bytes 2457624
  8.0 0.8 %transpose_kernel.1.weight_ref = bf16[1280,960]{1,0:T(8,128)(2,1)S(1)} custom-call(bf16[960,1280]{1,0:T(8,128)(2,1)S(1)} %bitcast.14), custom_call_target="tpu_custom_call" | custom-call | flops 20000000000 | bytes 20000000 | tf_op jit(solution)/shard_map/transpose_kernel/pallas_call | solution.py:213
  9.1 0.7 %prepare_kernel.1 = (f32[2,320,128]{2,1,0:T(8,128)S(1)}, bf16[320,384]{1,0:T(8,128)(2,1)S(1)}, bf16[320,384]{1,0:T(8,128)(2,1)S(1)}) custom-call(s32[6]{0:T(128)S(1)} %stack.39.place_ref, s32[1,2]{1,0:T(1,128)S(1)} %copy-done.9, s32[1,2]{1,0:T(1,128)S(1)} %copy-done.8, bf16[2,320,384]{2,1,0:T(8,128)(2,1)S(1)} %bitcast.18, f32[25,320]{1,0:T(8,128)S(1)} %copy-done.7), custom_call_target="tpu_custom_call" | custom-call | flops 20000000000 | bytes 20000000 | tf_op jit(solution)/shard_map/prepare_kernel/pallas_call | solution.py:213
  10.0 1.3 %collective-permute-start = (bf16[320,384]{1,0:T(8,128)(2,1)S(1)}, bf16[320,384]{1,0:T(8,128)(2,1)S(1)}, u32[]{:S(2)}, u32[]{:S(2)}) collective-permute-start(bf16[320,384]{1,0:T(8,128)(2,1)S(1)} %bitcast.16), channel_id=1, source_target_pairs={{4,0},{8,4},{12,8},{16,12},{20,16},{24,20},{28,24},{32,28},{36,32}... | collective-permute-start | bytes 737288 | tf_op jit(solution)/shard_map/ppermute | solution.py:22
  11.3 1.9 %forward_kernel.1 = (f32[2,320,384]{2,1,0:T(8,128)S(1)}, bf16[960,384]{1,0:T(8,128)(2,1)S(1)}) custom-call(s32[6]{0:T(128)S(1)} %stack.39.place_ref, bf16[320,384]{1,0:T(8,128)(2,1)S(1)} %collective-permute-done.1.arrived_ref, bf16[320,384]{1,0:T(8,128)(2,1)S(1)} %copy-done.3, bf16[1280,960]{1,0:T(8,128)(2,1)S(1)} %transpose_kernel.1.weight_ref), custom_call_target="tpu_custom_call" | custom-call | tf_op jit(solution)/shard_map/forward_kernel/pallas_call | solution.py:213
  13.2 4.4 %collective-permute-start.2 = (f32[2,320,384]{2,1,0:T(8,128)S(1)}, f32[2,320,384]{2,1,0:T(8,128)S(1)}, u32[]{:S(2)}, u32[]{:S(2)}) collective-permute-start(f32[2,320,384]{2,1,0:T(8,128)S(1)} %get-tuple-element.40), channel_id=1, source_target_pairs={{0,1},{1,0},{2,3},{3,2},{4,5},{5,4},{6,7},{7,6},{8,9},{9,8},{10,11... | collective-permute-start | bytes 2949128 | tf_op jit(solution)/shard_map/ppermute | solution.py:26
  17.6 1.4 %own_kernel.1.own_ref = f32[2,320,384]{2,1,0:T(8,128)S(1)} custom-call(s32[6]{0:T(128)S(1)} %stack.39.place_ref, bf16[1280,960]{1,0:T(8,128)(2,1)S(1)} %transpose_kernel.1.weight_ref, bf16[960,384]{1,0:T(8,128)(2,1)S(1)} %get-tuple-element.39.stacked_ref), custom_call_target="tpu_custom_call" | custom-call | flops 20000000000 | bytes 20000000 | tf_op jit(solution)/shard_map/own_kernel/pallas_call | solution.py:213
  19.1 0.7 %collective-permute-done.2.mate_ref = f32[2,320,384]{2,1,0:T(8,128)S(1)} collective-permute-done((f32[2,320,384]{2,1,0:T(8,128)S(1)}, f32[2,320,384]{2,1,0:T(8,128)S(1)}, u32[]{:S(2)}, u32[]{:S(2)}) %collective-permute-start.2) | collective-permute-done | bytes 983072 | tf_op jit(solution)/shard_map/ppermute | solution.py:26
  20.4 1.9 %collective-permute-start.4 = (bf16[320,384]{1,0:T(8,128)(2,1)S(1)}, bf16[320,384]{1,0:T(8,128)(2,1)S(1)}, u32[]{:S(2)}, u32[]{:S(2)}) collective-permute-start(bf16[320,384]{1,0:T(8,128)(2,1)S(1)} %get-tuple-element.41), channel_id=1, source_target_pairs={{0,2},{2,0},{1,3},{3,1},{4,6},{6,4},{5,7},{7,5},{8,10},{10,8},{9,1... | collective-permute-start | bytes 737288 | tf_op jit(solution)/shard_map/ppermute | solution.py:30
  22.4 0.7 scaled_kernel.1.scaled_ref
  23.1 3.4 %collective-permute-start.3 = (bf16[320,384]{1,0:T(8,128)(2,1)S(1)}, bf16[320,384]{1,0:T(8,128)(2,1)S(1)}, u32[]{:S(2)}, u32[]{:S(2)}) collective-permute-start(bf16[320,384]{1,0:T(8,128)(2,1)S(1)} %scaled_kernel.1.scaled_ref), channel_id=1, source_target_pairs={{0,2},{2,0},{1,3},{3,1},{4,6},{6,4},{5,7},{7,5},{8,10},{10,8},{9,1... | collective-permute-start | bytes 737288 | tf_op jit(solution)/shard_map/ppermute | solution.py:30
  26.4 0.8 %saved_kernel.1 = (f32[320,384]{1,0:T(8,128)S(1)}, f32[8,8,128]{2,1,0:T(8,128)S(1)}) custom-call(s32[1,2]{1,0:T(1,128)S(1)} %copy-done.9, bf16[2,320,384]{2,1,0:T(8,128)(2,1)S(1)} %bitcast.19), custom_call_target="tpu_custom_call" | custom-call | flops 20000000000 | bytes 20000000 | tf_op jit(solution)/shard_map/saved_kernel/pallas_call | solution.py:213
  27.3 2.2 %collective-permute-done.4.far_ref = bf16[320,384]{1,0:T(8,128)(2,1)S(1)} collective-permute-done((bf16[320,384]{1,0:T(8,128)(2,1)S(1)}, bf16[320,384]{1,0:T(8,128)(2,1)S(1)}, u32[]{:S(2)}, u32[]{:S(2)}) %collective-permute-start.4) | collective-permute-done | bytes 245792 | tf_op jit(solution)/shard_map/ppermute | solution.py:30
  29.5 1.5 %output_kernel.1 = (bf16[320,384]{1,0:T(8,128)(2,1)}, bf16[320,384]{1,0:T(8,128)(2,1)S(1)}) custom-call(s32[6]{0:T(128)S(1)} %stack.39.place_ref, f32[320,384]{1,0:T(8,128)S(1)} %get-tuple-element.47.near_ref, bf16[320,384]{1,0:T(8,128)(2,1)S(1)} %collective-permute-done.4.far_ref, bf16[320,384]{1,0:T(8,128)(2,1)S(1)} %collective-permute-done.1.arrived_ref, ...), custom_call_target="tpu_custom_call" | custom-call | tf_op jit(solution)/shard_map/output_kernel/pallas_call | solution.py:213
  31.0 15.5 %collective-permute-start.5 = (bf16[320,384]{1,0:T(8,128)(2,1)S(1)}, bf16[320,384]{1,0:T(8,128)(2,1)S(1)}, u32[]{:S(2)}, u32[]{:S(2)}) collective-permute-start(bf16[320,384]{1,0:T(8,128)(2,1)S(1)} %get-tuple-element.52), channel_id=1, source_target_pairs={{0,508},{4,504},{8,500},{12,496},{16,492},{20,488},{24,484},{28,48... | collective-permute-start | bytes 737288 | tf_op jit(solution)/shard_map/ppermute | solution.py:307
  46.6 4.2 %collective-permute-start.6 = (bf16[160,384]{1,0:T(8,128)(2,1)S(1)}, bf16[160,384]{1,0:T(8,128)(2,1)S(1)}, u32[]{:S(2)}, u32[]{:S(2)}) collective-permute-start(bf16[160,384]{1,0:T(8,128)(2,1)S(1)} %get-tuple-element.57), channel_id=1, source_target_pairs={{0,1},{1,0},{2,3},{3,2},{4,5},{5,4},{6,7},{7,6},{8,9},{9,8},{10,11... | collective-permute-start | bytes 368648 | tf_op jit(solution)/shard_map/ppermute | solution.py:26
  50.8 1.9 %collective-permute-start.7 = (bf16[160,384]{1,0:T(8,128)(2,1)S(1)}, bf16[160,384]{1,0:T(8,128)(2,1)S(1)}, u32[]{:S(2)}, u32[]{:S(2)}) collective-permute-start(bf16[160,384]{1,0:T(8,128)(2,1)S(1)} %get-tuple-element.58), channel_id=1, source_target_pairs={{0,1},{1,0},{2,3},{3,2},{4,5},{5,4},{6,7},{7,6},{8,9},{9,8},{10,11... | collective-permute-start | bytes 368648 | tf_op jit(solution)/shard_map/ppermute | solution.py:26
  52.7 2.4 %collective-permute-start.8 = (bf16[160,384]{1,0:T(8,128)(2,1)S(1)}, bf16[160,384]{1,0:T(8,128)(2,1)S(1)}, u32[]{:S(2)}, u32[]{:S(2)}) collective-permute-start(bf16[160,384]{1,0:T(8,128)(2,1)S(1)} %get-tuple-element.59), channel_id=1, source_target_pairs={{0,1},{1,0},{2,3},{3,2},{4,5},{5,4},{6,7},{7,6},{8,9},{9,8},{10,11... | collective-permute-start | bytes 368648 | tf_op jit(solution)/shard_map/ppermute | solution.py:26
  55.1 1.9 %collective-permute-start.9 = (bf16[160,384]{1,0:T(8,128)(2,1)S(1)}, bf16[160,384]{1,0:T(8,128)(2,1)S(1)}, u32[]{:S(2)}, u32[]{:S(2)}) collective-permute-start(bf16[160,384]{1,0:T(8,128)(2,1)S(1)} %get-tuple-element.60), channel_id=1, source_target_pairs={{0,1},{1,0},{2,3},{3,2},{4,5},{5,4},{6,7},{7,6},{8,9},{9,8},{10,11... | collective-permute-start | bytes 368648 | tf_op jit(solution)/shard_map/ppermute | solution.py:26
  57.1 1.3 %collective-permute-done.9.other_high_ref = bf16[160,384]{1,0:T(8,128)(2,1)S(1)} collective-permute-done((bf16[160,384]{1,0:T(8,128)(2,1)S(1)}, bf16[160,384]{1,0:T(8,128)(2,1)S(1)}, u32[]{:S(2)}, u32[]{:S(2)}) %collective-permute-start.9) | collective-permute-done | bytes 122912 | tf_op jit(solution)/shard_map/ppermute | solution.py:26
  58.4 3.2 %gradient_kernel.1 = bf16[320,384]{1,0:T(8,128)(2,1)} custom-call(s32[6]{0:T(128)S(1)} %stack.39.place_ref, f32[320,384]{1,0:T(8,128)S(1)} %get-tuple-element.53.normed_ref, f32[8,8,128]{2,1,0:T(8,128)S(1)} %get-tuple-element.54.factor_ref, bf16[320,384]{1,0:T(8,128)(2,1)S(1)} %collective-permute-done.returned_ref, bf16[320,384]{1,0:T(8,128)(2,1)S(1)} %copy-done.2, ...), custom_call_target="tpu_custom_call" | custom-call | tf_op jit(solution)/shard_map/gradient_kernel/pallas_call | solution.py:213
  61.6 5.0 %collective-permute-done.5 = bf16[320,384]{1,0:T(8,128)(2,1)S(1)} collective-permute-done((bf16[320,384]{1,0:T(8,128)(2,1)S(1)}, bf16[320,384]{1,0:T(8,128)(2,1)S(1)}, u32[]{:S(2)}, u32[]{:S(2)}) %collective-permute-start.5) | collective-permute-done | bytes 245792 | tf_op jit(solution)/shard_map/ppermute | solution.py:307
  66.6 0.7 %copy.14 = bf16[1,320,384]{2,1,0:T(8,128)(2,1)} copy(bf16[1,320,384]{2,1,0:T(8,128)(2,1)S(1)} %bitcast.20) | data formatting | bytes 491520
  (28 shorter events, 1.1 us)
Async XLA Ops:
  0.6 10.7 %collective-permute-start.1 = (bf16[320,384]{1,0:T(8,128)(2,1)}, bf16[320,384]{1,0:T(8,128)(2,1)S(1)}, u32[]{:S(2)}, u32[]{:S(2)}) collective-permute-start(bf16[320,384]{1,0:T(8,128)(2,1)} %bitcast.22), channel_id=1, source_target_pairs={{0,4},{4,8},{8,12},{12,16},{16,20},{20,24},{24,28},{28,32},{32,36}... | collective-permute-start | bytes 737288 | tf_op jit(solution)/shard_map/ppermute | solution.py:22
  6.3 1.7 %copy-start = (bf16[1,3,320,1280]{3,2,1,0:T(8,128)(2,1)S(1)}, bf16[1,3,320,1280]{3,2,1,0:T(8,128)(2,1)}, u32[]{:S(2)}) copy-start(bf16[1,3,320,1280]{3,2,1,0:T(8,128)(2,1)} %param.16) | copy-start | bytes 7372804
  8.0 1.0 %copy-start.5 = (bf16[1,2,320,384]{3,2,1,0:T(8,128)(2,1)S(1)}, bf16[1,2,320,384]{3,2,1,0:T(8,128)(2,1)}, u32[]{:S(2)}) copy-start(bf16[1,2,320,384]{3,2,1,0:T(8,128)(2,1)} %param.15) | copy-start | bytes 1474564
  8.0 1.0 %copy-start.7 = (f32[25,320]{1,0:T(8,128)S(1)}, f32[25,320]{1,0:T(8,128)}, u32[]{:S(2)}) copy-start(f32[25,320]{1,0:T(8,128)} %gain_ref) | copy-start | bytes 96004
  8.0 1.0 %copy-start.8 = (s32[1,2]{1,0:T(1,128)S(1)}, s32[1,2]{1,0:T(1,128)}, u32[]{:S(2)}) copy-start(s32[1,2]{1,0:T(1,128)} %stamps_ref.1) | copy-start | bytes 28
  8.0 1.0 %copy-start.9 = (s32[1,2]{1,0:T(1,128)S(1)}, s32[1,2]{1,0:T(1,128)}, u32[]{:S(2)}) copy-start(s32[1,2]{1,0:T(1,128)} %plan_ref.3) | copy-start | bytes 28
  9.1 0.9 %copy-start.4 = (bf16[1,320,384]{2,1,0:T(8,128)(2,1)S(1)}, bf16[1,320,384]{2,1,0:T(8,128)(2,1)}, u32[]{:S(2)}) copy-start(bf16[1,320,384]{2,1,0:T(8,128)(2,1)} %param.11) | copy-start | bytes 737284
  9.1 2.2 %copy-start.3 = (bf16[320,384]{1,0:T(8,128)(2,1)S(1)}, bf16[320,384]{1,0:T(8,128)(2,1)}, u32[]{:S(2)}) copy-start(bf16[320,384]{1,0:T(8,128)(2,1)} %entry_ref.3) | copy-start | bytes 737284
  10.0 12.4 %collective-permute-start = (bf16[320,384]{1,0:T(8,128)(2,1)S(1)}, bf16[320,384]{1,0:T(8,128)(2,1)S(1)}, u32[]{:S(2)}, u32[]{:S(2)}) collective-permute-start(bf16[320,384]{1,0:T(8,128)(2,1)S(1)} %bitcast.16), channel_id=1, source_target_pairs={{4,0},{8,4},{12,8},{16,12},{20,16},{24,20},{28,24},{32,28},{36,32}... | collective-permute-start | bytes 737288 | tf_op jit(solution)/shard_map/ppermute | solution.py:22
  13.2 6.6 %collective-permute-start.2 = (f32[2,320,384]{2,1,0:T(8,128)S(1)}, f32[2,320,384]{2,1,0:T(8,128)S(1)}, u32[]{:S(2)}, u32[]{:S(2)}) collective-permute-start(f32[2,320,384]{2,1,0:T(8,128)S(1)} %get-tuple-element.40), channel_id=1, source_target_pairs={{0,1},{1,0},{2,3},{3,2},{4,5},{5,4},{6,7},{7,6},{8,9},{9,8},{10,11... | collective-permute-start | bytes 2949128 | tf_op jit(solution)/shard_map/ppermute | solution.py:26
  17.6 4.8 %copy-start.2 = (bf16[320,384]{1,0:T(8,128)(2,1)S(1)}, bf16[320,384]{1,0:T(8,128)(2,1)}, u32[]{:S(2)}) copy-start(bf16[320,384]{1,0:T(8,128)(2,1)} %reward_ref.5) | copy-start | bytes 737284
  19.0 7.4 %copy-start.6 = (bf16[1,2,320,384]{3,2,1,0:T(8,128)(2,1)S(1)}, bf16[1,2,320,384]{3,2,1,0:T(8,128)(2,1)}, u32[]{:S(2)}) copy-start(bf16[1,2,320,384]{3,2,1,0:T(8,128)(2,1)} %param.14) | copy-start | bytes 1474564
  20.4 9.1 %collective-permute-start.4 = (bf16[320,384]{1,0:T(8,128)(2,1)S(1)}, bf16[320,384]{1,0:T(8,128)(2,1)S(1)}, u32[]{:S(2)}, u32[]{:S(2)}) collective-permute-start(bf16[320,384]{1,0:T(8,128)(2,1)S(1)} %get-tuple-element.41), channel_id=1, source_target_pairs={{0,2},{2,0},{1,3},{3,1},{4,6},{6,4},{5,7},{7,5},{8,10},{10,8},{9,1... | collective-permute-start | bytes 737288 | tf_op jit(solution)/shard_map/ppermute | solution.py:30
  23.1 23.5 %collective-permute-start.3 = (bf16[320,384]{1,0:T(8,128)(2,1)S(1)}, bf16[320,384]{1,0:T(8,128)(2,1)S(1)}, u32[]{:S(2)}, u32[]{:S(2)}) collective-permute-start(bf16[320,384]{1,0:T(8,128)(2,1)S(1)} %scaled_kernel.1.scaled_ref), channel_id=1, source_target_pairs={{0,2},{2,0},{1,3},{3,1},{4,6},{6,4},{5,7},{7,5},{8,10},{10,8},{9,1... | collective-permute-start | bytes 737288 | tf_op jit(solution)/shard_map/ppermute | solution.py:30
  27.3 31.1 %copy-start.1 = (bf16[1,3,320,1280]{3,2,1,0:T(8,128)(2,1)S(1)}, bf16[1,3,320,1280]{3,2,1,0:T(8,128)(2,1)}, u32[]{:S(2)}) copy-start(bf16[1,3,320,1280]{3,2,1,0:T(8,128)(2,1)} %param.16) | copy-start | bytes 7372804
  31.0 35.6 %collective-permute-start.5 = (bf16[320,384]{1,0:T(8,128)(2,1)S(1)}, bf16[320,384]{1,0:T(8,128)(2,1)S(1)}, u32[]{:S(2)}, u32[]{:S(2)}) collective-permute-start(bf16[320,384]{1,0:T(8,128)(2,1)S(1)} %get-tuple-element.52), channel_id=1, source_target_pairs={{0,508},{4,504},{8,500},{12,496},{16,492},{20,488},{24,484},{28,48... | collective-permute-start | bytes 737288 | tf_op jit(solution)/shard_map/ppermute | solution.py:307
  46.6 10.5 %collective-permute-start.6 = (bf16[160,384]{1,0:T(8,128)(2,1)S(1)}, bf16[160,384]{1,0:T(8,128)(2,1)S(1)}, u32[]{:S(2)}, u32[]{:S(2)}) collective-permute-start(bf16[160,384]{1,0:T(8,128)(2,1)S(1)} %get-tuple-element.57), channel_id=1, source_target_pairs={{0,1},{1,0},{2,3},{3,2},{4,5},{5,4},{6,7},{7,6},{8,9},{9,8},{10,11... | collective-permute-start | bytes 368648 | tf_op jit(solution)/shard_map/ppermute | solution.py:26
  50.8 6.3 %collective-permute-start.7 = (bf16[160,384]{1,0:T(8,128)(2,1)S(1)}, bf16[160,384]{1,0:T(8,128)(2,1)S(1)}, u32[]{:S(2)}, u32[]{:S(2)}) collective-permute-start(bf16[160,384]{1,0:T(8,128)(2,1)S(1)} %get-tuple-element.58), channel_id=1, source_target_pairs={{0,1},{1,0},{2,3},{3,2},{4,5},{5,4},{6,7},{7,6},{8,9},{9,8},{10,11... | collective-permute-start | bytes 368648 | tf_op jit(solution)/shard_map/ppermute | solution.py:26
  52.7 4.4 %collective-permute-start.8 = (bf16[160,384]{1,0:T(8,128)(2,1)S(1)}, bf16[160,384]{1,0:T(8,128)(2,1)S(1)}, u32[]{:S(2)}, u32[]{:S(2)}) collective-permute-start(bf16[160,384]{1,0:T(8,128)(2,1)S(1)} %get-tuple-element.59), channel_id=1, source_target_pairs={{0,1},{1,0},{2,3},{3,2},{4,5},{5,4},{6,7},{7,6},{8,9},{9,8},{10,11... | collective-permute-start | bytes 368648 | tf_op jit(solution)/shard_map/ppermute | solution.py:26
  55.1 3.2 %collective-permute-start.9 = (bf16[160,384]{1,0:T(8,128)(2,1)S(1)}, bf16[160,384]{1,0:T(8,128)(2,1)S(1)}, u32[]{:S(2)}, u32[]{:S(2)}) collective-permute-start(bf16[160,384]{1,0:T(8,128)(2,1)S(1)} %get-tuple-element.60), channel_id=1, source_target_pairs={{0,1},{1,0},{2,3},{3,2},{4,5},{5,4},{6,7},{7,6},{8,9},{9,8},{10,11... | collective-permute-start | bytes 368648 | tf_op jit(solution)/shard_map/ppermute | solution.py:26

commit v8 on v7

--- a/solution.py
+++ b/solution.py
@@ -117,41 +117,65 @@
 
 def scaled_kernel(place_ref, returned_ref, reward_ref, extra_ref, columns_ref, scaled_ref):
     cot_total = cotangent(place_ref, returned_ref, reward_ref, extra_ref)
-    scaled_ref[...] = (cot_total * columns_ref[1][:, :1]).astype(jnp.bfloat16)
-
-
-def halves_kernel(place_ref, own_ref, mate_ref, near_ref, far_ref):
-    chip = place_ref[2]
-    near_ref[...] = own_ref[chip] + mate_ref[chip]
-    far_ref[...] = (own_ref[1 - chip] + mate_ref[1 - chip]).astype(jnp.bfloat16)
-
-
-def output_kernel(
+    scaled_ref[...] = gained(cot_total, columns_ref, 1).astype(jnp.bfloat16)
+
+
+def halves_kernel(place_ref, own_ref, mate_ref, far_ref):
+    chip = 1 - place_ref[2]
+    far_ref[...] = (own_ref[chip] + mate_ref[chip]).astype(jnp.bfloat16)
+
+
+def gained(values, columns_ref, way):
+    size = columns_ref.shape[2]
+    return jnp.concatenate(
+        [
+            values[:, start : start + size] * columns_ref[way]
+            for start in range(0, values.shape[1], size)
+        ],
+        1,
+    )
+
+
+def near_kernel(
     place_ref,
-    near_ref,
-    far_ref,
+    plan_ref,
+    own_ref,
+    mate_ref,
     arrived_ref,
     entry_ref,
     added_ref,
     columns_ref,
-    cot_ref,
-    reward_ref,
-    out_ref,
-    sent_ref,
+    stored_ref,
+    near_ref,
+    normed_ref,
+    factor_ref,
 ):
+    chip = place_ref[2]
     x_in = jnp.where(place_ref[0] == 0, entry_ref[...], arrived_ref[...]).astype(jnp.float32)
-    conv_sum = near_ref[...] + far_ref[...].astype(jnp.float32)
-    act_out = x_in + conv_sum * columns_ref[0][:, :1] + added_ref[...].astype(jnp.float32)
-    act_out = act_out.astype(jnp.bfloat16)
-    out_ref[...] = act_out
-    cot_in = jnp.where(place_ref[5] == 1, reward_ref[...], cot_ref[...])
-    sent_ref[...] = jnp.where(place_ref[4] == 1, act_out, cot_in)
-
-
-def saved_kernel(plan_ref, stored_ref, normed_ref, factor_ref):
+    near = gained(own_ref[chip] + mate_ref[chip], columns_ref, 0)
+    near_ref[...] = x_in + near + added_ref[...].astype(jnp.float32)
     normed, factor = normalize(stored_ref[plan_ref[0, 1]].astype(jnp.float32))
     normed_ref[...] = normed
     factor_ref[...] = jnp.broadcast_to(factor, factor_ref.shape)
+
+
+def output_kernel(near_ref, far_ref, columns_ref, out_ref):
+    far = gained(far_ref[...].astype(jnp.float32), columns_ref, 0)
+    out_ref[...] = (near_ref[...] + far).astype(jnp.bfloat16)
+
+
+def sent_kernel(place_ref, near_ref, far_ref, columns_ref, cot_ref, reward_ref, sent_ref):
+    @pl.when(place_ref[4] == 1)
+    def _():
+        output_kernel(near_ref, far_ref, columns_ref, sent_ref)
+
+    @pl.when(place_ref[5] == 1)
+    def _():
+        sent_ref[...] = reward_ref[...]
+
+    @pl.when(place_ref[4] + place_ref[5] == 0)
+    def _():
+        sent_ref[...] = cot_ref[...]
 
 
 def split_kernel(scaled_ref, other_ref, *part_refs):
@@ -271,14 +295,18 @@
     )
     mate_part = swap_core(mate_side)
     (own,) = call(own_kernel, [pair], [SMEM, VMEM, VMEM], [place, turned, stacked], cost=20.0)
-    near, far_side = call(
-        halves_kernel,
-        [((rows, cells), jnp.float32), field],
-        [SMEM, VMEM, VMEM],
-        [place, own, mate_part],
-    )
+    (far_side,) = call(halves_kernel, [field], [SMEM, VMEM, VMEM], [place, own, mate_part])
     far = swap_chip(far_side)
-    returned, far_side = lax.optimization_barrier((returned, far_side))
+    stored, far_side = lax.optimization_barrier((stored, far_side))
+    whole = ((rows, cells), jnp.float32)
+    near, saved_normed, saved_factor = call(
+        near_kernel,
+        [whole, whole, ((rows // WIDTH, 8, 128), jnp.float32)],
+        [SMEM] * 2 + [VMEM] * 7,
+        [place, plan, own, mate_part, arrived, entry_latent, added, gains, stored],
+        cost=20.0,
+    )
+    returned, near = lax.optimization_barrier((returned, near))
     (scaled,) = call(
         scaled_kernel,
         [field],
@@ -286,27 +314,20 @@
         [place, returned, reward_head, extra, gains],
     )
     other = swap_chip(scaled)
-    stored, far_side = lax.optimization_barrier((stored, far_side))
-    saved_normed, saved_factor = call(
-        saved_kernel,
-        [((rows, cells), jnp.float32), ((rows // WIDTH, 8, 128), jnp.float32)],
-        [SMEM, VMEM],
-        [plan, stored],
-        cost=20.0,
-    )
-    far, scaled, saved_normed = lax.optimization_barrier((far, scaled, saved_normed))
-    act_out, sent = call(
-        output_kernel,
-        [field, field],
-        [SMEM] + [VMEM] * 8,
-        [place, near, far, arrived, entry_latent, added, gains, cot_carried[0], reward_head],
+    far, scaled = lax.optimization_barrier((far, scaled))
+    (sent,) = call(
+        sent_kernel,
+        [field],
+        [SMEM] + [VMEM] * 5,
+        [place, near, far, gains, cot_carried[0], reward_head],
     )
     half = sections // 2
     route = [(s, sections - 1 - s) for s in range(half)]
     route += [(s, (sections - s) % half) for s in range(half, sections)]
     mirror_in = lax.ppermute(sent, "section", route)
 
-    other, scaled, act_out = lax.optimization_barrier((other, scaled, act_out))
+    other, scaled, near, sent = lax.optimization_barrier((other, scaled, near, sent))
+    (act_out,) = call(output_kernel, [field], [VMEM] * 3, [near, far, gains])
     parts = call(
         split_kernel,
         [((rows // 2, cells), jnp.bfloat16)] * 4,

time: 67.7 us -> 66.8 us (0.987)
  waiting for transfers between devices: 9.28 us -> 8.58 us
    ppermute x5, waiting for transfers between devices: 2.03 us -> 1.29 us  [swap_core(): return lax.ppermute(block, 'ch', [(0, 1), (1, 0), (2, 3), (3, 2)])]
    pallas_call x10 -> x11, Pallas kernels: 11.7 us -> 11.7 us  [call(): pl.pallas_call(kernel, out_shape=[jax.ShapeDtypeStruct(shape, kind) for s...]
  transfers between devices with their start and end apart: 10 -> 10, of which waited for: 4 -> 4; matrix products, arithmetic and copies ran while one was open for 0% -> 0% of each run, Pallas kernels for 17% -> 18%
where the time goes in v8:
time: 66.8 us; the launch traced here: 66.3 us
  starting transfers between devices  42.4 us (63%)
  Pallas kernels  11.7 us (18%)
  waiting for transfers between devices  8.58 us (13%)
  local copies, waits for them, and re-layouts  2.79 us (4%)
  between operations  0.92 us (1%)
    ppermute x1, starting transfers between devices, local(): mirror_in = lax.ppermute(sent, 'section', route)  15.5 us
    ppermute x5, starting transfers between devices, swap_core(): return lax.ppermute(block, 'ch', [(0, 1), (1, 0), (2, 3), (3, 2)])  14.5 us
    pallas_call x11, Pallas kernels, call(): pl.pallas_call(kernel, out_shape=[jax.ShapeDtypeStruct(shape, kind) for s...  11.7 us
    ppermute x2, starting transfers between devices, shifted(): return lax.ppermute(block, axis, route)  6.94 us
    ppermute x2, starting transfers between devices, swap_chip(): return lax.ppermute(block, 'ch', [(0, 2), (2, 0), (1, 3), (3, 1)])  5.41 us
    ppermute x1, waiting for transfers between devices, local(): mirror_in = lax.ppermute(sent, 'section', route)  5.32 us
    unnamed x21, local copies, waits for them, and re-layouts  2.7 us
    ppermute x2, waiting for transfers between devices, swap_chip(): return lax.ppermute(block, 'ch', [(0, 2), (2, 0), (1, 3), (3, 1)])  1.96 us
  transfers between devices with their start and end apart: 10, of which 4 were waited for; matrix products, arithmetic and copies ran while one was open for 0% of the time, Pallas kernels for 18%

profile of v8, /device:TPU:1, one launch (start us, length us, event | category | flops | bytes accessed | tf_op | source)
XLA Modules:
  0.0 66.3 jit_solution(11089760731564034240)
XLA Ops:
  0.6 5.7 %collective-permute-start.1 = (bf16[320,384]{1,0:T(8,128)(2,1)}, bf16[320,384]{1,0:T(8,128)(2,1)S(1)}, u32[]{:S(2)}, u32[]{:S(2)}) collective-permute-start(bf16[320,384]{1,0:T(8,128)(2,1)} %bitcast.23), channel_id=1, source_target_pairs={{0,4},{4,8},{8,12},{12,16},{16,20},{20,24},{24,28},{28,32},{32,36}... | collective-permute-start | bytes 737288 | tf_op jit(solution)/shard_map/ppermute | solution.py:22
  6.3 1.7 %copy-done = bf16[1,3,320,1280]{3,2,1,0:T(8,128)(2,1)S(1)} copy-done((bf16[1,3,320,1280]{3,2,1,0:T(8,128)(2,1)S(1)}, bf16[1,3,320,1280]{3,2,1,0:T(8,128)(2,1)}, u32[]{:S(2)}) %copy-start) | copy-done | bytes 2457624
  8.0 0.8 %transpose_kernel.1.weight_ref = bf16[1280,960]{1,0:T(8,128)(2,1)S(1)} custom-call(bf16[960,1280]{1,0:T(8,128)(2,1)S(1)} %bitcast.14), custom_call_target="tpu_custom_call" | custom-call | flops 20000000000 | bytes 20000000 | tf_op jit(solution)/shard_map/transpose_kernel/pallas_call | solution.py:237
  9.1 0.7 %prepare_kernel.1 = (f32[2,320,128]{2,1,0:T(8,128)S(1)}, bf16[320,384]{1,0:T(8,128)(2,1)S(1)}, bf16[320,384]{1,0:T(8,128)(2,1)S(1)}) custom-call(s32[6]{0:T(128)S(1)} %stack.39.place_ref, s32[1,2]{1,0:T(1,128)S(1)} %copy-done.9, s32[1,2]{1,0:T(1,128)S(1)} %copy-done.8, bf16[2,320,384]{2,1,0:T(8,128)(2,1)S(1)} %bitcast.18, f32[25,320]{1,0:T(8,128)S(1)} %copy-done.7), custom_call_target="tpu_custom_call" | custom-call | flops 20000000000 | bytes 20000000 | tf_op jit(solution)/shard_map/prepare_kernel/pallas_call | solution.py:237
  10.0 1.3 %collective-permute-start = (bf16[320,384]{1,0:T(8,128)(2,1)S(1)}, bf16[320,384]{1,0:T(8,128)(2,1)S(1)}, u32[]{:S(2)}, u32[]{:S(2)}) collective-permute-start(bf16[320,384]{1,0:T(8,128)(2,1)S(1)} %bitcast.16), channel_id=1, source_target_pairs={{4,0},{8,4},{12,8},{16,12},{20,16},{24,20},{28,24},{32,28},{36,32}... | collective-permute-start | bytes 737288 | tf_op jit(solution)/shard_map/ppermute | solution.py:22
  11.3 1.9 %forward_kernel.1 = (f32[2,320,384]{2,1,0:T(8,128)S(1)}, bf16[960,384]{1,0:T(8,128)(2,1)S(1)}) custom-call(s32[6]{0:T(128)S(1)} %stack.39.place_ref, bf16[320,384]{1,0:T(8,128)(2,1)S(1)} %collective-permute-done.1.arrived_ref, bf16[320,384]{1,0:T(8,128)(2,1)S(1)} %copy-done.3, bf16[1280,960]{1,0:T(8,128)(2,1)S(1)} %transpose_kernel.1.weight_ref), custom_call_target="tpu_custom_call" | custom-call | tf_op jit(solution)/shard_map/forward_kernel/pallas_call | solution.py:237
  13.2 4.4 %collective-permute-start.2 = (f32[2,320,384]{2,1,0:T(8,128)S(1)}, f32[2,320,384]{2,1,0:T(8,128)S(1)}, u32[]{:S(2)}, u32[]{:S(2)}) collective-permute-start(f32[2,320,384]{2,1,0:T(8,128)S(1)} %get-tuple-element.38), channel_id=1, source_target_pairs={{0,1},{1,0},{2,3},{3,2},{4,5},{5,4},{6,7},{7,6},{8,9},{9,8},{10,11... | collective-permute-start | bytes 2949128 | tf_op jit(solution)/shard_map/ppermute | solution.py:26
  17.6 1.4 %own_kernel.1.own_ref = f32[2,320,384]{2,1,0:T(8,128)S(1)} custom-call(s32[6]{0:T(128)S(1)} %stack.39.place_ref, bf16[1280,960]{1,0:T(8,128)(2,1)S(1)} %transpose_kernel.1.weight_ref, bf16[960,384]{1,0:T(8,128)(2,1)S(1)} %get-tuple-element.37.stacked_ref), custom_call_target="tpu_custom_call" | custom-call | flops 20000000000 | bytes 20000000 | tf_op jit(solution)/shard_map/own_kernel/pallas_call | solution.py:237
  19.0 0.8 %collective-permute-done.2.mate_ref = f32[2,320,384]{2,1,0:T(8,128)S(1)} collective-permute-done((f32[2,320,384]{2,1,0:T(8,128)S(1)}, f32[2,320,384]{2,1,0:T(8,128)S(1)}, u32[]{:S(2)}, u32[]{:S(2)}) %collective-permute-start.2) | collective-permute-done | bytes 983072 | tf_op jit(solution)/shard_map/ppermute | solution.py:26
  20.4 1.9 %collective-permute-start.4 = (bf16[320,384]{1,0:T(8,128)(2,1)S(1)}, bf16[320,384]{1,0:T(8,128)(2,1)S(1)}, u32[]{:S(2)}, u32[]{:S(2)}) collective-permute-start(bf16[320,384]{1,0:T(8,128)(2,1)S(1)} %halves_kernel.1), channel_id=1, source_target_pairs={{0,2},{2,0},{1,3},{3,1},{4,6},{6,4},{5,7},{7,5},{8,10},{10,8},{9,1... | collective-permute-start | bytes 737288 | tf_op jit(solution)/shard_map/ppermute | solution.py:30
  22.3 1.0 %near_kernel.1 = (f32[320,384]{1,0:T(8,128)S(1)}, f32[320,384]{1,0:T(8,128)S(1)}, f32[8,8,128]{2,1,0:T(8,128)S(1)}) custom-call(s32[6]{0:T(128)S(1)} %stack.39.place_ref, s32[1,2]{1,0:T(1,128)S(1)} %copy-done.9, f32[2,320,384]{2,1,0:T(8,128)S(1)} %own_kernel.1.own_ref, f32[2,320,384]{2,1,0:T(8,128)S(1)} %collective-permute-done.2.mate_ref, ...), custom_call_target="tpu_custom_call" | custom-call | flops 20000000000 | bytes 20000000 | tf_op jit(solution)/shard_map/near_kernel/pallas_call | solution.py:237
  23.4 0.6 scaled_kernel.1.scaled_ref
  24.0 3.5 %collective-permute-start.3 = (bf16[320,384]{1,0:T(8,128)(2,1)S(1)}, bf16[320,384]{1,0:T(8,128)(2,1)S(1)}, u32[]{:S(2)}, u32[]{:S(2)}) collective-permute-start(bf16[320,384]{1,0:T(8,128)(2,1)S(1)} %scaled_kernel.1.scaled_ref), channel_id=1, source_target_pairs={{0,2},{2,0},{1,3},{3,1},{4,6},{6,4},{5,7},{7,5},{8,10},{10,8},{9,1... | collective-permute-start | bytes 737288 | tf_op jit(solution)/shard_map/ppermute | solution.py:30
  27.5 2.0 %collective-permute-done.4.far_ref = bf16[320,384]{1,0:T(8,128)(2,1)S(1)} collective-permute-done((bf16[320,384]{1,0:T(8,128)(2,1)S(1)}, bf16[320,384]{1,0:T(8,128)(2,1)S(1)}, u32[]{:S(2)}, u32[]{:S(2)}) %collective-permute-start.4) | collective-permute-done | bytes 245792 | tf_op jit(solution)/shard_map/ppermute | solution.py:30
  29.5 0.6 sent_kernel.1
  30.1 15.5 %collective-permute-start.5 = (bf16[320,384]{1,0:T(8,128)(2,1)S(1)}, bf16[320,384]{1,0:T(8,128)(2,1)S(1)}, u32[]{:S(2)}, u32[]{:S(2)}) collective-permute-start(bf16[320,384]{1,0:T(8,128)(2,1)S(1)} %sent_kernel.1), channel_id=1, source_target_pairs={{0,508},{4,504},{8,500},{12,496},{16,492},{20,488},{24,484},{28,48... | collective-permute-start | bytes 737288 | tf_op jit(solution)/shard_map/ppermute | solution.py:327
  45.7 3.9 %collective-permute-start.6 = (bf16[160,384]{1,0:T(8,128)(2,1)S(1)}, bf16[160,384]{1,0:T(8,128)(2,1)S(1)}, u32[]{:S(2)}, u32[]{:S(2)}) collective-permute-start(bf16[160,384]{1,0:T(8,128)(2,1)S(1)} %get-tuple-element.53), channel_id=1, source_target_pairs={{0,1},{1,0},{2,3},{3,2},{4,5},{5,4},{6,7},{7,6},{8,9},{9,8},{10,11... | collective-permute-start | bytes 368648 | tf_op jit(solution)/shard_map/ppermute | solution.py:26
  49.5 1.9 %collective-permute-start.7 = (bf16[160,384]{1,0:T(8,128)(2,1)S(1)}, bf16[160,384]{1,0:T(8,128)(2,1)S(1)}, u32[]{:S(2)}, u32[]{:S(2)}) collective-permute-start(bf16[160,384]{1,0:T(8,128)(2,1)S(1)} %get-tuple-element.54), channel_id=1, source_target_pairs={{0,1},{1,0},{2,3},{3,2},{4,5},{5,4},{6,7},{7,6},{8,9},{9,8},{10,11... | collective-permute-start | bytes 368648 | tf_op jit(solution)/shard_map/ppermute | solution.py:26
  51.5 2.4 %collective-permute-start.8 = (bf16[160,384]{1,0:T(8,128)(2,1)S(1)}, bf16[160,384]{1,0:T(8,128)(2,1)S(1)}, u32[]{:S(2)}, u32[]{:S(2)}) collective-permute-start(bf16[160,384]{1,0:T(8,128)(2,1)S(1)} %get-tuple-element.55), channel_id=1, source_target_pairs={{0,1},{1,0},{2,3},{3,2},{4,5},{5,4},{6,7},{7,6},{8,9},{9,8},{10,11... | collective-permute-start | bytes 368648 | tf_op jit(solution)/shard_map/ppermute | solution.py:26
  53.9 1.9 %collective-permute-start.9 = (bf16[160,384]{1,0:T(8,128)(2,1)S(1)}, bf16[160,384]{1,0:T(8,128)(2,1)S(1)}, u32[]{:S(2)}, u32[]{:S(2)}) collective-permute-start(bf16[160,384]{1,0:T(8,128)(2,1)S(1)} %get-tuple-element.56), channel_id=1, source_target_pairs={{0,1},{1,0},{2,3},{3,2},{4,5},{5,4},{6,7},{7,6},{8,9},{9,8},{10,11... | collective-permute-start | bytes 368648 | tf_op jit(solution)/shard_map/ppermute | solution.py:26
  55.8 0.8 %output_kernel.1 = bf16[320,384]{1,0:T(8,128)(2,1)} custom-call(f32[320,384]{1,0:T(8,128)S(1)} %get-tuple-element.48.near_ref, bf16[320,384]{1,0:T(8,128)(2,1)S(1)} %collective-permute-done.4.far_ref, f32[2,320,128]{2,1,0:T(8,128)S(1)} %get-tuple-element.40.columns_ref), custom_call_target="tpu_custom_call" | custom-call | tf_op jit(solution)/shard_map/output_kernel/pallas_call | solution.py:237
  57.1 3.2 %gradient_kernel.1 = bf16[320,384]{1,0:T(8,128)(2,1)} custom-call(s32[6]{0:T(128)S(1)} %stack.39.place_ref, f32[320,384]{1,0:T(8,128)S(1)} %get-tuple-element.49.normed_ref, f32[8,8,128]{2,1,0:T(8,128)S(1)} %get-tuple-element.50.factor_ref, bf16[320,384]{1,0:T(8,128)(2,1)S(1)} %collective-permute-done.returned_ref, bf16[320,384]{1,0:T(8,128)(2,1)S(1)} %copy-done.2, ...), custom_call_target="tpu_custom_call" | custom-call | tf_op jit(solution)/shard_map/gradient_kernel/pallas_call | solution.py:237
  60.3 5.3 %collective-permute-done.5 = bf16[320,384]{1,0:T(8,128)(2,1)S(1)} collective-permute-done((bf16[320,384]{1,0:T(8,128)(2,1)S(1)}, bf16[320,384]{1,0:T(8,128)(2,1)S(1)}, u32[]{:S(2)}, u32[]{:S(2)}) %collective-permute-start.5) | collective-permute-done | bytes 245792 | tf_op jit(solution)/shard_map/ppermute | solution.py:327
  65.7 0.7 %copy.14 = bf16[1,320,384]{2,1,0:T(8,128)(2,1)} copy(bf16[1,320,384]{2,1,0:T(8,128)(2,1)S(1)} %bitcast.21) | data formatting | bytes 491520
  (29 shorter events, 1.6 us)
Async XLA Ops:
  0.6 10.7 %collective-permute-start.1 = (bf16[320,384]{1,0:T(8,128)(2,1)}, bf16[320,384]{1,0:T(8,128)(2,1)S(1)}, u32[]{:S(2)}, u32[]{:S(2)}) collective-permute-start(bf16[320,384]{1,0:T(8,128)(2,1)} %bitcast.23), channel_id=1, source_target_pairs={{0,4},{4,8},{8,12},{12,16},{16,20},{20,24},{24,28},{28,32},{32,36}... | collective-permute-start | bytes 737288 | tf_op jit(solution)/shard_map/ppermute | solution.py:22
  6.3 1.7 %copy-start = (bf16[1,3,320,1280]{3,2,1,0:T(8,128)(2,1)S(1)}, bf16[1,3,320,1280]{3,2,1,0:T(8,128)(2,1)}, u32[]{:S(2)}) copy-start(bf16[1,3,320,1280]{3,2,1,0:T(8,128)(2,1)} %param.16) | copy-start | bytes 7372804
  8.0 1.0 %copy-start.5 = (bf16[1,2,320,384]{3,2,1,0:T(8,128)(2,1)S(1)}, bf16[1,2,320,384]{3,2,1,0:T(8,128)(2,1)}, u32[]{:S(2)}) copy-start(bf16[1,2,320,384]{3,2,1,0:T(8,128)(2,1)} %param.15) | copy-start | bytes 1474564
  8.0 1.0 %copy-start.7 = (f32[25,320]{1,0:T(8,128)S(1)}, f32[25,320]{1,0:T(8,128)}, u32[]{:S(2)}) copy-start(f32[25,320]{1,0:T(8,128)} %gain_ref) | copy-start | bytes 96004
  8.0 1.0 %copy-start.8 = (s32[1,2]{1,0:T(1,128)S(1)}, s32[1,2]{1,0:T(1,128)}, u32[]{:S(2)}) copy-start(s32[1,2]{1,0:T(1,128)} %stamps_ref.1) | copy-start | bytes 28
  8.0 1.0 %copy-start.9 = (s32[1,2]{1,0:T(1,128)S(1)}, s32[1,2]{1,0:T(1,128)}, u32[]{:S(2)}) copy-start(s32[1,2]{1,0:T(1,128)} %plan_ref.3) | copy-start | bytes 28
  9.1 0.9 %copy-start.4 = (bf16[1,320,384]{2,1,0:T(8,128)(2,1)S(1)}, bf16[1,320,384]{2,1,0:T(8,128)(2,1)}, u32[]{:S(2)}) copy-start(bf16[1,320,384]{2,1,0:T(8,128)(2,1)} %param.11) | copy-start | bytes 737284
  9.1 2.2 %copy-start.3 = (bf16[320,384]{1,0:T(8,128)(2,1)S(1)}, bf16[320,384]{1,0:T(8,128)(2,1)}, u32[]{:S(2)}) copy-start(bf16[320,384]{1,0:T(8,128)(2,1)} %entry_ref.3) | copy-start | bytes 737284
  10.0 13.3 %collective-permute-start = (bf16[320,384]{1,0:T(8,128)(2,1)S(1)}, bf16[320,384]{1,0:T(8,128)(2,1)S(1)}, u32[]{:S(2)}, u32[]{:S(2)}) collective-permute-start(bf16[320,384]{1,0:T(8,128)(2,1)S(1)} %bitcast.16), channel_id=1, source_target_pairs={{4,0},{8,4},{12,8},{16,12},{20,16},{24,20},{28,24},{32,28},{36,32}... | collective-permute-start | bytes 737288 | tf_op jit(solution)/shard_map/ppermute | solution.py:22
  13.2 6.6 %collective-permute-start.2 = (f32[2,320,384]{2,1,0:T(8,128)S(1)}, f32[2,320,384]{2,1,0:T(8,128)S(1)}, u32[]{:S(2)}, u32[]{:S(2)}) collective-permute-start(f32[2,320,384]{2,1,0:T(8,128)S(1)} %get-tuple-element.38), channel_id=1, source_target_pairs={{0,1},{1,0},{2,3},{3,2},{4,5},{5,4},{6,7},{7,6},{8,9},{9,8},{10,11... | collective-permute-start | bytes 2949128 | tf_op jit(solution)/shard_map/ppermute | solution.py:26
  17.6 4.7 %copy-start.6 = (bf16[1,2,320,384]{3,2,1,0:T(8,128)(2,1)S(1)}, bf16[1,2,320,384]{3,2,1,0:T(8,128)(2,1)}, u32[]{:S(2)}) copy-start(bf16[1,2,320,384]{3,2,1,0:T(8,128)(2,1)} %param.14) | copy-start | bytes 1474564
  20.4 9.1 %collective-permute-start.4 = (bf16[320,384]{1,0:T(8,128)(2,1)S(1)}, bf16[320,384]{1,0:T(8,128)(2,1)S(1)}, u32[]{:S(2)}, u32[]{:S(2)}) collective-permute-start(bf16[320,384]{1,0:T(8,128)(2,1)S(1)} %halves_kernel.1), channel_id=1, source_target_pairs={{0,2},{2,0},{1,3},{3,1},{4,6},{6,4},{5,7},{7,5},{8,10},{10,8},{9,1... | collective-permute-start | bytes 737288 | tf_op jit(solution)/shard_map/ppermute | solution.py:30
  22.3 1.0 %copy-start.2 = (bf16[320,384]{1,0:T(8,128)(2,1)S(1)}, bf16[320,384]{1,0:T(8,128)(2,1)}, u32[]{:S(2)}) copy-start(bf16[320,384]{1,0:T(8,128)(2,1)} %reward_ref.5) | copy-start | bytes 737284
  23.3 33.8 %copy-start.1 = (bf16[1,3,320,1280]{3,2,1,0:T(8,128)(2,1)S(1)}, bf16[1,3,320,1280]{3,2,1,0:T(8,128)(2,1)}, u32[]{:S(2)}) copy-start(bf16[1,3,320,1280]{3,2,1,0:T(8,128)(2,1)} %param.16) | copy-start | bytes 7372804
  24.0 21.6 %collective-permute-start.3 = (bf16[320,384]{1,0:T(8,128)(2,1)S(1)}, bf16[320,384]{1,0:T(8,128)(2,1)S(1)}, u32[]{:S(2)}, u32[]{:S(2)}) collective-permute-start(bf16[320,384]{1,0:T(8,128)(2,1)S(1)} %scaled_kernel.1.scaled_ref), channel_id=1, source_target_pairs={{0,2},{2,0},{1,3},{3,1},{4,6},{6,4},{5,7},{7,5},{8,10},{10,8},{9,1... | collective-permute-start | bytes 737288 | tf_op jit(solution)/shard_map/ppermute | solution.py:30
  30.1 35.6 %collective-permute-start.5 = (bf16[320,384]{1,0:T(8,128)(2,1)S(1)}, bf16[320,384]{1,0:T(8,128)(2,1)S(1)}, u32[]{:S(2)}, u32[]{:S(2)}) collective-permute-start(bf16[320,384]{1,0:T(8,128)(2,1)S(1)} %sent_kernel.1), channel_id=1, source_target_pairs={{0,508},{4,504},{8,500},{12,496},{16,492},{20,488},{24,484},{28,48... | collective-permute-start | bytes 737288 | tf_op jit(solution)/shard_map/ppermute | solution.py:327
  45.7 10.9 %collective-permute-start.6 = (bf16[160,384]{1,0:T(8,128)(2,1)S(1)}, bf16[160,384]{1,0:T(8,128)(2,1)S(1)}, u32[]{:S(2)}, u32[]{:S(2)}) collective-permute-start(bf16[160,384]{1,0:T(8,128)(2,1)S(1)} %get-tuple-element.53), channel_id=1, source_target_pairs={{0,1},{1,0},{2,3},{3,2},{4,5},{5,4},{6,7},{7,6},{8,9},{9,8},{10,11... | collective-permute-start | bytes 368648 | tf_op jit(solution)/shard_map/ppermute | solution.py:26
  49.5 7.0 %collective-permute-start.7 = (bf16[160,384]{1,0:T(8,128)(2,1)S(1)}, bf16[160,384]{1,0:T(8,128)(2,1)S(1)}, u32[]{:S(2)}, u32[]{:S(2)}) collective-permute-start(bf16[160,384]{1,0:T(8,128)(2,1)S(1)} %get-tuple-element.54), channel_id=1, source_target_pairs={{0,1},{1,0},{2,3},{3,2},{4,5},{5,4},{6,7},{7,6},{8,9},{9,8},{10,11... | collective-permute-start | bytes 368648 | tf_op jit(solution)/shard_map/ppermute | solution.py:26
  51.5 5.1 %collective-permute-start.8 = (bf16[160,384]{1,0:T(8,128)(2,1)S(1)}, bf16[160,384]{1,0:T(8,128)(2,1)S(1)}, u32[]{:S(2)}, u32[]{:S(2)}) collective-permute-start(bf16[160,384]{1,0:T(8,128)(2,1)S(1)} %get-tuple-element.55), channel_id=1, source_target_pairs={{0,1},{1,0},{2,3},{3,2},{4,5},{5,4},{6,7},{7,6},{8,9},{9,8},{10,11... | collective-permute-start | bytes 368648 | tf_op jit(solution)/shard_map/ppermute | solution.py:26
  53.9 3.2 %collective-permute-start.9 = (bf16[160,384]{1,0:T(8,128)(2,1)S(1)}, bf16[160,384]{1,0:T(8,128)(2,1)S(1)}, u32[]{:S(2)}, u32[]{:S(2)}) collective-permute-start(bf16[160,384]{1,0:T(8,128)(2,1)S(1)} %get-tuple-element.56), channel_id=1, source_target_pairs={{0,1},{1,0},{2,3},{3,2},{4,5},{5,4},{6,7},{7,6},{8,9},{9,8},{10,11... | collective-permute-start | bytes 368648 | tf_op jit(solution)/shard_map/ppermute | solution.py:26

commit v9 on v8

--- a/solution.py
+++ b/solution.py
@@ -80,20 +80,21 @@
     acted = normed / (1.0 + jnp.exp(-normed))
     for k in range(3):
         stacked_ref[k * rows : (k + 1) * rows, :] = frame_shift(acted, k - 1).astype(jnp.bfloat16)
-    own_side(1 - place_ref[1], weight_ref, stacked_ref, mate_ref)
-
-
-def own_side(core, weight_ref, stacked_ref, out_ref):
+    own_side(1 - place_ref[1], place_ref[2], weight_ref, stacked_ref, mate_ref)
+
+
+def own_side(core, chip, weight_ref, stacked_ref, out_ref):
     rows = out_ref.shape[1]
-    for chip in range(2):
-        start = pl.multiple_of((chip * 2 + core) * rows, rows)
-        out_ref[chip] = jnp.dot(
+    for side in range(2):
+        block = jnp.bitwise_xor(chip, 1 - side) * 2 + core
+        start = pl.multiple_of(block * rows, rows)
+        out_ref[side] = jnp.dot(
             weight_ref[pl.ds(start, rows), :], stacked_ref[...], preferred_element_type=jnp.float32
         )
 
 
 def own_kernel(place_ref, weight_ref, stacked_ref, own_ref):
-    own_side(place_ref[1], weight_ref, stacked_ref, own_ref)
+    own_side(place_ref[1], place_ref[2], weight_ref, stacked_ref, own_ref)
 
 
 def prepare_kernel(
@@ -120,9 +121,8 @@
     scaled_ref[...] = gained(cot_total, columns_ref, 1).astype(jnp.bfloat16)
 
 
-def halves_kernel(place_ref, own_ref, mate_ref, far_ref):
-    chip = 1 - place_ref[2]
-    far_ref[...] = (own_ref[chip] + mate_ref[chip]).astype(jnp.bfloat16)
+def halves_kernel(own_ref, mate_ref, far_ref):
+    far_ref[...] = (own_ref[0] + mate_ref[0]).astype(jnp.bfloat16)
 
 
 def gained(values, columns_ref, way):
@@ -149,14 +149,16 @@
     near_ref,
     normed_ref,
     factor_ref,
+    slope_ref,
 ):
-    chip = place_ref[2]
     x_in = jnp.where(place_ref[0] == 0, entry_ref[...], arrived_ref[...]).astype(jnp.float32)
-    near = gained(own_ref[chip] + mate_ref[chip], columns_ref, 0)
+    near = gained(own_ref[1] + mate_ref[1], columns_ref, 0)
     near_ref[...] = x_in + near + added_ref[...].astype(jnp.float32)
     normed, factor = normalize(stored_ref[plan_ref[0, 1]].astype(jnp.float32))
     normed_ref[...] = normed
     factor_ref[...] = jnp.broadcast_to(factor, factor_ref.shape)
+    sigmoid = 1.0 / (1.0 + jnp.exp(-normed))
+    slope_ref[...] = sigmoid * (1.0 + normed * (1.0 - sigmoid))
 
 
 def output_kernel(near_ref, far_ref, columns_ref, out_ref):
@@ -189,6 +191,7 @@
     place_ref,
     normed_ref,
     factor_ref,
+    slope_ref,
     returned_ref,
     reward_ref,
     extra_ref,
@@ -217,15 +220,13 @@
     put(1 - chip, 1 - core, other_high_ref[...], rows // 2)
     cot_total = cotangent(place_ref, returned_ref, reward_ref, extra_ref)
     normed = normed_ref[...]
-    sigmoid = 1.0 / (1.0 + jnp.exp(-normed))
-    slope = sigmoid * (1.0 + normed * (1.0 - sigmoid))
     folded = jnp.dot(weight_ref[...], whole_ref[...], preferred_element_type=jnp.float32)
     d_acted = (
         frame_shift(folded[:rows], 1)
         + folded[rows : 2 * rows]
         + frame_shift(folded[2 * rows :], -1)
     )
-    d_normed = by_group(d_acted * slope)
+    d_normed = by_group(d_acted * slope_ref[...])
     grouped = by_group(normed)
     result = factor_ref[:, :1, :1] * (
         d_normed - group_mean(d_normed) - grouped * group_mean(d_normed * grouped)
@@ -295,13 +296,13 @@
     )
     mate_part = swap_core(mate_side)
     (own,) = call(own_kernel, [pair], [SMEM, VMEM, VMEM], [place, turned, stacked], cost=20.0)
-    (far_side,) = call(halves_kernel, [field], [SMEM, VMEM, VMEM], [place, own, mate_part])
+    (far_side,) = call(halves_kernel, [field], [VMEM, VMEM], [own, mate_part])
     far = swap_chip(far_side)
     stored, far_side = lax.optimization_barrier((stored, far_side))
     whole = ((rows, cells), jnp.float32)
-    near, saved_normed, saved_factor = call(
+    near, saved_normed, saved_factor, slope = call(
         near_kernel,
-        [whole, whole, ((rows // WIDTH, 8, 128), jnp.float32)],
+        [whole, whole, ((rows // WIDTH, 8, 128), jnp.float32), whole],
         [SMEM] * 2 + [VMEM] * 7,
         [place, plan, own, mate_part, arrived, entry_latent, added, gains, stored],
         cost=20.0,
@@ -338,11 +339,12 @@
     (cot_out,) = call(
         gradient_kernel,
         [field],
-        [SMEM] + [VMEM] * 12,
+        [SMEM] + [VMEM] * 13,
         [
             place,
             saved_normed,
             saved_factor,
+            slope,
             returned,
             reward_head,
             extra,

time: 66.8 us -> 66.2 us (level)
  transfers between devices with their start and end apart: 10 -> 10, of which waited for: 4 -> 4; matrix products, arithmetic and copies ran while one was open for 0% -> 0% of each run, Pallas kernels for 18% -> 17%
where the time goes in v9:
time: 66.2 us; the launch traced here: 65.8 us
  starting transfers between devices  42.2 us (64%)
  Pallas kernels  11.2 us (17%)
  waiting for transfers between devices  8.67 us (13%)
  local copies, waits for them, and re-layouts  2.79 us (4%)
  between operations  0.91 us (1%)
    ppermute x1, starting transfers between devices, local(): mirror_in = lax.ppermute(sent, 'section', route)  15.5 us
    ppermute x5, starting transfers between devices, swap_core(): return lax.ppermute(block, 'ch', [(0, 1), (1, 0), (2, 3), (3, 2)])  14.3 us
    pallas_call x11, Pallas kernels, call(): pl.pallas_call(kernel, out_shape=[jax.ShapeDtypeStruct(shape, kind) for s...  11.2 us
    ppermute x2, starting transfers between devices, shifted(): return lax.ppermute(block, axis, route)  6.94 us
    ppermute x1, waiting for transfers between devices, local(): mirror_in = lax.ppermute(sent, 'section', route)  5.61 us
    ppermute x2, starting transfers between devices, swap_chip(): return lax.ppermute(block, 'ch', [(0, 2), (2, 0), (1, 3), (3, 1)])  5.41 us
    unnamed x21, local copies, waits for them, and re-layouts  2.7 us
    ppermute x2, waiting for transfers between devices, swap_chip(): return lax.ppermute(block, 'ch', [(0, 2), (2, 0), (1, 3), (3, 1)])  1.76 us
  transfers between devices with their start and end apart: 10, of which 4 were waited for; matrix products, arithmetic and copies ran while one was open for 0% of the time, Pallas kernels for 17%

profile of v9, /device:TPU:1, one launch (start us, length us, event | category | flops | bytes accessed | tf_op | source)
XLA Modules:
  0.0 65.8 jit_solution(9872399238092918917)
XLA Ops:
  0.6 5.7 %collective-permute-start.1 = (bf16[320,384]{1,0:T(8,128)(2,1)}, bf16[320,384]{1,0:T(8,128)(2,1)S(1)}, u32[]{:S(2)}, u32[]{:S(2)}) collective-permute-start(bf16[320,384]{1,0:T(8,128)(2,1)} %bitcast.23), channel_id=1, source_target_pairs={{0,4},{4,8},{8,12},{12,16},{16,20},{20,24},{24,28},{28,32},{32,36}... | collective-permute-start | bytes 737288 | tf_op jit(solution)/shard_map/ppermute | solution.py:22
  6.3 1.7 %copy-done = bf16[1,3,320,1280]{3,2,1,0:T(8,128)(2,1)S(1)} copy-done((bf16[1,3,320,1280]{3,2,1,0:T(8,128)(2,1)S(1)}, bf16[1,3,320,1280]{3,2,1,0:T(8,128)(2,1)}, u32[]{:S(2)}) %copy-start) | copy-done | bytes 2457624
  8.0 0.8 %transpose_kernel.1.weight_ref = bf16[1280,960]{1,0:T(8,128)(2,1)S(1)} custom-call(bf16[960,1280]{1,0:T(8,128)(2,1)S(1)} %bitcast.14), custom_call_target="tpu_custom_call" | custom-call | flops 20000000000 | bytes 20000000 | tf_op jit(solution)/shard_map/transpose_kernel/pallas_call | solution.py:238
  9.1 0.7 %prepare_kernel.1 = (f32[2,320,128]{2,1,0:T(8,128)S(1)}, bf16[320,384]{1,0:T(8,128)(2,1)S(1)}, bf16[320,384]{1,0:T(8,128)(2,1)S(1)}) custom-call(s32[6]{0:T(128)S(1)} %stack.39.place_ref, s32[1,2]{1,0:T(1,128)S(1)} %copy-done.9, s32[1,2]{1,0:T(1,128)S(1)} %copy-done.8, bf16[2,320,384]{2,1,0:T(8,128)(2,1)S(1)} %bitcast.18, f32[25,320]{1,0:T(8,128)S(1)} %copy-done.7), custom_call_target="tpu_custom_call" | custom-call | flops 20000000000 | bytes 20000000 | tf_op jit(solution)/shard_map/prepare_kernel/pallas_call | solution.py:238
  10.0 1.3 %collective-permute-start = (bf16[320,384]{1,0:T(8,128)(2,1)S(1)}, bf16[320,384]{1,0:T(8,128)(2,1)S(1)}, u32[]{:S(2)}, u32[]{:S(2)}) collective-permute-start(bf16[320,384]{1,0:T(8,128)(2,1)S(1)} %bitcast.16), channel_id=1, source_target_pairs={{4,0},{8,4},{12,8},{16,12},{20,16},{24,20},{28,24},{32,28},{36,32}... | collective-permute-start | bytes 737288 | tf_op jit(solution)/shard_map/ppermute | solution.py:22
  11.3 1.9 %forward_kernel.1 = (f32[2,320,384]{2,1,0:T(8,128)S(1)}, bf16[960,384]{1,0:T(8,128)(2,1)S(1)}) custom-call(s32[6]{0:T(128)S(1)} %stack.39.place_ref, bf16[320,384]{1,0:T(8,128)(2,1)S(1)} %collective-permute-done.1.arrived_ref, bf16[320,384]{1,0:T(8,128)(2,1)S(1)} %copy-done.3, bf16[1280,960]{1,0:T(8,128)(2,1)S(1)} %transpose_kernel.1.weight_ref), custom_call_target="tpu_custom_call" | custom-call | tf_op jit(solution)/shard_map/forward_kernel/pallas_call | solution.py:238
  13.2 4.4 %collective-permute-start.2 = (f32[2,320,384]{2,1,0:T(8,128)S(1)}, f32[2,320,384]{2,1,0:T(8,128)S(1)}, u32[]{:S(2)}, u32[]{:S(2)}) collective-permute-start(f32[2,320,384]{2,1,0:T(8,128)S(1)} %get-tuple-element.39), channel_id=1, source_target_pairs={{0,1},{1,0},{2,3},{3,2},{4,5},{5,4},{6,7},{7,6},{8,9},{9,8},{10,11... | collective-permute-start | bytes 2949128 | tf_op jit(solution)/shard_map/ppermute | solution.py:26
  17.6 1.4 %own_kernel.1.own_ref = f32[2,320,384]{2,1,0:T(8,128)S(1)} custom-call(s32[6]{0:T(128)S(1)} %stack.39.place_ref, bf16[1280,960]{1,0:T(8,128)(2,1)S(1)} %transpose_kernel.1.weight_ref, bf16[960,384]{1,0:T(8,128)(2,1)S(1)} %get-tuple-element.38.stacked_ref), custom_call_target="tpu_custom_call" | custom-call | flops 20000000000 | bytes 20000000 | tf_op jit(solution)/shard_map/own_kernel/pallas_call | solution.py:238
  19.0 0.8 %collective-permute-done.2.mate_ref = f32[2,320,384]{2,1,0:T(8,128)S(1)} collective-permute-done((f32[2,320,384]{2,1,0:T(8,128)S(1)}, f32[2,320,384]{2,1,0:T(8,128)S(1)}, u32[]{:S(2)}, u32[]{:S(2)}) %collective-permute-start.2) | collective-permute-done | bytes 983072 | tf_op jit(solution)/shard_map/ppermute | solution.py:26
  19.8 1.9 %collective-permute-start.4 = (bf16[320,384]{1,0:T(8,128)(2,1)S(1)}, bf16[320,384]{1,0:T(8,128)(2,1)S(1)}, u32[]{:S(2)}, u32[]{:S(2)}) collective-permute-start(bf16[320,384]{1,0:T(8,128)(2,1)S(1)} %halves_kernel.1), channel_id=1, source_target_pairs={{0,2},{2,0},{1,3},{3,1},{4,6},{6,4},{5,7},{7,5},{8,10},{10,8},{9,1... | collective-permute-start | bytes 737288 | tf_op jit(solution)/shard_map/ppermute | solution.py:30
  21.8 1.2 %near_kernel.1 = (f32[320,384]{1,0:T(8,128)S(1)}, f32[320,384]{1,0:T(8,128)S(1)}, f32[8,8,128]{2,1,0:T(8,128)S(1)}, f32[320,384]{1,0:T(8,128)S(1)}) custom-call(s32[6]{0:T(128)S(1)} %stack.39.place_ref, s32[1,2]{1,0:T(1,128)S(1)} %copy-done.9, f32[2,320,384]{2,1,0:T(8,128)S(1)} %own_kernel.1.own_ref, f32[2,320,384]{2,1,0:T(8,128)S(1)} %collective-permute-done.2.mate_ref, ...), custom_call_target="tpu_custom_call" | custom-call | flops 20000000000 | bytes 20000000 | tf_op jit(solution)/shard_map/near_kernel/pallas_call | solution.py:238
  23.0 0.6 scaled_kernel.1.scaled_ref
  23.7 3.5 %collective-permute-start.3 = (bf16[320,384]{1,0:T(8,128)(2,1)S(1)}, bf16[320,384]{1,0:T(8,128)(2,1)S(1)}, u32[]{:S(2)}, u32[]{:S(2)}) collective-permute-start(bf16[320,384]{1,0:T(8,128)(2,1)S(1)} %scaled_kernel.1.scaled_ref), channel_id=1, source_target_pairs={{0,2},{2,0},{1,3},{3,1},{4,6},{6,4},{5,7},{7,5},{8,10},{10,8},{9,1... | collective-permute-start | bytes 737288 | tf_op jit(solution)/shard_map/ppermute | solution.py:30
  27.2 1.8 %collective-permute-done.4.far_ref = bf16[320,384]{1,0:T(8,128)(2,1)S(1)} collective-permute-done((bf16[320,384]{1,0:T(8,128)(2,1)S(1)}, bf16[320,384]{1,0:T(8,128)(2,1)S(1)}, u32[]{:S(2)}, u32[]{:S(2)}) %collective-permute-start.4) | collective-permute-done | bytes 245792 | tf_op jit(solution)/shard_map/ppermute | solution.py:30
  28.9 0.6 sent_kernel.1
  29.5 15.5 %collective-permute-start.5 = (bf16[320,384]{1,0:T(8,128)(2,1)S(1)}, bf16[320,384]{1,0:T(8,128)(2,1)S(1)}, u32[]{:S(2)}, u32[]{:S(2)}) collective-permute-start(bf16[320,384]{1,0:T(8,128)(2,1)S(1)} %sent_kernel.1), channel_id=1, source_target_pairs={{0,508},{4,504},{8,500},{12,496},{16,492},{20,488},{24,484},{28,48... | collective-permute-start | bytes 737288 | tf_op jit(solution)/shard_map/ppermute | solution.py:328
  45.1 3.7 %collective-permute-start.6 = (bf16[160,384]{1,0:T(8,128)(2,1)S(1)}, bf16[160,384]{1,0:T(8,128)(2,1)S(1)}, u32[]{:S(2)}, u32[]{:S(2)}) collective-permute-start(bf16[160,384]{1,0:T(8,128)(2,1)S(1)} %get-tuple-element.55), channel_id=1, source_target_pairs={{0,1},{1,0},{2,3},{3,2},{4,5},{5,4},{6,7},{7,6},{8,9},{9,8},{10,11... | collective-permute-start | bytes 368648 | tf_op jit(solution)/shard_map/ppermute | solution.py:26
  48.8 1.9 %collective-permute-start.7 = (bf16[160,384]{1,0:T(8,128)(2,1)S(1)}, bf16[160,384]{1,0:T(8,128)(2,1)S(1)}, u32[]{:S(2)}, u32[]{:S(2)}) collective-permute-start(bf16[160,384]{1,0:T(8,128)(2,1)S(1)} %get-tuple-element.56), channel_id=1, source_target_pairs={{0,1},{1,0},{2,3},{3,2},{4,5},{5,4},{6,7},{7,6},{8,9},{9,8},{10,11... | collective-permute-start | bytes 368648 | tf_op jit(solution)/shard_map/ppermute | solution.py:26
  50.7 2.4 %collective-permute-start.8 = (bf16[160,384]{1,0:T(8,128)(2,1)S(1)}, bf16[160,384]{1,0:T(8,128)(2,1)S(1)}, u32[]{:S(2)}, u32[]{:S(2)}) collective-permute-start(bf16[160,384]{1,0:T(8,128)(2,1)S(1)} %get-tuple-element.57), channel_id=1, source_target_pairs={{0,1},{1,0},{2,3},{3,2},{4,5},{5,4},{6,7},{7,6},{8,9},{9,8},{10,11... | collective-permute-start | bytes 368648 | tf_op jit(solution)/shard_map/ppermute | solution.py:26
  53.1 1.9 %collective-permute-start.9 = (bf16[160,384]{1,0:T(8,128)(2,1)S(1)}, bf16[160,384]{1,0:T(8,128)(2,1)S(1)}, u32[]{:S(2)}, u32[]{:S(2)}) collective-permute-start(bf16[160,384]{1,0:T(8,128)(2,1)S(1)} %get-tuple-element.58), channel_id=1, source_target_pairs={{0,1},{1,0},{2,3},{3,2},{4,5},{5,4},{6,7},{7,6},{8,9},{9,8},{10,11... | collective-permute-start | bytes 368648 | tf_op jit(solution)/shard_map/ppermute | solution.py:26
  55.1 0.8 %output_kernel.1 = bf16[320,384]{1,0:T(8,128)(2,1)} custom-call(f32[320,384]{1,0:T(8,128)S(1)} %get-tuple-element.49.near_ref, bf16[320,384]{1,0:T(8,128)(2,1)S(1)} %collective-permute-done.4.far_ref, f32[2,320,128]{2,1,0:T(8,128)S(1)} %get-tuple-element.41.columns_ref), custom_call_target="tpu_custom_call" | custom-call | tf_op jit(solution)/shard_map/output_kernel/pallas_call | solution.py:238
  56.4 3.1 %gradient_kernel.1 = bf16[320,384]{1,0:T(8,128)(2,1)} custom-call(s32[6]{0:T(128)S(1)} %stack.39.place_ref, f32[320,384]{1,0:T(8,128)S(1)} %get-tuple-element.50.normed_ref, f32[8,8,128]{2,1,0:T(8,128)S(1)} %get-tuple-element.51.factor_ref, f32[320,384]{1,0:T(8,128)S(1)} %get-tuple-element.52.slope_ref, ...), custom_call_target="tpu_custom_call" | custom-call | tf_op jit(solution)/shard_map/gradient_kernel/pallas_call | solution.py:238
  59.5 5.6 %collective-permute-done.5 = bf16[320,384]{1,0:T(8,128)(2,1)S(1)} collective-permute-done((bf16[320,384]{1,0:T(8,128)(2,1)S(1)}, bf16[320,384]{1,0:T(8,128)(2,1)S(1)}, u32[]{:S(2)}, u32[]{:S(2)}) %collective-permute-start.5) | collective-permute-done | bytes 245792 | tf_op jit(solution)/shard_map/ppermute | solution.py:328
  65.1 0.7 %copy.14 = bf16[1,320,384]{2,1,0:T(8,128)(2,1)} copy(bf16[1,320,384]{2,1,0:T(8,128)(2,1)S(1)} %bitcast.21) | data formatting | bytes 491520
  (29 shorter events, 1.1 us)
Async XLA Ops:
  0.6 10.7 %collective-permute-start.1 = (bf16[320,384]{1,0:T(8,128)(2,1)}, bf16[320,384]{1,0:T(8,128)(2,1)S(1)}, u32[]{:S(2)}, u32[]{:S(2)}) collective-permute-start(bf16[320,384]{1,0:T(8,128)(2,1)} %bitcast.23), channel_id=1, source_target_pairs={{0,4},{4,8},{8,12},{12,16},{16,20},{20,24},{24,28},{28,32},{32,36}... | collective-permute-start | bytes 737288 | tf_op jit(solution)/shard_map/ppermute | solution.py:22
  6.3 1.7 %copy-start = (bf16[1,3,320,1280]{3,2,1,0:T(8,128)(2,1)S(1)}, bf16[1,3,320,1280]{3,2,1,0:T(8,128)(2,1)}, u32[]{:S(2)}) copy-start(bf16[1,3,320,1280]{3,2,1,0:T(8,128)(2,1)} %param.16) | copy-start | bytes 7372804
  8.0 1.0 %copy-start.5 = (bf16[1,2,320,384]{3,2,1,0:T(8,128)(2,1)S(1)}, bf16[1,2,320,384]{3,2,1,0:T(8,128)(2,1)}, u32[]{:S(2)}) copy-start(bf16[1,2,320,384]{3,2,1,0:T(8,128)(2,1)} %param.15) | copy-start | bytes 1474564
  8.0 1.0 %copy-start.7 = (f32[25,320]{1,0:T(8,128)S(1)}, f32[25,320]{1,0:T(8,128)}, u32[]{:S(2)}) copy-start(f32[25,320]{1,0:T(8,128)} %gain_ref) | copy-start | bytes 96004
  8.0 1.0 %copy-start.8 = (s32[1,2]{1,0:T(1,128)S(1)}, s32[1,2]{1,0:T(1,128)}, u32[]{:S(2)}) copy-start(s32[1,2]{1,0:T(1,128)} %stamps_ref.1) | copy-start | bytes 28
  8.0 1.0 %copy-start.9 = (s32[1,2]{1,0:T(1,128)S(1)}, s32[1,2]{1,0:T(1,128)}, u32[]{:S(2)}) copy-start(s32[1,2]{1,0:T(1,128)} %plan_ref.3) | copy-start | bytes 28
  9.1 0.9 %copy-start.4 = (bf16[1,320,384]{2,1,0:T(8,128)(2,1)S(1)}, bf16[1,320,384]{2,1,0:T(8,128)(2,1)}, u32[]{:S(2)}) copy-start(bf16[1,320,384]{2,1,0:T(8,128)(2,1)} %param.11) | copy-start | bytes 737284
  9.1 2.2 %copy-start.3 = (bf16[320,384]{1,0:T(8,128)(2,1)S(1)}, bf16[320,384]{1,0:T(8,128)(2,1)}, u32[]{:S(2)}) copy-start(bf16[320,384]{1,0:T(8,128)(2,1)} %entry_ref.3) | copy-start | bytes 737284
  10.0 13.0 %collective-permute-start = (bf16[320,384]{1,0:T(8,128)(2,1)S(1)}, bf16[320,384]{1,0:T(8,128)(2,1)S(1)}, u32[]{:S(2)}, u32[]{:S(2)}) collective-permute-start(bf16[320,384]{1,0:T(8,128)(2,1)S(1)} %bitcast.16), channel_id=1, source_target_pairs={{4,0},{8,4},{12,8},{16,12},{20,16},{24,20},{28,24},{32,28},{36,32}... | collective-permute-start | bytes 737288 | tf_op jit(solution)/shard_map/ppermute | solution.py:22
  13.2 6.6 %collective-permute-start.2 = (f32[2,320,384]{2,1,0:T(8,128)S(1)}, f32[2,320,384]{2,1,0:T(8,128)S(1)}, u32[]{:S(2)}, u32[]{:S(2)}) collective-permute-start(f32[2,320,384]{2,1,0:T(8,128)S(1)} %get-tuple-element.39), channel_id=1, source_target_pairs={{0,1},{1,0},{2,3},{3,2},{4,5},{5,4},{6,7},{7,6},{8,9},{9,8},{10,11... | collective-permute-start | bytes 2949128 | tf_op jit(solution)/shard_map/ppermute | solution.py:26
  17.6 4.2 %copy-start.6 = (bf16[1,2,320,384]{3,2,1,0:T(8,128)(2,1)S(1)}, bf16[1,2,320,384]{3,2,1,0:T(8,128)(2,1)}, u32[]{:S(2)}) copy-start(bf16[1,2,320,384]{3,2,1,0:T(8,128)(2,1)} %param.14) | copy-start | bytes 1474564
  19.8 9.1 %collective-permute-start.4 = (bf16[320,384]{1,0:T(8,128)(2,1)S(1)}, bf16[320,384]{1,0:T(8,128)(2,1)S(1)}, u32[]{:S(2)}, u32[]{:S(2)}) collective-permute-start(bf16[320,384]{1,0:T(8,128)(2,1)S(1)} %halves_kernel.1), channel_id=1, source_target_pairs={{0,2},{2,0},{1,3},{3,1},{4,6},{6,4},{5,7},{7,5},{8,10},{10,8},{9,1... | collective-permute-start | bytes 737288 | tf_op jit(solution)/shard_map/ppermute | solution.py:30
  21.8 1.2 %copy-start.2 = (bf16[320,384]{1,0:T(8,128)(2,1)S(1)}, bf16[320,384]{1,0:T(8,128)(2,1)}, u32[]{:S(2)}) copy-start(bf16[320,384]{1,0:T(8,128)(2,1)} %reward_ref.5) | copy-start | bytes 737284
  23.0 33.4 %copy-start.1 = (bf16[1,3,320,1280]{3,2,1,0:T(8,128)(2,1)S(1)}, bf16[1,3,320,1280]{3,2,1,0:T(8,128)(2,1)}, u32[]{:S(2)}) copy-start(bf16[1,3,320,1280]{3,2,1,0:T(8,128)(2,1)} %param.16) | copy-start | bytes 7372804
  23.7 21.4 %collective-permute-start.3 = (bf16[320,384]{1,0:T(8,128)(2,1)S(1)}, bf16[320,384]{1,0:T(8,128)(2,1)S(1)}, u32[]{:S(2)}, u32[]{:S(2)}) collective-permute-start(bf16[320,384]{1,0:T(8,128)(2,1)S(1)} %scaled_kernel.1.scaled_ref), channel_id=1, source_target_pairs={{0,2},{2,0},{1,3},{3,1},{4,6},{6,4},{5,7},{7,5},{8,10},{10,8},{9,1... | collective-permute-start | bytes 737288 | tf_op jit(solution)/shard_map/ppermute | solution.py:30
  29.5 35.6 %collective-permute-start.5 = (bf16[320,384]{1,0:T(8,128)(2,1)S(1)}, bf16[320,384]{1,0:T(8,128)(2,1)S(1)}, u32[]{:S(2)}, u32[]{:S(2)}) collective-permute-start(bf16[320,384]{1,0:T(8,128)(2,1)S(1)} %sent_kernel.1), channel_id=1, source_target_pairs={{0,508},{4,504},{8,500},{12,496},{16,492},{20,488},{24,484},{28,48... | collective-permute-start | bytes 737288 | tf_op jit(solution)/shard_map/ppermute | solution.py:328
  45.1 10.7 %collective-permute-start.6 = (bf16[160,384]{1,0:T(8,128)(2,1)S(1)}, bf16[160,384]{1,0:T(8,128)(2,1)S(1)}, u32[]{:S(2)}, u32[]{:S(2)}) collective-permute-start(bf16[160,384]{1,0:T(8,128)(2,1)S(1)} %get-tuple-element.55), channel_id=1, source_target_pairs={{0,1},{1,0},{2,3},{3,2},{4,5},{5,4},{6,7},{7,6},{8,9},{9,8},{10,11... | collective-permute-start | bytes 368648 | tf_op jit(solution)/shard_map/ppermute | solution.py:26
  48.8 7.0 %collective-permute-start.7 = (bf16[160,384]{1,0:T(8,128)(2,1)S(1)}, bf16[160,384]{1,0:T(8,128)(2,1)S(1)}, u32[]{:S(2)}, u32[]{:S(2)}) collective-permute-start(bf16[160,384]{1,0:T(8,128)(2,1)S(1)} %get-tuple-element.56), channel_id=1, source_target_pairs={{0,1},{1,0},{2,3},{3,2},{4,5},{5,4},{6,7},{7,6},{8,9},{9,8},{10,11... | collective-permute-start | bytes 368648 | tf_op jit(solution)/shard_map/ppermute | solution.py:26
  50.7 5.1 %collective-permute-start.8 = (bf16[160,384]{1,0:T(8,128)(2,1)S(1)}, bf16[160,384]{1,0:T(8,128)(2,1)S(1)}, u32[]{:S(2)}, u32[]{:S(2)}) collective-permute-start(bf16[160,384]{1,0:T(8,128)(2,1)S(1)} %get-tuple-element.57), channel_id=1, source_target_pairs={{0,1},{1,0},{2,3},{3,2},{4,5},{5,4},{6,7},{7,6},{8,9},{9,8},{10,11... | collective-permute-start | bytes 368648 | tf_op jit(solution)/shard_map/ppermute | solution.py:26
  53.1 3.2 %collective-permute-start.9 = (bf16[160,384]{1,0:T(8,128)(2,1)S(1)}, bf16[160,384]{1,0:T(8,128)(2,1)S(1)}, u32[]{:S(2)}, u32[]{:S(2)}) collective-permute-start(bf16[160,384]{1,0:T(8,128)(2,1)S(1)} %get-tuple-element.58), channel_id=1, source_target_pairs={{0,1},{1,0},{2,3},{3,2},{4,5},{5,4},{6,7},{7,6},{8,9},{9,8},{10,11... | collective-permute-start | bytes 368648 | tf_op jit(solution)/shard_map/ppermute | solution.py:26

commit v10 on v9

--- a/solution.py
+++ b/solution.py
@@ -77,9 +77,11 @@
     first = place_ref[0] == 0
     x_in = jnp.where(first, entry_ref[...], arrived_ref[...]).astype(jnp.float32)
     normed, _ = normalize(x_in)
-    acted = normed / (1.0 + jnp.exp(-normed))
-    for k in range(3):
-        stacked_ref[k * rows : (k + 1) * rows, :] = frame_shift(acted, k - 1).astype(jnp.bfloat16)
+    acted = (normed / (1.0 + jnp.exp(-normed))).astype(jnp.bfloat16)
+    empty = jnp.zeros((rows, CELLS), jnp.bfloat16)
+    stacked_ref[:rows, :] = jnp.concatenate([empty, acted[:, :-CELLS]], 1)
+    stacked_ref[rows : 2 * rows, :] = acted
+    stacked_ref[2 * rows :, :] = jnp.concatenate([acted[:, CELLS:], empty], 1)
     own_side(1 - place_ref[1], place_ref[2], weight_ref, stacked_ref, mate_ref)
 
 
@@ -97,18 +99,14 @@
     own_side(place_ref[1], place_ref[2], weight_ref, stacked_ref, own_ref)
 
 
-def prepare_kernel(
-    place_ref, plan_ref, stamps_ref, skip_ref, gain_ref, columns_ref, added_ref, extra_ref
-):
-    for way in range(2):
-        columns_ref[way] = jnp.broadcast_to(
-            column(gain_ref, stamps_ref[0, way]), columns_ref.shape[1:]
-        )
-    encoder = place_ref[4] == 1
+def prepare_kernel(place_ref, plan_ref, stamps_ref, skip_ref, gain_ref, columns_ref, added_ref):
+    spread(gain_ref, stamps_ref[0, 0], columns_ref)
     added = skip_ref[plan_ref[0, 0]]
-    extra = skip_ref[plan_ref[0, 1]]
-    added_ref[...] = jnp.where(encoder, jnp.zeros_like(added), added)
-    extra_ref[...] = jnp.where(encoder, extra, jnp.zeros_like(extra))
+    added_ref[...] = jnp.where(place_ref[4] == 1, jnp.zeros_like(added), added)
+
+
+def spread(gain_ref, stamp, columns_ref):
+    columns_ref[...] = jnp.broadcast_to(column(gain_ref, stamp), columns_ref.shape)
 
 
 def cotangent(place_ref, returned_ref, reward_ref, extra_ref):
@@ -118,18 +116,19 @@
 
 def scaled_kernel(place_ref, returned_ref, reward_ref, extra_ref, columns_ref, scaled_ref):
     cot_total = cotangent(place_ref, returned_ref, reward_ref, extra_ref)
-    scaled_ref[...] = gained(cot_total, columns_ref, 1).astype(jnp.bfloat16)
-
-
-def halves_kernel(own_ref, mate_ref, far_ref):
+    scaled_ref[...] = gained(cot_total, columns_ref).astype(jnp.bfloat16)
+
+
+def halves_kernel(own_ref, mate_ref, far_ref, after_ref):
+    after_ref[...] = jnp.zeros_like(after_ref)
     far_ref[...] = (own_ref[0] + mate_ref[0]).astype(jnp.bfloat16)
 
 
-def gained(values, columns_ref, way):
-    size = columns_ref.shape[2]
+def gained(values, columns_ref):
+    size = columns_ref.shape[1]
     return jnp.concatenate(
         [
-            values[:, start : start + size] * columns_ref[way]
+            values[:, start : start + size] * columns_ref[...]
             for start in range(0, values.shape[1], size)
         ],
         1,
@@ -138,22 +137,21 @@
 
 def near_kernel(
     place_ref,
-    plan_ref,
+    after_ref,
     own_ref,
     mate_ref,
     arrived_ref,
     entry_ref,
     added_ref,
     columns_ref,
-    stored_ref,
     near_ref,
-    normed_ref,
-    factor_ref,
-    slope_ref,
 ):
     x_in = jnp.where(place_ref[0] == 0, entry_ref[...], arrived_ref[...]).astype(jnp.float32)
-    near = gained(own_ref[1] + mate_ref[1], columns_ref, 0)
+    near = gained(own_ref[1] + mate_ref[1], columns_ref)
     near_ref[...] = x_in + near + added_ref[...].astype(jnp.float32)
+
+
+def saved_kernel(plan_ref, after_ref, stored_ref, normed_ref, factor_ref, slope_ref):
     normed, factor = normalize(stored_ref[plan_ref[0, 1]].astype(jnp.float32))
     normed_ref[...] = normed
     factor_ref[...] = jnp.broadcast_to(factor, factor_ref.shape)
@@ -161,8 +159,16 @@
     slope_ref[...] = sigmoid * (1.0 + normed * (1.0 - sigmoid))
 
 
+def back_kernel(
+    place_ref, plan_ref, stamps_ref, after_ref, skip_ref, gain_ref, extra_ref, back_ref
+):
+    spread(gain_ref, stamps_ref[0, 1], back_ref)
+    extra = skip_ref[plan_ref[0, 1]]
+    extra_ref[...] = jnp.where(place_ref[4] == 1, extra, jnp.zeros_like(extra))
+
+
 def output_kernel(near_ref, far_ref, columns_ref, out_ref):
-    far = gained(far_ref[...].astype(jnp.float32), columns_ref, 0)
+    far = gained(far_ref[...].astype(jnp.float32), columns_ref)
     out_ref[...] = (near_ref[...] + far).astype(jnp.bfloat16)
 
 
@@ -278,9 +284,10 @@
     arrived = shifted(act_carried[0], "section", 1)
     (turned,) = call(transpose_kernel, [((full, 3 * rows), jnp.bfloat16)], [VMEM], [weight], cost=20.0)
     turned, skips, time_gain = lax.optimization_barrier((turned, skips, time_gain))
-    gains, added, extra = call(
+    column_kind = ((rows, 128), jnp.float32)
+    gains, added = call(
         prepare_kernel,
-        [((2, rows, 128), jnp.float32), field, field],
+        [column_kind, field],
         [SMEM] * 3 + [VMEM] * 2,
         [place, plan, timesteps, skips, time_gain],
         cost=20.0,
@@ -296,23 +303,36 @@
     )
     mate_part = swap_core(mate_side)
     (own,) = call(own_kernel, [pair], [SMEM, VMEM, VMEM], [place, turned, stacked], cost=20.0)
-    (far_side,) = call(halves_kernel, [field], [VMEM, VMEM], [own, mate_part])
+    far_side, after = call(
+        halves_kernel, [field, ((8, 128), jnp.float32)], [VMEM, VMEM], [own, mate_part]
+    )
     far = swap_chip(far_side)
-    stored, far_side = lax.optimization_barrier((stored, far_side))
     whole = ((rows, cells), jnp.float32)
-    near, saved_normed, saved_factor, slope = call(
+    (near,) = call(
         near_kernel,
-        [whole, whole, ((rows // WIDTH, 8, 128), jnp.float32), whole],
-        [SMEM] * 2 + [VMEM] * 7,
-        [place, plan, own, mate_part, arrived, entry_latent, added, gains, stored],
+        [whole],
+        [SMEM] + [VMEM] * 7,
+        [place, after, own, mate_part, arrived, entry_latent, added, gains],
+    )
+    saved_normed, saved_factor, slope = call(
+        saved_kernel,
+        [whole, ((rows // WIDTH, 8, 128), jnp.float32), whole],
+        [SMEM] + [VMEM] * 2,
+        [plan, after, stored],
         cost=20.0,
     )
-    returned, near = lax.optimization_barrier((returned, near))
+    extra, back_gains = call(
+        back_kernel,
+        [field, column_kind],
+        [SMEM] * 3 + [VMEM] * 3,
+        [place, plan, timesteps, after, skips, time_gain],
+    )
+    returned, near, slope = lax.optimization_barrier((returned, near, slope))
     (scaled,) = call(
         scaled_kernel,
         [field],
         [SMEM] + [VMEM] * 4,
-        [place, returned, reward_head, extra, gains],
+        [place, returned, reward_head, extra, back_gains],
     )
     other = swap_chip(scaled)
     far, scaled = lax.optimization_barrier((far, scaled))

time: 66.2 us -> 66.2 us (level)
  Pallas kernels: 11.2 us -> 12.4 us
  waiting for transfers between devices: 8.67 us -> 7.75 us
    ppermute x2, waiting for transfers between devices: 1.76 us -> 0.58 us  [swap_chip(): return lax.ppermute(block, 'ch', [(0, 2), (2, 0), (1, 3), (3, 1)])]
    pallas_call x11 -> x13, Pallas kernels: 11.2 us -> 12.4 us  [call(): pl.pallas_call(kernel, out_shape=[jax.ShapeDtypeStruct(shape, kind) for s...]
  transfers between devices with their start and end apart: 10 -> 10, of which waited for: 4 -> 4; matrix products, arithmetic and copies ran while one was open for 0% -> 0% of each run, Pallas kernels for 17% -> 19%
where the time goes in v10:
time: 66.2 us; the launch traced here: 65.8 us
  starting transfers between devices  41.9 us (63%)
  Pallas kernels  12.4 us (19%)
  waiting for transfers between devices  7.75 us (12%)
  local copies, waits for them, and re-layouts  2.83 us (4%)
  between operations  0.91 us (1%)
    ppermute x1, starting transfers between devices, local(): mirror_in = lax.ppermute(sent, 'section', route)  15.5 us
    ppermute x5, starting transfers between devices, swap_core(): return lax.ppermute(block, 'ch', [(0, 1), (1, 0), (2, 3), (3, 2)])  14.1 us
    pallas_call x13, Pallas kernels, call(): pl.pallas_call(kernel, out_shape=[jax.ShapeDtypeStruct(shape, kind) for s...  12.4 us
    ppermute x2, starting transfers between devices, shifted(): return lax.ppermute(block, axis, route)  6.94 us
    ppermute x1, waiting for transfers between devices, local(): mirror_in = lax.ppermute(sent, 'section', route)  5.88 us
    ppermute x2, starting transfers between devices, swap_chip(): return lax.ppermute(block, 'ch', [(0, 2), (2, 0), (1, 3), (3, 1)])  5.41 us
    unnamed x21, local copies, waits for them, and re-layouts  2.74 us
  transfers between devices with their start and end apart: 10, of which 4 were waited for; matrix products, arithmetic and copies ran while one was open for 0% of the time, Pallas kernels for 19%

profile of v10, /device:TPU:1, one launch (start us, length us, event | category | flops | bytes accessed | tf_op | source)
XLA Modules:
  0.0 65.8 jit_solution(15470893644332734390)
XLA Ops:
  0.6 5.7 %collective-permute-start.1 = (bf16[320,384]{1,0:T(8,128)(2,1)}, bf16[320,384]{1,0:T(8,128)(2,1)S(1)}, u32[]{:S(2)}, u32[]{:S(2)}) collective-permute-start(bf16[320,384]{1,0:T(8,128)(2,1)} %bitcast.24), channel_id=1, source_target_pairs={{0,4},{4,8},{8,12},{12,16},{16,20},{20,24},{24,28},{28,32},{32,36}... | collective-permute-start | bytes 737288 | tf_op jit(solution)/shard_map/ppermute | solution.py:22
  6.3 1.7 %copy-done = bf16[1,3,320,1280]{3,2,1,0:T(8,128)(2,1)S(1)} copy-done((bf16[1,3,320,1280]{3,2,1,0:T(8,128)(2,1)S(1)}, bf16[1,3,320,1280]{3,2,1,0:T(8,128)(2,1)}, u32[]{:S(2)}) %copy-start) | copy-done | bytes 2457624
  8.0 0.8 %transpose_kernel.1.weight_ref = bf16[1280,960]{1,0:T(8,128)(2,1)S(1)} custom-call(bf16[960,1280]{1,0:T(8,128)(2,1)S(1)} %bitcast.14), custom_call_target="tpu_custom_call" | custom-call | flops 20000000000 | bytes 20000000 | tf_op jit(solution)/shard_map/transpose_kernel/pallas_call | solution.py:244
  9.1 0.7 %prepare_kernel.1 = (f32[320,128]{1,0:T(8,128)S(1)}, bf16[320,384]{1,0:T(8,128)(2,1)S(1)}) custom-call(s32[6]{0:T(128)S(1)} %stack.39.place_ref, s32[1,2]{1,0:T(1,128)S(1)} %copy-done.7, s32[1,2]{1,0:T(1,128)S(1)} %copy-done.8, bf16[2,320,384]{2,1,0:T(8,128)(2,1)S(1)} %bitcast.16, f32[25,320]{1,0:T(8,128)S(1)} %copy-done.6), custom_call_target="tpu_custom_call" | custom-call | flops 20000000000 | bytes 20000000 | tf_op jit(solution)/shard_map/prepare_kernel/pallas_call | solution.py:244
  10.0 1.3 %collective-permute-start = (bf16[320,384]{1,0:T(8,128)(2,1)S(1)}, bf16[320,384]{1,0:T(8,128)(2,1)S(1)}, u32[]{:S(2)}, u32[]{:S(2)}) collective-permute-start(bf16[320,384]{1,0:T(8,128)(2,1)S(1)} %bitcast.18), channel_id=1, source_target_pairs={{4,0},{8,4},{12,8},{16,12},{20,16},{24,20},{28,24},{32,28},{36,32}... | collective-permute-start | bytes 737288 | tf_op jit(solution)/shard_map/ppermute | solution.py:22
  11.3 1.8 %forward_kernel.1 = (f32[2,320,384]{2,1,0:T(8,128)S(1)}, bf16[960,384]{1,0:T(8,128)(2,1)S(1)}) custom-call(s32[6]{0:T(128)S(1)} %stack.39.place_ref, bf16[320,384]{1,0:T(8,128)(2,1)S(1)} %collective-permute-done.1.arrived_ref, bf16[320,384]{1,0:T(8,128)(2,1)S(1)} %copy-done.3, bf16[1280,960]{1,0:T(8,128)(2,1)S(1)} %transpose_kernel.1.weight_ref), custom_call_target="tpu_custom_call" | custom-call | tf_op jit(solution)/shard_map/forward_kernel/pallas_call | solution.py:244
  13.2 4.4 %collective-permute-start.2 = (f32[2,320,384]{2,1,0:T(8,128)S(1)}, f32[2,320,384]{2,1,0:T(8,128)S(1)}, u32[]{:S(2)}, u32[]{:S(2)}) collective-permute-start(f32[2,320,384]{2,1,0:T(8,128)S(1)} %get-tuple-element.41), channel_id=1, source_target_pairs={{0,1},{1,0},{2,3},{3,2},{4,5},{5,4},{6,7},{7,6},{8,9},{9,8},{10,11... | collective-permute-start | bytes 2949128 | tf_op jit(solution)/shard_map/ppermute | solution.py:26
  17.6 1.4 %own_kernel.1.own_ref = f32[2,320,384]{2,1,0:T(8,128)S(1)} custom-call(s32[6]{0:T(128)S(1)} %stack.39.place_ref, bf16[1280,960]{1,0:T(8,128)(2,1)S(1)} %transpose_kernel.1.weight_ref, bf16[960,384]{1,0:T(8,128)(2,1)S(1)} %get-tuple-element.40.stacked_ref), custom_call_target="tpu_custom_call" | custom-call | flops 20000000000 | bytes 20000000 | tf_op jit(solution)/shard_map/own_kernel/pallas_call | solution.py:244
  19.0 0.8 %collective-permute-done.2.mate_ref = f32[2,320,384]{2,1,0:T(8,128)S(1)} collective-permute-done((f32[2,320,384]{2,1,0:T(8,128)S(1)}, f32[2,320,384]{2,1,0:T(8,128)S(1)}, u32[]{:S(2)}, u32[]{:S(2)}) %collective-permute-start.2) | collective-permute-done | bytes 983072 | tf_op jit(solution)/shard_map/ppermute | solution.py:26
  19.8 1.9 %collective-permute-start.4 = (bf16[320,384]{1,0:T(8,128)(2,1)S(1)}, bf16[320,384]{1,0:T(8,128)(2,1)S(1)}, u32[]{:S(2)}, u32[]{:S(2)}) collective-permute-start(bf16[320,384]{1,0:T(8,128)(2,1)S(1)} %get-tuple-element.49), channel_id=1, source_target_pairs={{0,2},{2,0},{1,3},{3,1},{4,6},{6,4},{5,7},{7,5},{8,10},{10,8},{9,1... | collective-permute-start | bytes 737288 | tf_op jit(solution)/shard_map/ppermute | solution.py:30
  21.8 1.0 %saved_kernel.1 = (f32[320,384]{1,0:T(8,128)S(1)}, f32[8,8,128]{2,1,0:T(8,128)S(1)}, f32[320,384]{1,0:T(8,128)S(1)}) custom-call(s32[1,2]{1,0:T(1,128)S(1)} %copy-done.7, f32[8,128]{1,0:T(8,128)S(1)} %get-tuple-element.42.after_ref, bf16[2,320,384]{2,1,0:T(8,128)(2,1)S(1)} %bitcast.20), custom_call_target="tpu_custom_call" | custom-call | flops 20000000000 | bytes 20000000 | tf_op jit(solution)/shard_map/saved_kernel/pallas_call | solution.py:244
  22.8 0.7 %back_kernel.1 = (bf16[320,384]{1,0:T(8,128)(2,1)S(1)}, f32[320,128]{1,0:T(8,128)S(1)}) custom-call(s32[6]{0:T(128)S(1)} %stack.39.place_ref, s32[1,2]{1,0:T(1,128)S(1)} %copy-done.7, s32[1,2]{1,0:T(1,128)S(1)} %copy-done.8, f32[8,128]{1,0:T(8,128)S(1)} %get-tuple-element.42.after_ref, bf16[2,320,384]{2,1,0:T(8,128)(2,1)S(1)} %bitcast.17, ...), custom_call_target="tpu_custom_call" | custom-call | tf_op jit(solution)/shard_map/back_kernel/pallas_call | solution.py:244
  23.4 0.7 %near_kernel.1.near_ref = f32[320,384]{1,0:T(8,128)S(1)} custom-call(s32[6]{0:T(128)S(1)} %stack.39.place_ref, f32[8,128]{1,0:T(8,128)S(1)} %get-tuple-element.42.after_ref, f32[2,320,384]{2,1,0:T(8,128)S(1)} %own_kernel.1.own_ref, f32[2,320,384]{2,1,0:T(8,128)S(1)} %collective-permute-done.2.mate_ref, ...), custom_call_target="tpu_custom_call" | custom-call | tf_op jit(solution)/shard_map/near_kernel/pallas_call | solution.py:244
  24.2 0.6 scaled_kernel.1.scaled_ref
  24.8 3.5 %collective-permute-start.3 = (bf16[320,384]{1,0:T(8,128)(2,1)S(1)}, bf16[320,384]{1,0:T(8,128)(2,1)S(1)}, u32[]{:S(2)}, u32[]{:S(2)}) collective-permute-start(bf16[320,384]{1,0:T(8,128)(2,1)S(1)} %scaled_kernel.1.scaled_ref), channel_id=1, source_target_pairs={{0,2},{2,0},{1,3},{3,1},{4,6},{6,4},{5,7},{7,5},{8,10},{10,8},{9,1... | collective-permute-start | bytes 737288 | tf_op jit(solution)/shard_map/ppermute | solution.py:30
  29.5 15.5 %collective-permute-start.5 = (bf16[320,384]{1,0:T(8,128)(2,1)S(1)}, bf16[320,384]{1,0:T(8,128)(2,1)S(1)}, u32[]{:S(2)}, u32[]{:S(2)}) collective-permute-start(bf16[320,384]{1,0:T(8,128)(2,1)S(1)} %sent_kernel.1), channel_id=1, source_target_pairs={{0,508},{4,504},{8,500},{12,496},{16,492},{20,488},{24,484},{28,48... | collective-permute-start | bytes 737288 | tf_op jit(solution)/shard_map/ppermute | solution.py:348
  45.1 3.4 %collective-permute-start.6 = (bf16[160,384]{1,0:T(8,128)(2,1)S(1)}, bf16[160,384]{1,0:T(8,128)(2,1)S(1)}, u32[]{:S(2)}, u32[]{:S(2)}) collective-permute-start(bf16[160,384]{1,0:T(8,128)(2,1)S(1)} %get-tuple-element.59), channel_id=1, source_target_pairs={{0,1},{1,0},{2,3},{3,2},{4,5},{5,4},{6,7},{7,6},{8,9},{9,8},{10,11... | collective-permute-start | bytes 368648 | tf_op jit(solution)/shard_map/ppermute | solution.py:26
  48.5 1.9 %collective-permute-start.7 = (bf16[160,384]{1,0:T(8,128)(2,1)S(1)}, bf16[160,384]{1,0:T(8,128)(2,1)S(1)}, u32[]{:S(2)}, u32[]{:S(2)}) collective-permute-start(bf16[160,384]{1,0:T(8,128)(2,1)S(1)} %get-tuple-element.60), channel_id=1, source_target_pairs={{0,1},{1,0},{2,3},{3,2},{4,5},{5,4},{6,7},{7,6},{8,9},{9,8},{10,11... | collective-permute-start | bytes 368648 | tf_op jit(solution)/shard_map/ppermute | solution.py:26
  50.4 2.4 %collective-permute-start.8 = (bf16[160,384]{1,0:T(8,128)(2,1)S(1)}, bf16[160,384]{1,0:T(8,128)(2,1)S(1)}, u32[]{:S(2)}, u32[]{:S(2)}) collective-permute-start(bf16[160,384]{1,0:T(8,128)(2,1)S(1)} %get-tuple-element.61), channel_id=1, source_target_pairs={{0,1},{1,0},{2,3},{3,2},{4,5},{5,4},{6,7},{7,6},{8,9},{9,8},{10,11... | collective-permute-start | bytes 368648 | tf_op jit(solution)/shard_map/ppermute | solution.py:26
  52.8 1.9 %collective-permute-start.9 = (bf16[160,384]{1,0:T(8,128)(2,1)S(1)}, bf16[160,384]{1,0:T(8,128)(2,1)S(1)}, u32[]{:S(2)}, u32[]{:S(2)}) collective-permute-start(bf16[160,384]{1,0:T(8,128)(2,1)S(1)} %get-tuple-element.62), channel_id=1, source_target_pairs={{0,1},{1,0},{2,3},{3,2},{4,5},{5,4},{6,7},{7,6},{8,9},{9,8},{10,11... | collective-permute-start | bytes 368648 | tf_op jit(solution)/shard_map/ppermute | solution.py:26
  54.8 0.8 %output_kernel.1 = bf16[320,384]{1,0:T(8,128)(2,1)} custom-call(f32[320,384]{1,0:T(8,128)S(1)} %near_kernel.1.near_ref, bf16[320,384]{1,0:T(8,128)(2,1)S(1)} %collective-permute-done.4.far_ref, f32[320,128]{1,0:T(8,128)S(1)} %get-tuple-element.44.columns_ref), custom_call_target="tpu_custom_call" | custom-call | tf_op jit(solution)/shard_map/output_kernel/pallas_call | solution.py:244
  56.1 3.1 %gradient_kernel.1 = bf16[320,384]{1,0:T(8,128)(2,1)} custom-call(s32[6]{0:T(128)S(1)} %stack.39.place_ref, f32[320,384]{1,0:T(8,128)S(1)} %get-tuple-element.54.normed_ref, f32[8,8,128]{2,1,0:T(8,128)S(1)} %get-tuple-element.55.factor_ref, f32[320,384]{1,0:T(8,128)S(1)} %get-tuple-element.56.slope_ref, ...), custom_call_target="tpu_custom_call" | custom-call | tf_op jit(solution)/shard_map/gradient_kernel/pallas_call | solution.py:244
  59.2 5.9 %collective-permute-done.5 = bf16[320,384]{1,0:T(8,128)(2,1)S(1)} collective-permute-done((bf16[320,384]{1,0:T(8,128)(2,1)S(1)}, bf16[320,384]{1,0:T(8,128)(2,1)S(1)}, u32[]{:S(2)}, u32[]{:S(2)}) %collective-permute-start.5) | collective-permute-done | bytes 245792 | tf_op jit(solution)/shard_map/ppermute | solution.py:348
  65.1 0.7 %copy.14 = bf16[1,320,384]{2,1,0:T(8,128)(2,1)} copy(bf16[1,320,384]{2,1,0:T(8,128)(2,1)S(1)} %bitcast.21) | data formatting | bytes 491520
  (31 shorter events, 2.3 us)
Async XLA Ops:
  0.6 10.7 %collective-permute-start.1 = (bf16[320,384]{1,0:T(8,128)(2,1)}, bf16[320,384]{1,0:T(8,128)(2,1)S(1)}, u32[]{:S(2)}, u32[]{:S(2)}) collective-permute-start(bf16[320,384]{1,0:T(8,128)(2,1)} %bitcast.24), channel_id=1, source_target_pairs={{0,4},{4,8},{8,12},{12,16},{16,20},{20,24},{24,28},{28,32},{32,36}... | collective-permute-start | bytes 737288 | tf_op jit(solution)/shard_map/ppermute | solution.py:22
  6.3 1.7 %copy-start = (bf16[1,3,320,1280]{3,2,1,0:T(8,128)(2,1)S(1)}, bf16[1,3,320,1280]{3,2,1,0:T(8,128)(2,1)}, u32[]{:S(2)}) copy-start(bf16[1,3,320,1280]{3,2,1,0:T(8,128)(2,1)} %param.16) | copy-start | bytes 7372804
  8.0 1.0 %copy-start.4 = (bf16[1,2,320,384]{3,2,1,0:T(8,128)(2,1)S(1)}, bf16[1,2,320,384]{3,2,1,0:T(8,128)(2,1)}, u32[]{:S(2)}) copy-start(bf16[1,2,320,384]{3,2,1,0:T(8,128)(2,1)} %param.15) | copy-start | bytes 1474564
  8.0 1.0 %copy-start.6 = (f32[25,320]{1,0:T(8,128)S(1)}, f32[25,320]{1,0:T(8,128)}, u32[]{:S(2)}) copy-start(f32[25,320]{1,0:T(8,128)} %gain_ref.1) | copy-start | bytes 96004
  8.0 1.0 %copy-start.7 = (s32[1,2]{1,0:T(1,128)S(1)}, s32[1,2]{1,0:T(1,128)}, u32[]{:S(2)}) copy-start(s32[1,2]{1,0:T(1,128)} %plan_ref.5) | copy-start | bytes 28
  8.0 1.0 %copy-start.8 = (s32[1,2]{1,0:T(1,128)S(1)}, s32[1,2]{1,0:T(1,128)}, u32[]{:S(2)}) copy-start(s32[1,2]{1,0:T(1,128)} %stamps_ref.3) | copy-start | bytes 28
  9.1 0.9 %copy-start.5 = (bf16[1,320,384]{2,1,0:T(8,128)(2,1)S(1)}, bf16[1,320,384]{2,1,0:T(8,128)(2,1)}, u32[]{:S(2)}) copy-start(bf16[1,320,384]{2,1,0:T(8,128)(2,1)} %param.11) | copy-start | bytes 737284
  9.1 2.2 %copy-start.3 = (bf16[320,384]{1,0:T(8,128)(2,1)S(1)}, bf16[320,384]{1,0:T(8,128)(2,1)}, u32[]{:S(2)}) copy-start(bf16[320,384]{1,0:T(8,128)(2,1)} %entry_ref.3) | copy-start | bytes 737284
  10.0 14.1 %collective-permute-start = (bf16[320,384]{1,0:T(8,128)(2,1)S(1)}, bf16[320,384]{1,0:T(8,128)(2,1)S(1)}, u32[]{:S(2)}, u32[]{:S(2)}) collective-permute-start(bf16[320,384]{1,0:T(8,128)(2,1)S(1)} %bitcast.18), channel_id=1, source_target_pairs={{4,0},{8,4},{12,8},{16,12},{20,16},{24,20},{28,24},{32,28},{36,32}... | collective-permute-start | bytes 737288 | tf_op jit(solution)/shard_map/ppermute | solution.py:22
  13.2 6.6 %collective-permute-start.2 = (f32[2,320,384]{2,1,0:T(8,128)S(1)}, f32[2,320,384]{2,1,0:T(8,128)S(1)}, u32[]{:S(2)}, u32[]{:S(2)}) collective-permute-start(f32[2,320,384]{2,1,0:T(8,128)S(1)} %get-tuple-element.41), channel_id=1, source_target_pairs={{0,1},{1,0},{2,3},{3,2},{4,5},{5,4},{6,7},{7,6},{8,9},{9,8},{10,11... | collective-permute-start | bytes 2949128 | tf_op jit(solution)/shard_map/ppermute | solution.py:26
  17.6 4.2 %copy-start.9 = (bf16[1,2,320,384]{3,2,1,0:T(8,128)(2,1)S(1)}, bf16[1,2,320,384]{3,2,1,0:T(8,128)(2,1)}, u32[]{:S(2)}) copy-start(bf16[1,2,320,384]{3,2,1,0:T(8,128)(2,1)} %param.14) | copy-start | bytes 1474564
  19.8 9.1 %collective-permute-start.4 = (bf16[320,384]{1,0:T(8,128)(2,1)S(1)}, bf16[320,384]{1,0:T(8,128)(2,1)S(1)}, u32[]{:S(2)}, u32[]{:S(2)}) collective-permute-start(bf16[320,384]{1,0:T(8,128)(2,1)S(1)} %get-tuple-element.49), channel_id=1, source_target_pairs={{0,2},{2,0},{1,3},{3,1},{4,6},{6,4},{5,7},{7,5},{8,10},{10,8},{9,1... | collective-permute-start | bytes 737288 | tf_op jit(solution)/shard_map/ppermute | solution.py:30
  22.8 1.4 %copy-start.2 = (bf16[320,384]{1,0:T(8,128)(2,1)S(1)}, bf16[320,384]{1,0:T(8,128)(2,1)}, u32[]{:S(2)}) copy-start(bf16[320,384]{1,0:T(8,128)(2,1)} %reward_ref.5) | copy-start | bytes 737284
  24.1 31.9 %copy-start.1 = (bf16[1,3,320,1280]{3,2,1,0:T(8,128)(2,1)S(1)}, bf16[1,3,320,1280]{3,2,1,0:T(8,128)(2,1)}, u32[]{:S(2)}) copy-start(bf16[1,3,320,1280]{3,2,1,0:T(8,128)(2,1)} %param.16) | copy-start | bytes 7372804
  24.8 20.2 %collective-permute-start.3 = (bf16[320,384]{1,0:T(8,128)(2,1)S(1)}, bf16[320,384]{1,0:T(8,128)(2,1)S(1)}, u32[]{:S(2)}, u32[]{:S(2)}) collective-permute-start(bf16[320,384]{1,0:T(8,128)(2,1)S(1)} %scaled_kernel.1.scaled_ref), channel_id=1, source_target_pairs={{0,2},{2,0},{1,3},{3,1},{4,6},{6,4},{5,7},{7,5},{8,10},{10,8},{9,1... | collective-permute-start | bytes 737288 | tf_op jit(solution)/shard_map/ppermute | solution.py:30
  29.5 35.5 %collective-permute-start.5 = (bf16[320,384]{1,0:T(8,128)(2,1)S(1)}, bf16[320,384]{1,0:T(8,128)(2,1)S(1)}, u32[]{:S(2)}, u32[]{:S(2)}) collective-permute-start(bf16[320,384]{1,0:T(8,128)(2,1)S(1)} %sent_kernel.1), channel_id=1, source_target_pairs={{0,508},{4,504},{8,500},{12,496},{16,492},{20,488},{24,484},{28,48... | collective-permute-start | bytes 737288 | tf_op jit(solution)/shard_map/ppermute | solution.py:348
  45.1 10.4 %collective-permute-start.6 = (bf16[160,384]{1,0:T(8,128)(2,1)S(1)}, bf16[160,384]{1,0:T(8,128)(2,1)S(1)}, u32[]{:S(2)}, u32[]{:S(2)}) collective-permute-start(bf16[160,384]{1,0:T(8,128)(2,1)S(1)} %get-tuple-element.59), channel_id=1, source_target_pairs={{0,1},{1,0},{2,3},{3,2},{4,5},{5,4},{6,7},{7,6},{8,9},{9,8},{10,11... | collective-permute-start | bytes 368648 | tf_op jit(solution)/shard_map/ppermute | solution.py:26
  48.5 7.1 %collective-permute-start.7 = (bf16[160,384]{1,0:T(8,128)(2,1)S(1)}, bf16[160,384]{1,0:T(8,128)(2,1)S(1)}, u32[]{:S(2)}, u32[]{:S(2)}) collective-permute-start(bf16[160,384]{1,0:T(8,128)(2,1)S(1)} %get-tuple-element.60), channel_id=1, source_target_pairs={{0,1},{1,0},{2,3},{3,2},{4,5},{5,4},{6,7},{7,6},{8,9},{9,8},{10,11... | collective-permute-start | bytes 368648 | tf_op jit(solution)/shard_map/ppermute | solution.py:26
  50.4 5.1 %collective-permute-start.8 = (bf16[160,384]{1,0:T(8,128)(2,1)S(1)}, bf16[160,384]{1,0:T(8,128)(2,1)S(1)}, u32[]{:S(2)}, u32[]{:S(2)}) collective-permute-start(bf16[160,384]{1,0:T(8,128)(2,1)S(1)} %get-tuple-element.61), channel_id=1, source_target_pairs={{0,1},{1,0},{2,3},{3,2},{4,5},{5,4},{6,7},{7,6},{8,9},{9,8},{10,11... | collective-permute-start | bytes 368648 | tf_op jit(solution)/shard_map/ppermute | solution.py:26
  52.8 3.2 %collective-permute-start.9 = (bf16[160,384]{1,0:T(8,128)(2,1)S(1)}, bf16[160,384]{1,0:T(8,128)(2,1)S(1)}, u32[]{:S(2)}, u32[]{:S(2)}) collective-permute-start(bf16[160,384]{1,0:T(8,128)(2,1)S(1)} %get-tuple-element.62), channel_id=1, source_target_pairs={{0,1},{1,0},{2,3},{3,2},{4,5},{5,4},{6,7},{7,6},{8,9},{9,8},{10,11... | collective-permute-start | bytes 368648 | tf_op jit(solution)/shard_map/ppermute | solution.py:26
